TPU v7x, 256 devices: a whole 4x4x8 slice. The times are simulated.
256 devices in a mesh: ctx: 16 (over y, x), exp: 16 (over z, core).
Axes of the slice: x: 4, y: 4, z: 8, core: 2. Of those that a mesh axis runs over, the one named last changes fastest.
Arguments:
- query_raw: bfloat16 [16384, 2048], P('ctx', 'exp'), may hold values from -6 to 6
- key_raw: bfloat16 [16384, 2048], P('ctx', 'exp'), may hold values from -8 to 8
- values: bfloat16 [16384, 4096], P('ctx', 'exp'), may hold values from -6 to 6
- out_gate: bfloat16 [16384, 4096], P('ctx', 'exp'), may hold values from -6 to 6
- log_decay: float32 [32, 16384], P('exp', 'ctx'), may hold values from -0.8 to 0, as said below
- beta_rate: float32 [32, 16384], P('exp', 'ctx'), may hold values from 0 to 1
- head_gain: float32 [128], replicated, may hold values from 0.1 to 1.9
- out_weight: bfloat16 [4096, 2048], P('exp'), may hold values from -0.09375 to 0.09375
- residual: bfloat16 [16384, 2048], P(('ctx', 'exp')), may hold values from -3 to 3
- post_gain: float32 [2048], replicated, may hold values from 0.1 to 1.9
- router_weight: bfloat16 [2048, 256], replicated, may hold values from -0.0625 to 0.0625
- routes: int32 [16384, 10], P(('ctx', 'exp')), may hold values from 0 to 255, all different within a row; in each aligned block of 64 rows (0 to 63, 64 to 127, ...) at most 4 rows name the same one
- placement: int32 [256], replicated, may hold values from 0 to 255, each once
- expert_in: bfloat16 [256, 2048, 1024], P(('ctx', 'exp')), may hold values from -0.125 to 0.125
- expert_out: bfloat16 [256, 512, 2048], P(('ctx', 'exp')), may hold values from -0.5 to 0.5
Outputs:
- core_out: bfloat16 [16384, 4096], P('ctx', 'exp')
- layer_out: bfloat16 [16384, 2048], P(('ctx', 'exp'))
Inputs may be any that keep to these rules, and one draw needn't show every extreme that they name: `routes`: each row names 10 different experts; among the 64 rows of one device (aligned blocks of rows) no expert is named by more than 4 rows. A permutation: expert e's weights are entry placement[e] of expert_in and expert_out. `log_decay`: negative.
All inputs are finite; a program needn't handle non-finite values.
Results may differ from a plain program's by a relative error of at most 0.03.
Values may be sent and summed in bfloat16 or wider, within the bound.
No kernel may reach another device: no remote copies, remote signals or barrier semaphores. Data moves between devices by JAX's collectives and lax.ppermute only.
A program may use at most 128 MiB of HBM per device.

v0:
```python
import math

import jax
import jax.numpy as jnp
from jax import lax
from jax.sharding import PartitionSpec as P

D = 2048
HK = 16
HV = 32
K = 128
V = 128
TOP = 10
BLOCK = 64


EPS = 1e-06
HIGH = lax.Precision.HIGHEST


def entering(shard, axis, join, neutral):
    place = lax.axis_index(axis)
    gathered = jax.tree.map(
        lambda a, kind: lax.all_gather(a.astype(kind), axis), shard, (jnp.bfloat16, jnp.bfloat16)
    )
    state = jax.tree.map(lambda a, e: jnp.zeros_like(a) + jnp.asarray(e, a.dtype), shard, neutral)

    def one(step, state):
        return join(
            state,
            jax.tree.map(
                lambda a, own: lax.dynamic_index_in_dim(a, step, 0, False).astype(own.dtype),
                gathered,
                shard,
            ),
        )

    return lax.fori_loop(0, place, one, state)


def unit_rows(matrix):
    return matrix / jnp.sqrt(jnp.sum(matrix * matrix, axis=-1, keepdims=True) + EPS)


def lower_solve(system, rhs):
    return lax.linalg.triangular_solve(system, rhs, left_side=True, lower=True, unit_diagonal=True)


def matmul_heads(left, right):
    return jnp.einsum("...ij,...jk->...ik", left, right, precision=HIGH)


def block_parts(query, keys, vals, decay, learning_speed):
    width = decay.shape[-1]
    index = jnp.arange(width, dtype=jnp.int32)
    strict = index[:, None] > index[None, :]
    within = index[:, None] >= index[None, :]
    cumul = jnp.cumsum(decay, axis=-1)
    spread = cumul[..., :, None] - cumul[..., None, :]
    fall_strict = jnp.where(strict, jnp.exp(jnp.where(strict, spread, 0.0)), 0.0)
    fall_within = jnp.where(within, jnp.exp(jnp.where(within, spread, 0.0)), 0.0)
    inner = jnp.einsum("...ik,...jk->...ij", keys, keys, precision=HIGH)
    system = jnp.eye(width, dtype=jnp.float32) + learning_speed[..., :, None] * fall_strict * inner
    scaled_keys = (learning_speed * jnp.exp(cumul))[..., None] * keys
    wvec = lower_solve(system, scaled_keys)
    uvec = lower_solve(system, learning_speed[..., None] * vals)
    last = cumul[..., -1:]
    qk_mix = jnp.einsum("...ik,...jk->...ij", query, keys, precision=HIGH) * fall_within
    q_decayed = jnp.exp(cumul)[..., None] * query
    k_decayed = jnp.exp(last - cumul)[..., None] * keys
    eye = jnp.eye(keys.shape[-1], dtype=jnp.float32)
    trans = jnp.exp(last)[..., None] * eye - jnp.einsum(
        "...ck,...cl->...kl", k_decayed, wvec, precision=HIGH
    )
    drive = jnp.einsum("...ck,...cv->...kv", k_decayed, uvec, precision=HIGH)
    return ((wvec, uvec, qk_mix, q_decayed, k_decayed, last), trans, drive)


def sweep(carry, part):
    wvec, uvec, qk_mix, q_decayed, k_decayed, last = part
    fresh = uvec - jnp.einsum("...ck,...kv->...cv", wvec, carry, precision=HIGH)
    output = jnp.einsum("...ck,...kv->...cv", q_decayed, carry, precision=HIGH)
    output = output + jnp.einsum("...cj,...jv->...cv", qk_mix, fresh, precision=HIGH)
    carry = jnp.exp(last)[..., None] * carry + jnp.einsum(
        "...ck,...cv->...kv", k_decayed, fresh, precision=HIGH
    )
    return (carry, output)


def expert_rows(piece, gate_up, down):
    shape = piece.shape
    flat = piece.reshape(-1, shape[-1])
    hidden = jnp.dot(flat, gate_up, preferred_element_type=jnp.float32)
    width = down.shape[0]
    act = (jax.nn.silu(hidden[:, :width]) * hidden[:, width:]).astype(jnp.bfloat16)
    return (
        jnp.dot(act, down, preferred_element_type=jnp.float32).astype(jnp.bfloat16).reshape(shape)
    )


def local(
    query_raw,
    key_raw,
    values,
    out_gate,
    log_decay,
    beta_rate,
    head_gain,
    out_weight,
    residual,
    post_gain,
    router_weight,
    routes,
    placement,
    expert_in,
    expert_out,
):
    rows_ctx = query_raw.shape[0]
    groups = query_raw.shape[1] // K
    heads = values.shape[1] // V
    ratio = HV // HK
    blocks = rows_ctx // BLOCK
    queries = unit_rows(query_raw.astype(jnp.float32).reshape(rows_ctx, groups, K)) * (
        1.0 / math.sqrt(K)
    )
    keys = unit_rows(key_raw.astype(jnp.float32).reshape(rows_ctx, groups, K))
    queries = jnp.repeat(queries, ratio, axis=1)
    keys = jnp.repeat(keys, ratio, axis=1)
    vals = values.astype(jnp.float32).reshape(rows_ctx, heads, V)

    def by_block(tensor):
        return jnp.transpose(tensor.reshape(blocks, BLOCK, heads, tensor.shape[-1]), (0, 2, 1, 3))

    def by_block_rate(tensor):
        return jnp.transpose(tensor.reshape(heads, blocks, BLOCK), (1, 0, 2))

    parts, trans, drive = block_parts(
        by_block(queries),
        by_block(keys),
        by_block(vals),
        by_block_rate(log_decay),
        by_block_rate(beta_rate),
    )

    def compose(carry, item):
        total_map, total_drive = carry
        step_map, step_drive = item
        return (
            (matmul_heads(step_map, total_map), matmul_heads(step_map, total_drive) + step_drive),
            None,
        )

    eye = jnp.broadcast_to(jnp.eye(K, dtype=jnp.float32), (heads, K, K))
    blank = jnp.zeros((heads, K, V), jnp.float32)
    (whole_map, whole_drive), unused = lax.scan(compose, (eye, blank), (trans, drive))

    def combine(earlier, later):
        return (matmul_heads(later[0], earlier[0]), matmul_heads(later[0], earlier[1]) + later[1])

    prefix = entering((whole_map, whole_drive), "ctx", combine, (eye, blank))
    entry = prefix[1]
    ended, outputs = lax.scan(sweep, entry, parts)
    core = jnp.transpose(outputs, (0, 2, 1, 3)).reshape(rows_ctx, heads, V)
    gate = out_gate.astype(jnp.float32).reshape(rows_ctx, heads, V)
    scaled = core / jnp.sqrt(jnp.mean(core * core, axis=-1, keepdims=True) + EPS)
    core_out = (
        (scaled * head_gain * jax.nn.silu(gate)).astype(jnp.bfloat16).reshape(rows_ctx, heads * V)
    )
    tok_rows = residual.shape[0]
    attn = lax.psum_scatter(
        jnp.dot(core_out, out_weight, preferred_element_type=jnp.float32).astype(jnp.bfloat16),
        "exp",
        scatter_dimension=0,
        tiled=True,
    ).astype(jnp.float32)
    mid = lax.optimization_barrier(
        (residual.astype(jnp.float32) + attn).astype(jnp.bfloat16)
    ).astype(jnp.float32)
    normed = (mid / jnp.sqrt(jnp.mean(mid * mid, axis=-1, keepdims=True) + EPS) * post_gain).astype(
        jnp.bfloat16
    )
    logits = jnp.dot(normed, router_weight, preferred_element_type=jnp.float32)
    n_ctx = lax.axis_size("ctx")
    n_exp = lax.axis_size("exp")
    experts = n_ctx * n_exp
    cap = 8 * tok_rows * TOP // (5 * experts)
    expert_ids = jnp.arange(experts, dtype=jnp.int32)
    chosen = routes[:, :, None] == expert_ids[None, None, :]
    picked = jnp.sum(jnp.where(chosen, logits[:, None, :], 0.0), axis=-1)
    raised = jnp.exp(picked)
    gates = raised / jnp.sum(raised, axis=-1, keepdims=True)
    target = jnp.sum(jnp.where(chosen, placement[None, None, :], 0), axis=-1).reshape(-1)
    onehot = (target[:, None] == expert_ids[None, :]).astype(jnp.int32)
    position = jnp.sum(onehot * (jnp.cumsum(onehot, axis=0) - 1), axis=1)
    row_ctx = target // n_exp
    row_exp = target % n_exp
    source = jnp.repeat(normed, TOP, axis=0)
    gate_up = expert_in[0]
    down = expert_out[0]
    slot = (row_exp * n_ctx + row_ctx) * cap + position
    outgoing = (
        jnp.zeros((n_exp * n_ctx * cap, D), jnp.bfloat16)
        .at[slot]
        .set(source)
        .reshape(n_exp, n_ctx, cap, D)
    )
    arrived = lax.all_to_all(outgoing, "exp", split_axis=0, concat_axis=0, tiled=True)
    computed = expert_rows(
        lax.all_to_all(arrived, "ctx", split_axis=1, concat_axis=1, tiled=True), gate_up, down
    )
    finished = lax.all_to_all(computed, "ctx", split_axis=1, concat_axis=1, tiled=True)
    returned = lax.all_to_all(finished, "exp", split_axis=0, concat_axis=0, tiled=True)
    results = returned.reshape(-1, D)[slot].astype(jnp.float32).reshape(tok_rows, TOP, D)
    mixture = jnp.sum(gates[:, :, None] * results, axis=1)
    layer_out = (mid + mixture).astype(jnp.bfloat16)
    return (core_out, layer_out)


def solution(mesh):
    placed = (
        P("ctx", "exp"),
        P("ctx", "exp"),
        P("ctx", "exp"),
        P("ctx", "exp"),
        P("exp", "ctx"),
        P("exp", "ctx"),
        P(),
        P("exp", None),
        P(("ctx", "exp"), None),
        P(),
        P(),
        P(("ctx", "exp"), None),
        P(),
        P(("ctx", "exp"), None, None),
        P(("ctx", "exp"), None, None),
    )
    return jax.shard_map(
        local,
        mesh=mesh,
        in_specs=placed,
        out_specs=(P("ctx", "exp"), P(("ctx", "exp"), None)),
        check_vma=False,
    )
```

profile of v0, /device:TPU:32, one launch (start us, length us, event | category | flops | bytes accessed | tf_op | source)
XLA Modules:
  0.0 921.1 jit_solution(8506587918118082963)
XLA Ops:
  12.3 2.8 fusion.40
  15.1 159.2 %custom-call.5 = f32[16,2,1,64,64]{3,4,2,1,0:T(8,128)} custom-call(f32[16,2,1,64,64]{4,3,2,1,0:T(8,128)} %fusion.40), custom_call_target="InvertDiagBlocksLowerTriangular" | custom-call | tf_op jit(solution)/shard_map/triangular_solve/custom-call.1 | solution.py:46
  174.3 2.6 reshape.326
  176.9 3.3 fusion.54
  180.2 4.0 fusion.52
  185.3 5.1 fusion.62
  190.3 5.5 multiply_subtract_fusion
  195.9 39.8 %while.39 = (s32[]{:T(128)}, f32[2,128,128]{2,1,0:T(8,128)S(1)}, f32[2,128,128]{2,1,0:T(8,128)S(1)}, f32[16,2,128,128]{3,2,1,0:T(8,128)}, f32[16,2,128,128]{3,2,1,0:T(8,128)}, /*index=5*/s32[]{:T(128)}, s32[]{:T(128)}) while((s32[]{:T(128)}, f32[2,128,128]{2,1,0:T(8,128)S(1)}, f32[2,128,128]{2,1,0:T(8,128)S(1)}, ...), condition=%wide.region_3.5_spmd.clone, body=%wide.region_2.4_spmd.clone.sunk | while | flops 100728832 | bytes 1443426 | solution.py:155
  237.8 2.8 convolution_multiply_fusion
  240.6 1.7 broadcast_multiply_fusion
  242.3 44.5 %all-gather.7.cloned.1.call-done = bf16[32,128,128]{2,1,0:T(8,128)(2,1)} async-done(((bf16[2,128,128]{2,1,0:T(8,128)(2,1)}), bf16[32,128,128]{2,1,0:T(8,128)(2,1)}) %all-gather.7.cloned.1.call-update) | async-done | bytes 1048592 | tf_op jit(solution)/shard_map/all_gather | solution.py:24
  286.8 50.1 %all-gather.5.cloned.1.call-done = bf16[32,128,128]{2,1,0:T(8,128)(2,1)} async-done(((bf16[2,128,128]{2,1,0:T(8,128)(2,1)}), bf16[32,128,128]{2,1,0:T(8,128)(2,1)}) %all-gather.5.cloned.1.call-update) | async-done | bytes 1048592 | tf_op jit(solution)/shard_map/all_gather | solution.py:24
  336.9 82.0 %while.38 = (s32[]{:T(128)}, f32[2,128,128]{2,1,0:T(8,128)S(1)}, f32[16,2,64,128]{3,2,1,0:T(8,128)}, f32[16,2,1]{1,2,0:T(1,128)S(1)}, f32[16,2,64,128]{3,2,1,0:T...) while((s32[]{:T(128)}, f32[2,128,128]{2,1,0:T(8,128)S(1)}, ...), condition=%wide.region_8.10_spmd, body=%wide.region_7.9_spmd.sunk | while | flops 88178688 | bytes 1247377 | solution.py:162
  340.4 1.7 fusion.139
  345.5 1.7 fusion.139
  350.6 1.7 fusion.139
  360.9 1.7 fusion.139
  366.0 1.7 fusion.139
  376.2 1.7 fusion.139
  391.6 1.7 fusion.139
  396.7 1.7 fusion.139
  407.0 1.7 fusion.139
  412.1 1.7 fusion.139
  417.2 1.7 fusion.139
  420.8 2.1 copy.153
  425.5 3.2 convolution_convert_fusion.1
  430.6 73.2 %reduce-scatter.2.cloned.1.call-done = bf16[64,2048]{1,0:T(8,128)(2,1)} async-done(((bf16[1024,2048]{1,0:T(8,128)(2,1)}), bf16[64,2048]{1,0:T(8,128)(2,1)}) %reduce-scatter.2.cloned.1.call-update) | async-done | bytes 262160 | tf_op jit(solution)/shard_map/reduce_scatter | solution.py:170
  505.1 2.5 broadcast_in_dim.112
  507.6 5.5 reshape.339
  513.1 10.4 %scatter_custom_fusion = bf16[1024,2048]{1,0:T(8,128)(2,1)} fusion(s32[640]{0:T(1024)S(1)} %fusion.89, bf16[640,2048]{1,0:T(8,128)(2,1)} %reshape.339, bf16[]{:T(256)} %constant.105.clone.1), kind=kCustom, calls=%fused_computation.47 | custom fusion | bytes 4194816 | tf_op jit(solution)/shard_map/scatter | solution.py:204
  523.5 7.2 reshape.318
  530.7 101.3 %all_to_all.20 = bf16[16,16,4,2048]{3,2,1,0:T(4,128)(2,1)S(1)} all-to-all(bf16[16,16,4,2048]{3,2,1,0:T(4,128)(2,1)} %reshape.318), channel_id=1, replica_groups=mesh['ctx'=16,'exp'=16] {'exp'}, dimensions={0} | all-to-all | bytes 8388608 | tf_op jit(solution)/shard_map/all_to_all | solution.py:207
  632.0 3.0 copy.162
  635.0 57.7 %all_to_all.21 = bf16[16,16,4,2048]{3,2,0,1:T(4,128)(2,1)S(1)} all-to-all(bf16[16,16,4,2048]{3,2,0,1:T(4,128)(2,1)S(1)} %copy.162), channel_id=1, replica_groups=mesh['ctx'=16,'exp'=16] {'ctx'}, dimensions={1} | all-to-all | bytes 8388608 | tf_op jit(solution)/shard_map/all_to_all | solution.py:209
  692.7 4.0 copy.163
  696.7 6.9 reshape.319
  703.6 7.5 fusion.31
  711.1 4.3 convolution_convert_fusion
  715.5 7.2 reshape.320
  722.7 4.3 copy.164
  726.9 53.8 %all_to_all.22 = bf16[16,16,4,2048]{3,2,0,1:T(4,128)(2,1)S(1)} all-to-all(bf16[16,16,4,2048]{3,2,0,1:T(4,128)(2,1)S(1)} %copy.164), channel_id=1, replica_groups=mesh['ctx'=16,'exp'=16] {'ctx'}, dimensions={1} | all-to-all | bytes 8388608 | tf_op jit(solution)/shard_map/all_to_all | solution.py:211
  780.7 4.0 copy.165
  784.8 7.8 all-to-all-start.3
  794.6 90.5 %all-to-all-done.3 = bf16[16,16,4,2048]{3,2,1,0:T(4,128)(2,1)} async-done(((bf16[16,16,4,2048]{3,2,1,0:T(4,128)(2,1)}), bf16[16,16,4,2048]{3,2,1,0:T(4,128)(2,1)}, u32[]{:S(2)}, u32[]{:S(2)}) %all-to-all-start.3) | async-done | bytes 4194336 | tf_op jit(solution)/shard_map/all_to_all | solution.py:212
  885.1 6.9 reshape.321
  892.0 9.7 %gather_fusion = bf16[640,2048]{1,0:T(8,128)(2,1)} fusion(bf16[1024,2048]{1,0:T(8,128)(2,1)} %reshape.321, s32[1024]{0:T(1024)S(1)} %pad_clamp_fusion), kind=kCustom, calls=%fused_computation | custom fusion | bytes 5245440 | tf_op jit(solution)/shard_map/gather | solution.py:213
  901.7 5.8 reshape.325
  907.5 5.8 multiply_reduce_fusion
  (223 shorter events, 120.9 us)
Async XLA Ops:
  7.2 704.0 %copy-start = (bf16[1,512,2048]{2,1,0:T(8,128)(2,1)S(1)}, bf16[1,512,2048]{2,1,0:T(8,128)(2,1)}, u32[]{:S(2)}) copy-start(bf16[1,512,2048]{2,1,0:T(8,128)(2,1)} %param.37) | copy-start | bytes 6291460
  7.2 279.6 %all-gather.7.cloned.1.call-start = ((), (), s32[]{:S(2)}) async-start(), calls=%async_computation.7 | async-start | bytes 1114112 | tf_op jit(solution)/shard_map/all_gather | solution.py:24
  180.2 15.6 %copy-start.2 = (f32[16,2,64,128]{3,2,1,0:T(8,128)}, f32[16,2,64,128]{3,2,1,0:T(8,128)S(1)}, u32[]{:S(2)}) copy-start(f32[16,2,64,128]{3,2,1,0:T(8,128)S(1)} %fusion.54) | copy-start | bytes 3145732
  184.2 1.0 copy-start.1
  195.9 41.5 %copy-start.4 = (bf16[1024,128]{1,0:T(8,128)(2,1)S(1)}, bf16[1024,128]{1,0:T(8,128)(2,1)}, u32[]{:S(2)}) copy-start(bf16[1024,128]{1,0:T(8,128)(2,1)} %param.23) | copy-start | bytes 786436
  195.9 41.7 %copy-start.11 = (f32[128]{0:T(128)S(1)}, f32[128]{0:T(128)}, u32[]{:S(2)}) copy-start(f32[128]{0:T(128)} %param.29) | copy-start | bytes 1540
  236.3 100.5 %all-gather.5.cloned.1.call-start = ((), (), s32[]{:S(2)}) async-start(), calls=%async_computation.6 | async-start | bytes 1114112 | tf_op jit(solution)/shard_map/all_gather | solution.py:24
  237.1 266.7 %reduce-scatter.2.cloned.1.call-start = ((), (), s32[]{:S(2)}) async-start(), calls=%async_computation.5 | async-start | bytes 4456448 | tf_op jit(solution)/shard_map/reduce_scatter | solution.py:170
  418.9 5.3 copy-start.6
  420.8 4.7 copy-start.5
  424.7 0.8 copy-start.3
  425.5 3.2 copy-start.8
  425.5 3.2 copy-start.10
  428.7 75.1 %copy-start.7 = (bf16[64,2048]{1,0:T(8,128)(2,1)S(1)}, bf16[64,2048]{1,0:T(8,128)(2,1)}, u32[]{:S(2)}) copy-start(bf16[64,2048]{1,0:T(8,128)(2,1)} %param.31) | copy-start | bytes 786436
  428.7 76.2 %copy-start.9 = (f32[2048]{0:T(1024)S(1)}, f32[2048]{0:T(1024)}, u32[]{:S(2)}) copy-start(f32[2048]{0:T(1024)} %param.32) | copy-start | bytes 24580
  784.8 100.3 %all-to-all-start.3 = ((bf16[16,16,4,2048]{3,2,1,0:T(4,128)(2,1)}), bf16[16,16,4,2048]{3,2,1,0:T(4,128)(2,1)}, u32[]{:S(2)}, u32[]{:S(2)}) async-start(bf16[16,16,4,2048]{3,2,1,0:T(4,128)(2,1)} %copy.165), calls=%async_computation.4 | async-start | bytes 8388608 | tf_op jit(solution)/shard_map/all_to_all | solution.py:212
Sparse Core Ops, SparseCore 0:
  236.4 50.3 all-gather.6
  289.8 47.0 all-gather.4
  428.8 74.9 reduce-scatter.1
where the time goes:
time: 932 us; the launch traced here: 921 us
  waiting for transfers between devices  258 us (28%)
  blocking collectives  213 us (23%)
  other arithmetic  177 us (19%)
  matrix products  160 us (17%)
  local copies, waits for them, and re-layouts  89 us (10%)
  between operations  14.6 us (2%)
    another operation x3, other arithmetic, lower_solve(): lax.linalg.triangular_solve(system, rhs, left_side=True, lower=True, unit...  159 us
    all_to_all x1, blocking collectives, local(): lax.all_to_all(outgoing, 'exp', split_axis=0, concat_axis=0, tiled=True)  101 us
    all_gather x2, waiting for transfers between devices, entering(): lax.all_gather(a.astype(kind), axis)  94.6 us
    all_to_all x1, waiting for transfers between devices, local(): lax.all_to_all(finished, 'exp', split_axis=0, concat_axis=0, tiled=True)  90.5 us
    reduce_scatter x1, waiting for transfers between devices, local(): lax.psum_scatter(jnp.dot(core_out, out_weight, preferred_element_type=jnp...  73.2 us
    all_to_all x1, blocking collectives, local(): lax.all_to_all(arrived, 'ctx', split_axis=1, concat_axis=1, tiled=True)  57.7 us
    all_to_all x1, blocking collectives, local(): lax.all_to_all(computed, 'ctx', split_axis=1, concat_axis=1, tiled=True)  53.8 us
    dot_general x32, matrix products, matmul_heads(): return jnp.einsum('...ij,...jk->...ik', left, right, precision=HIGH)  38.7 us
  transfers between devices with their start and end apart: 4, of which 4 were waited for; matrix products, arithmetic and copies ran while one was open for 1% of the time, Pallas kernels for 0%

commit v1 on v0

v1 whole, which is shorter than its diff:
```python
import math

import jax
import jax.numpy as jnp
from jax import lax
from jax.experimental import pallas as pl
from jax.experimental.pallas import tpu as pltpu
from jax.sharding import PartitionSpec as P

F32=jnp.float32; BF=jnp.bfloat16
EPS=1e-6
C=64
K=128
UNROLL = 4

def mm(a,b):
    return lax.dot_general(a,b,(((1,),(0,)),((),())),preferred_element_type=F32)

def split(a):
    hi=a.astype(BF)
    return hi,(a-hi.astype(F32)).astype(BF)

def mm3(a,b):
    ah,al=split(a); bh,bl=split(b)
    return mm(ah,bh)+(mm(al,bh)+mm(ah,bl))

def mm1(a,b):
    return mm(a.astype(BF),b.astype(BF))

def delta_kernel(q_ref,k_ref,v_ref,row_ref,col_ref,go_g,go_o,z_out,wq_s,u_s,p_s,kw_s,dr_s,z_s,el_s):
    n=q_ref.shape[0]//C
    rows=lax.broadcasted_iota(jnp.int32,(2*C,2*C),0)
    cols=lax.broadcasted_iota(jnp.int32,(2*C,2*C),1)
    same=(rows//C)==(cols//C)
    strict=same&(rows>cols)
    within=same&(rows>=cols)
    lane=lax.broadcasted_iota(jnp.int32,(2*C,128),1)
    half=lax.broadcasted_iota(jnp.int32,(2*C,1),0)<C
    levels=[]
    b=1
    while b<C:
        levels.append(strict&((rows//(2*b))==(cols//(2*b)))&((rows//b)!=(cols//b)))
        b*=2
    def unit(m):
        return m*lax.rsqrt(jnp.sum(m*m,axis=-1,keepdims=True)+EPS)
    def prep(step,carry):
        amat=[];xs=[];rhs=[];kts=[];ids=[]
        allc=col_ref[...]
        for u in range(UNROLL):
            c=step*UNROLL+u
            ids.append(c)
            at=pl.ds(pl.multiple_of(c*C,C),C)
            kk=unit(k_ref[at,:].astype(F32))
            qq=unit(q_ref[at,:].astype(F32))*(1.0/math.sqrt(K))
            k2=jnp.concatenate([kk,kk],0)
            q2=jnp.concatenate([qq,qq],0)
            kt=k2.T
            mix=mm3(jnp.concatenate([k2,q2],0),kt)
            g_row=row_ref[pl.ds(c,1),:]
            last_row=row_ref[pl.ds(n+c,1),:]
            g_col=jnp.sum(jnp.where(lane==c,allc,0.0),axis=1,keepdims=True)
            b_col=jnp.sum(jnp.where(lane==n+c,allc,0.0),axis=1,keepdims=True)
            fall=jnp.exp(jnp.where(within,g_col-g_row,0.0))
            a=jnp.where(strict,fall*b_col*mix[:2*C],0.0)
            p_s[c]=jnp.where(within,fall*mix[2*C:],0.0).astype(BF)
            eg=jnp.exp(g_col)
            vv=v_ref[at,:].astype(F32)
            v2=jnp.concatenate([vv[:,:K],vv[:,K:]],0)
            rhs.append(jnp.concatenate([(b_col*eg)*k2,b_col*v2],1))
            wq_s[c,1]=(eg*q2).astype(BF)
            kts.append(kt*jnp.exp(last_row-g_row))
            el_s[c]=jnp.exp(last_row)
            amat.append(a)
            xs.append(jnp.where(rows==cols,1.0,0.0)-jnp.where(levels[0],a,0.0))
        for lev in levels[1:]:
            mids=[mm3(jnp.where(lev,a,0.0),x) for a,x in zip(amat,xs)]
            xs=[x-mm3(x,m) for x,m in zip(xs,mids)]
        wus=[mm3(x,r) for x,r in zip(xs,rhs)]
        for c,wu,kt in zip(ids,wus,kts):
            wq_s[c,0]=wu[:,:K].astype(BF)
            u_s[c]=wu[:,K:]
            both=jnp.concatenate([jnp.where(half,wu,0.0),jnp.where(half,0.0,wu)],1)
            td=mm3(kt,both)
            for h in range(2):
                kw_s[h,c]=td[:,h*2*K:h*2*K+K]
                dr_s[h,c]=td[:,h*2*K+K:(h+1)*2*K]
        return carry
    lax.fori_loop(0,n//UNROLL,prep,0)
    eye=jnp.where(lax.broadcasted_iota(jnp.int32,(K,K),0)==lax.broadcasted_iota(jnp.int32,(K,K),1),1.0,0.0)
    start=jnp.concatenate([eye,jnp.zeros((K,K),F32)],1)
    def chain(c,zs):
        new=[]
        el=el_s[c]
        for h in range(2):
            z=zs[h]
            z_s[c,h]=z.astype(BF)
            e=jnp.sum(jnp.where(lax.broadcasted_iota(jnp.int32,(1,2*C),1)==h*C,el,0.0),axis=1,keepdims=True)
            t=e*z-mm3(kw_s[h,c],z)
            new.append(jnp.concatenate([t[:,:K],t[:,K:]+dr_s[h,c]],1))
        return tuple(new)
    zs=lax.fori_loop(0,n,chain,(start,start))
    for h in range(2):
        z_out[h]=zs[h].astype(BF)
    def emit(step,carry):
        for u in range(UNROLL):
            c=step*UNROLL+u
            fresh=[];outs=[]
            for h in range(2):
                z=z_s[c,h]
                w=wq_s[c,0,h*C:(h+1)*C,:]
                q=wq_s[c,1,h*C:(h+1)*C,:]
                r=mm(jnp.concatenate([w,q],0),z)
                f=-r[:C]
                uu=u_s[c,h*C:(h+1)*C,:]
                fresh.append(jnp.concatenate([f[:,:K],f[:,K:]+uu],1))
                outs.append(r[C:])
            out=jnp.concatenate(outs,0)+mm(p_s[c],jnp.concatenate(fresh,0).astype(BF))
            at=pl.ds(pl.multiple_of(c*C,C),C)
            for h in range(2):
                go_g[h,at,:]=out[h*C:(h+1)*C,:K].astype(BF)
                go_o[h,at,:]=out[h*C:(h+1)*C,K:]
        return carry
    lax.fori_loop(0,n//UNROLL,emit,0)

def delta_local(q,k,v,ld,beta):
    t=q.shape[0]; n=t//C
    g=jnp.cumsum(ld.reshape(2,n,C),axis=-1)
    last=jnp.broadcast_to(g[:,:,-1:],g.shape)
    pack=lambda a: jnp.transpose(a,(1,0,2)).reshape(n,2*C)
    row=jnp.concatenate([pack(g),pack(last)],0)
    col=jnp.zeros((2*C,128),F32)
    col=jnp.concatenate([pack(g).T,pack(beta.reshape(2,n,C)).T,jnp.zeros((2*C,128-2*n),F32)],1)
    vm=pl.BlockSpec(memory_space=pltpu.VMEM)
    return pl.pallas_call(
        delta_kernel,
        out_shape=(jax.ShapeDtypeStruct((2,t,K),BF),jax.ShapeDtypeStruct((2,t,K),F32),jax.ShapeDtypeStruct((2,K,2*K),BF)),
        in_specs=[vm]*5,out_specs=(vm,vm,vm),
        scratch_shapes=[pltpu.VMEM((n,2,2*C,K),BF),pltpu.VMEM((n,2*C,K),F32),pltpu.VMEM((n,2*C,2*C),BF),
            pltpu.VMEM((2,n,K,K),F32),pltpu.VMEM((2,n,K,K),F32),pltpu.VMEM((n,2,K,2*K),BF),pltpu.VMEM((n,1,2*C),F32)],
        compiler_params=pltpu.CompilerParams(vmem_limit_bytes=48*2**20),
    )(q,k,v,row,col)


CAP = 4
GROUP = 4
TOK = 64
SIDE = 4
D = 2048
VM = pl.BlockSpec(memory_space=pltpu.VMEM)


def params(mib):
    return pltpu.CompilerParams(vmem_limit_bytes=mib * 2**20)


def fold_kernel(x_ref, own, a1, a2, a3, total_ref, prefix_ref):
    x = x_ref[0]
    eye = jnp.where(
        lax.broadcasted_iota(jnp.int32, (K, K), 0) == lax.broadcasted_iota(jnp.int32, (K, K), 1),
        1.0,
        0.0,
    )
    for h in range(2):
        near = [own[h].astype(F32), a1[h].astype(F32), a2[h].astype(F32), a3[h].astype(F32)]
        z = jnp.concatenate([eye, jnp.zeros((K, K), F32)], 1)
        prefix = z
        for j in range(SIDE):
            item = near[0]
            for d in range(1, SIDE):
                item = jnp.where((x - j) % SIDE == d, near[d], item)
            if j == 0:
                z = item
            else:
                zh, zl = split(z)
                m = item[:, :K].astype(BF)
                t = mm(m, zh) + mm(m, zl)
                z = jnp.concatenate([t[:, :K], t[:, K:] + item[:, K:]], 1)
            if j < SIDE - 1:
                prefix = jnp.where(x == j + 1, z, prefix)
        total_ref[h] = z.astype(BF)
        prefix_ref[h] = prefix


def core_kernel(par_ref, g_ref, o_ref, prefix, b1, b2, b3, gate_ref, gain_ref, core_ref, mine, sib):
    gain = gain_ref[...]
    even = par_ref[0] == 0
    state = []
    for h in range(2):
        e = b3[h][:, K:].astype(F32)
        for b in (b2, b1):
            eh, el = split(e)
            m = b[h][:, :K]
            e = mm(m, eh) + mm(m, el) + b[h][:, K:].astype(F32)
        e = mm3(prefix[h][:, :K], e) + prefix[h][:, K:]
        eh, el = split(e)
        state.append(jnp.concatenate([eh, el], 1))
    step = 2 * TOK

    def body(i, carry):
        at = pl.ds(pl.multiple_of(i * step, step), step)
        outs = []
        for h in range(2):
            both = mm(g_ref[h, at, :], state[h])
            core = o_ref[h, at, :] + both[:, :K] + both[:, K:]
            gate = gate_ref[at, h * K : (h + 1) * K].astype(F32)
            scaled = core * lax.rsqrt(jnp.mean(core * core, axis=-1, keepdims=True) + EPS)
            outs.append((scaled * gain * (gate / (1.0 + jnp.exp(-gate)))).astype(BF))
        out = jnp.concatenate(outs, 1)
        core_ref[at, :] = out
        to = pl.ds(pl.multiple_of(i * TOK, TOK), TOK)
        mine[to, :] = jnp.where(even, out[:TOK], out[TOK:])
        sib[to, :] = jnp.where(even, out[TOK:], out[:TOK])
        return carry

    lax.fori_loop(0, g_ref.shape[1] // step, body, 0)


def project_kernel(a_ref, b_ref, wa_ref, wb_ref, out_ref):
    out_ref[...] = (mm(a_ref[...], wa_ref[...]) + mm(b_ref[...], wb_ref[...])).astype(BF)


def project(a, b, wa, wb):
    rows, depth = a.shape
    wide = 512
    return pl.pallas_call(
        project_kernel,
        grid=(D // wide,),
        out_shape=jax.ShapeDtypeStruct((rows, D), BF),
        in_specs=[
            pl.BlockSpec((rows, depth), lambda i: (0, 0)),
            pl.BlockSpec((rows, depth), lambda i: (0, 0)),
            pl.BlockSpec((depth, wide), lambda i: (0, i)),
            pl.BlockSpec((depth, wide), lambda i: (0, i)),
        ],
        out_specs=pl.BlockSpec((rows, wide), lambda i: (0, i)),
        compiler_params=params(40),
    )(a, b, wa, wb)


def dispatch_kernel(sel_ref, rows_ref, out_ref):
    out = lax.dot_general(
        sel_ref[...], rows_ref[...], (((0,), (0,)), ((), ())), preferred_element_type=F32
    ).astype(BF)
    out_ref[...] = out.reshape(out_ref.shape)


def dispatch(sel, rows):
    n_ctx = 16
    part = GROUP * TOK
    return pl.pallas_call(
        dispatch_kernel,
        grid=(rows.shape[0] // part,),
        out_shape=jax.ShapeDtypeStruct((n_ctx, TOK, D), BF),
        in_specs=[
            pl.BlockSpec((part, sel.shape[1]), lambda g: (g, 0)),
            pl.BlockSpec((part, D), lambda g: (g, 0)),
        ],
        out_specs=pl.BlockSpec((n_ctx, GROUP * CAP, D), lambda g: (0, g, 0)),
        compiler_params=params(40),
    )(sel, rows)


def expert_kernel(x_ref, up_ref, down_ref, out_ref):
    hidden = mm(x_ref[...], up_ref[...])
    width = down_ref.shape[0]
    gate = hidden[:, :width]
    act = (gate / (1.0 + jnp.exp(-gate)) * hidden[:, width:]).astype(BF)
    out_ref[...] = mm(act, down_ref[...]).astype(BF)


def expert(x, gate_up, down):
    part = 256
    return pl.pallas_call(
        expert_kernel,
        grid=(x.shape[0] // part,),
        out_shape=jax.ShapeDtypeStruct(x.shape, BF),
        in_specs=[
            pl.BlockSpec((part, D), lambda i: (i, 0)),
            pl.BlockSpec(gate_up.shape, lambda i: (0, 0)),
            pl.BlockSpec(down.shape, lambda i: (0, 0)),
        ],
        out_specs=pl.BlockSpec((part, D), lambda i: (i, 0)),
        compiler_params=params(48),
    )(x, gate_up, down)


def combine_kernel(par_ref, w_ref, y_ref, mine, sib):
    even = par_ref[0] == 0
    rows = y_ref[...].reshape(w_ref.shape[1], D)
    out = mm(w_ref[...], rows).astype(BF)
    for i in range(GROUP // 2):
        a = out[2 * i * TOK : (2 * i + 1) * TOK]
        b = out[(2 * i + 1) * TOK : (2 * i + 2) * TOK]
        mine[i * TOK : (i + 1) * TOK, :] = jnp.where(even, a, b)
        sib[i * TOK : (i + 1) * TOK, :] = jnp.where(even, b, a)


def combine(parity, weights, y):
    part = GROUP * TOK
    rows = weights.shape[0]
    half = jax.ShapeDtypeStruct((rows // 2, D), BF)
    return pl.pallas_call(
        combine_kernel,
        grid=(rows // part,),
        out_shape=(half, half),
        in_specs=[
            pl.BlockSpec(memory_space=pltpu.SMEM),
            pl.BlockSpec((part, weights.shape[1]), lambda g: (g, 0)),
            pl.BlockSpec((y.shape[0], GROUP * CAP, D), lambda g: (0, g, 0)),
        ],
        out_specs=(
            pl.BlockSpec((part // 2, D), lambda g: (g, 0)),
            pl.BlockSpec((part // 2, D), lambda g: (g, 0)),
        ),
        compiler_params=params(40),
    )(parity, weights, y)


def along_x(d):
    return [(i, (i // SIDE) * SIDE + (i % SIDE + d) % SIDE) for i in range(SIDE * SIDE)]


def along_y(d):
    return [(i, i + SIDE * d) for i in range(SIDE * (SIDE - d))]


def local(
    query_raw,
    key_raw,
    values,
    out_gate,
    log_decay,
    beta_rate,
    head_gain,
    out_weight,
    residual,
    post_gain,
    router_weight,
    routes,
    placement,
    expert_in,
    expert_out,
):
    n_exp = lax.axis_size("exp")
    experts = router_weight.shape[1]
    at_exp = lax.axis_index("exp")
    at_x = (lax.axis_index("ctx") % SIDE).reshape(1)
    parity = (at_exp % 2).reshape(1)
    core_pairs = [(i, i ^ 1) for i in range(n_exp)]
    same_core = [list(range(0, n_exp, 2)), list(range(1, n_exp, 2))]

    routes_all = lax.all_gather(routes, "exp", tiled=True)
    weight_sib = lax.ppermute(out_weight, "exp", core_pairs)

    g, o, z = delta_local(query_raw, key_raw, values, log_decay, beta_rate)
    near = [lax.ppermute(z, "ctx", along_x(d)) for d in range(1, SIDE)]
    whole = jax.ShapeDtypeStruct(z.shape, BF)
    total, prefix = pl.pallas_call(
        fold_kernel,
        out_shape=(whole, jax.ShapeDtypeStruct(z.shape, F32)),
        in_specs=[pl.BlockSpec(memory_space=pltpu.SMEM)] + [VM] * 4,
        out_specs=(VM, VM),
        compiler_params=params(32),
    )(at_x, z, *near)
    far = [lax.ppermute(total, "ctx", along_y(d)) for d in range(1, SIDE)]
    half = jax.ShapeDtypeStruct((values.shape[0] // 2, values.shape[1]), BF)
    core_out, mine, sib = pl.pallas_call(
        core_kernel,
        out_shape=(jax.ShapeDtypeStruct(values.shape, BF), half, half),
        in_specs=[pl.BlockSpec(memory_space=pltpu.SMEM)] + [VM] * 8,
        out_specs=(VM, VM, VM),
        compiler_params=params(40),
    )(parity, g, o, prefix, *far, out_gate, head_gain.reshape(1, K))

    got = lax.ppermute(sib, "exp", core_pairs)
    terms = project(mine, got, out_weight, weight_sib)
    attn = lax.psum_scatter(
        terms, "exp", scatter_dimension=0, tiled=True, axis_index_groups=same_core
    ).astype(F32)
    mid = lax.optimization_barrier((residual.astype(F32) + attn).astype(BF)).astype(F32)
    normed = (mid / jnp.sqrt(jnp.mean(mid * mid, axis=-1, keepdims=True) + EPS) * post_gain).astype(
        BF
    )
    normed_all = lax.all_gather(normed, "exp", tiled=True)

    rows = routes_all.shape[0]
    ids = jnp.arange(experts, dtype=jnp.int32)
    chosen = jnp.any(routes_all[:, :, None] == ids[None, None, :], axis=1)
    wide = n_exp * GROUP * CAP
    lanes = jnp.arange(wide, dtype=jnp.int32)
    holder = (lanes // (GROUP * CAP)) * n_exp + at_exp
    spread = (placement[:, None] == holder[None, :]).astype(BF)
    named = jnp.dot(chosen.astype(BF), spread, preferred_element_type=F32)
    order = jnp.arange(TOK, dtype=jnp.int32)
    before = (order[:, None] > order[None, :]).astype(BF)
    rank = jnp.einsum(
        "ts,bsl->btl",
        before,
        named.astype(BF).reshape(rows // TOK, TOK, wide),
        preferred_element_type=F32,
    ).reshape(rows, wide)
    block = (jnp.arange(rows, dtype=jnp.int32) // TOK) % GROUP
    sel = (
        (named > 0.5)
        & (rank == (lanes % CAP).astype(F32)[None, :])
        & (block[:, None] == ((lanes // CAP) % GROUP)[None, :])
    )

    logits = jnp.dot(normed_all, router_weight, preferred_element_type=F32)
    raised = jnp.where(chosen, jnp.exp(logits), 0.0)
    gates = raised / jnp.sum(raised, axis=-1, keepdims=True)
    mine_gates = jnp.dot(gates, spread.astype(F32), precision=lax.Precision.HIGHEST)
    weights = jnp.where(sel, mine_gates, 0.0).astype(BF)

    outgoing = dispatch(sel.astype(BF), normed_all)
    arrived = lax.all_to_all(outgoing, "ctx", split_axis=0, concat_axis=0, tiled=True)
    computed = expert(arrived.reshape(-1, D), expert_in[0], expert_out[0]).reshape(arrived.shape)
    returned = lax.all_to_all(computed, "ctx", split_axis=0, concat_axis=0, tiled=True)
    mine_sum, sib_sum = combine(parity, weights, returned)
    got_sum = lax.ppermute(sib_sum, "exp", core_pairs)
    pair = (mine_sum.astype(F32) + got_sum.astype(F32)).astype(BF)
    mixture = lax.psum_scatter(
        pair, "exp", scatter_dimension=0, tiled=True, axis_index_groups=same_core
    ).astype(F32)
    return (core_out, (mid + mixture).astype(BF))


def solution(mesh):
    placed = (
        P("ctx", "exp"),
        P("ctx", "exp"),
        P("ctx", "exp"),
        P("ctx", "exp"),
        P("exp", "ctx"),
        P("exp", "ctx"),
        P(),
        P("exp", None),
        P(("ctx", "exp"), None),
        P(),
        P(),
        P(("ctx", "exp"), None),
        P(),
        P(("ctx", "exp"), None, None),
        P(("ctx", "exp"), None, None),
    )
    return jax.shard_map(
        local,
        mesh=mesh,
        in_specs=placed,
        out_specs=(P("ctx", "exp"), P(("ctx", "exp"), None)),
        check_vma=False,
    )
```

time: 932 us -> 362 us (0.39)
  other arithmetic: 177 us -> 8.66 us
  matrix products: 160 us -> 4.94 us
  blocking collectives: 213 us -> 73.4 us
  waiting for transfers between devices: 258 us -> 175 us
  local copies, waits for them, and re-layouts: 89 us -> 14.4 us
  Pallas kernels: 0 us -> 48.6 us
  starting transfers between devices: 7.96 us -> 21.4 us
    another operation x6 -> x1, other arithmetic: 160 us -> 0.44 us  [delta_local(): g = jnp.cumsum(ld.reshape(2, n, C), axis=-1)]
    all_to_all x3 -> x1, blocking collectives: 213 us -> 58 us  [local(): lax.all_to_all(outgoing, 'ctx', split_axis=0, concat_axis=0, tiled=True)]
    dot_general x104 -> x4, matrix products: 153 us -> 4.94 us  [the longest x1 3.53 us: local(): logits = jnp.dot(normed_all, router_weight, preferred_element_type=F32)]
    all_gather x2 -> x1, waiting for transfers between devices: 94.6 us -> 23.1 us  [local(): normed_all = lax.all_gather(normed, 'exp', tiled=True)]
    pallas_call x0 -> x7, Pallas kernels: none -> 48.6 us  [the longest x1 19.9 us: delta_local(): pl.pallas_call(delta_kernel, out_shape=(jax.ShapeDtypeStruct((2, t, K), B...]
    reshape x9 -> x5, local copies, waits for them, and re-layouts: 39.8 us -> 1.98 us  [the longest x1 0.94 us: delta_local(): g = jnp.cumsum(ld.reshape(2, n, C), axis=-1)]
    all_to_all x1, waiting for transfers between devices: 90.5 us -> 56.7 us  [local(): lax.all_to_all(computed, 'ctx', split_axis=0, concat_axis=0, tiled=True)]
    ppermute x0 -> x9, starting transfers between devices: none -> 16.7 us  [the longest x3 10.9 us: local(): far = [lax.ppermute(total, 'ctx', along_y(d)) for d in range(1, SIDE)]]
  transfers between devices with their start and end apart: 4 -> 13, of which waited for: 4 -> 10; matrix products, arithmetic and copies ran while one was open for 1% -> 3% of each run, Pallas kernels for 0% -> 7%
where the time goes in v1:
time: 362 us; the launch traced here: 360 us
  waiting for transfers between devices  175 us (48%)
  blocking collectives  73.4 us (20%)
  Pallas kernels  48.6 us (13%)
  starting transfers between devices  21.4 us (6%)
  local copies, waits for them, and re-layouts  14.4 us (4%)
  between operations  14 us (4%)
  other arithmetic  8.66 us (2%)
  matrix products  4.94 us (1%)
    all_to_all x1, blocking collectives, local(): lax.all_to_all(outgoing, 'ctx', split_axis=0, concat_axis=0, tiled=True)  58 us
    all_to_all x1, waiting for transfers between devices, local(): lax.all_to_all(computed, 'ctx', split_axis=0, concat_axis=0, tiled=True)  56.7 us
    reduce_scatter x1, waiting for transfers between devices, local(): lax.psum_scatter(terms, 'exp', scatter_dimension=0, tiled=True, axis_inde...  43.8 us
    reduce_scatter x1, waiting for transfers between devices, local(): lax.psum_scatter(pair, 'exp', scatter_dimension=0, tiled=True, axis_index...  38.7 us
    all_gather x1, waiting for transfers between devices, local(): normed_all = lax.all_gather(normed, 'exp', tiled=True)  23.1 us
    pallas_call x1, Pallas kernels, delta_local(): pl.pallas_call(delta_kernel, out_shape=(jax.ShapeDtypeStruct((2, t, K), B...  19.9 us
    all_gather x1, blocking collectives, local(): routes_all = lax.all_gather(routes, 'exp', tiled=True)  15.4 us
    unnamed x39, local copies, waits for them, and re-layouts  11.9 us
  transfers between devices with their start and end apart: 13, of which 10 were waited for; matrix products, arithmetic and copies ran while one was open for 3% of the time, Pallas kernels for 7%

profile of v1, /device:TPU:32, one launch (start us, length us, event | category | flops | bytes accessed | tf_op | source)
XLA Modules:
  0.0 360.0 jit_solution(7743208675273191407)
XLA Ops:
  7.3 0.9 reshape.125
  8.3 0.4 reduce_window_sum.11
  9.3 0.8 reshape.128
  10.4 1.0 copy-done.7
  11.4 0.9 copy-done.8
  12.4 0.9 copy-done.9
  13.3 19.9 %shard_map.158 = (bf16[2,1024,128]{2,1,0:T(8,128)(2,1)S(1)}, f32[2,1024,128]{2,1,0:T(8,128)S(1)}, bf16[2,128,256]{2,1,0:T(8,128)(2,1)S(1)}) custom-call(bf16[1024,128]{1,0:T(8,128)(2,1)S(1)} %copy-done.8, bf16[1024,128]{1,0:T(8,128)(2,1)S(1)} %copy-done.9, bf16[1024,256]{1,0:T(8,128)(2,1)S(1)} %copy-done.7, f32[32,128]{1,0:T(8,128)S(1)} %pad_maximum_fusion.row_ref, ...), custom_call_target="tpu_custom_call" | custom-call | tf_op jit(solution)/shard_map/pallas_call | solution.py:134
  33.2 0.8 copy-done.5
  34.0 1.5 collective-permute-start
  35.5 2.7 collective-permute-start.1
  38.2 1.4 collective-permute-start.2
  39.7 1.3 collective-permute-done.a1
  41.0 0.7 copy-done.10
  41.6 3.1 collective-permute-done.1.a2
  44.8 0.6 copy-done.12
  45.4 0.9 copy-done.11
  46.3 0.9 copy-done.13
  47.2 2.4 shard_map.159
  49.6 3.5 collective-permute-start.3
  53.1 5.5 %collective-permute-start.4 = (bf16[2,128,256]{2,1,0:T(8,128)(2,1)}, bf16[2,128,256]{2,1,0:T(8,128)(2,1)}, u32[]{:S(2)}, u32[]{:S(2)}) collective-permute-start(bf16[2,128,256]{2,1,0:T(8,128)(2,1)} %get-tuple-element.16), channel_id=1, source_target_pairs={{0,128},{16,144},{32,160},{48,176},{64,192},{80,208},{96,224},{112... | collective-permute-start | bytes 393224 | tf_op jit(solution)/shard_map/ppermute | solution.py:365
  58.6 1.9 collective-permute-start.5
  60.8 1.9 collective-permute-done.5.b3
  62.7 1.0 copy-done.4
  63.7 1.0 copy-done.6
  64.8 0.7 copy-done.14
  65.4 4.6 %shard_map.160 = (bf16[1024,256]{1,0:T(8,128)(2,1)}, bf16[512,256]{1,0:T(8,128)(2,1)S(1)}, bf16[512,256]{1,0:T(8,128)(2,1)S(1)}) custom-call(s32[1]{0:T(128)} %bitcast.par_ref, bf16[2,1024,128]{2,1,0:T(8,128)(2,1)S(1)} %copy-done.6, f32[2,1024,128]{2,1,0:T(8,128)S(1)} %get-tuple-element.13.o_ref, f32[2,128,256]{2,1,0:T(8,128)S(1)} %get-tuple-element.15.prefix, ...), custom_call_target="tpu_custom_call" | custom-call | tf_op jit(solution)/shard_map/pallas_call | solution.py:367
  70.1 1.5 collective-permute-done.6.b_ref
  71.6 4.6 %shard_map.161 = bf16[512,2048]{1,0:T(8,128)(2,1)} custom-call(bf16[512,256]{1,0:T(8,128)(2,1)S(1)} %get-tuple-element.18.a_ref, bf16[512,256]{1,0:T(8,128)(2,1)S(1)} %collective-permute-done.6.b_ref, bf16[256,2048]{1,0:T(8,128)(2,1)S(1)} %copy-done.3, bf16[256,2048]{1,0:T(8,128)(2,1)} %collective-permute-done.7.wb_ref), custom_call_target="tpu_custom_call" | custom-call | tf_op jit(solution)/shard_map/pallas_call | solution.py:225
  76.3 43.8 %reduce-scatter.3.cloned.1.call-done = bf16[64,2048]{1,0:T(8,128)(2,1)} async-done(((bf16[512,2048]{1,0:T(8,128)(2,1)}), bf16[64,2048]{1,0:T(8,128)(2,1)}) %reduce-scatter.3.cloned.1.call-update) | async-done | bytes 262160 | tf_op jit(solution)/shard_map/reduce_scatter | solution.py:377
  120.1 1.0 add_convert_fusion.1
  121.3 0.8 fusion.8
  122.2 15.4 %all-gather = s32[16,64,10]{1,2,0:T(8,128)S(1)} all-gather(s32[1,64,10]{1,2,0:T(8,128)S(1)} %bitcast.50), channel_id=1, replica_groups=mesh['ctx'=16,'exp'=16] {'exp'}, dimensions={0}, use_global_device_ids=true | all-gather | bytes 43520 | tf_op jit(solution)/shard_map/all_gather | solution.py:352
  137.7 1.9 fusion
  139.7 0.4 fusion.33
  140.7 23.1 %all-gather.3.cloned.1.call-done.rows_ref = bf16[1024,2048]{1,0:T(8,128)(2,1)} async-done(((bf16[64,2048]{1,0:T(8,128)(2,1)}), bf16[1024,2048]{1,0:T(8,128)(2,1)}) %all-gather.3.cloned.1.call-update) | async-done | bytes 4194320 | tf_op jit(solution)/shard_map/all_gather | solution.py:384
  163.8 2.2 copy-done.1
  166.0 2.1 shard_map.162
  168.1 58.0 %all_to_all.10 = bf16[16,64,2048]{2,1,0:T(8,128)(2,1)} all-to-all(bf16[16,64,2048]{2,1,0:T(8,128)(2,1)S(1)} %shard_map.162), channel_id=1, replica_groups=mesh['ctx'=16,'exp'=16] {'ctx'}, dimensions={0} | all-to-all | bytes 8388608 | tf_op jit(solution)/shard_map/all_to_all | solution.py:416
  226.1 11.0 %shard_map.163 = bf16[1024,2048]{1,0:T(8,128)(2,1)} custom-call(bf16[1024,2048]{1,0:T(8,128)(2,1)} %bitcast.42, bf16[2048,1024]{1,0:T(8,128)(2,1)} %bitcast.43, bf16[512,2048]{1,0:T(8,128)(2,1)S(1)} %bitcast.39), custom_call_target="tpu_custom_call" | custom-call | tf_op jit(solution)/shard_map/pallas_call | solution.py:273
  237.2 4.5 %all-to-all-start.1 = ((bf16[16,64,2048]{2,1,0:T(8,128)(2,1)}), bf16[16,64,2048]{2,1,0:T(8,128)(2,1)}, u32[]{:S(2)}, u32[]{:S(2)}) async-start(bf16[16,64,2048]{2,1,0:T(8,128)(2,1)} %bitcast.41), calls=%async_computation.2 | async-start | bytes 8388608 | tf_op jit(solution)/shard_map/all_to_all | solution.py:418
  241.8 3.5 fusion.34
  245.3 0.7 fusion.2.w_ref
  246.0 56.7 %all-to-all-done.1.y_ref = bf16[16,64,2048]{2,1,0:T(8,128)(2,1)} async-done(((bf16[16,64,2048]{2,1,0:T(8,128)(2,1)}), bf16[16,64,2048]{2,1,0:T(8,128)(2,1)}, u32[]{:S(2)}, u32[]{:S(2)}) %all-to-all-start.1) | async-done | bytes 4194336 | tf_op jit(solution)/shard_map/all_to_all | solution.py:418
  302.7 3.9 %shard_map.164 = (bf16[512,2048]{1,0:T(8,128)(2,1)S(1)}, bf16[512,2048]{1,0:T(8,128)(2,1)S(1)}) custom-call(s32[1]{0:T(128)} %bitcast.par_ref, bf16[1024,256]{1,0:T(8,128)(2,1)S(1)} %fusion.2.w_ref, bf16[16,64,2048]{2,1,0:T(8,128)(2,1)} %all-to-all-done.1.y_ref), custom_call_target="tpu_custom_call" | custom-call | tf_op jit(solution)/shard_map/pallas_call | solution.py:302
  306.7 4.1 %collective-permute-done.8 = bf16[512,2048]{1,0:T(8,128)(2,1)S(1)} collective-permute-done((bf16[512,2048]{1,0:T(8,128)(2,1)S(1)}, bf16[512,2048]{1,0:T(8,128)(2,1)S(1)}, u32[]{:S(2)}, u32[]{:S(2)}) %collective-permute-start.8) | collective-permute-done | bytes 2097184 | tf_op jit(solution)/shard_map/ppermute | solution.py:420
  310.9 2.1 add_convert_fusion
  313.0 38.7 %reduce-scatter.5.cloned.1.call-done = bf16[64,2048]{1,0:T(8,128)(2,1)} async-done(((bf16[512,2048]{1,0:T(8,128)(2,1)}), bf16[64,2048]{1,0:T(8,128)(2,1)}) %reduce-scatter.5.cloned.1.call-update) | async-done | bytes 262160 | tf_op jit(solution)/shard_map/reduce_scatter | solution.py:422
  351.7 1.7 fusion.9
  (59 shorter events, 2.4 us)
Async XLA Ops:
  7.2 234.6 %copy-start = (bf16[2048,256]{1,0:T(8,128)(2,1)S(1)}, bf16[2048,256]{1,0:T(8,128)(2,1)}, u32[]{:S(2)}) copy-start(bf16[2048,256]{1,0:T(8,128)(2,1)} %param.25) | copy-start | bytes 3145732
  7.2 64.4 %copy-start.3 = (bf16[256,2048]{1,0:T(8,128)(2,1)S(1)}, bf16[256,2048]{1,0:T(8,128)(2,1)}, u32[]{:S(2)}) copy-start(bf16[256,2048]{1,0:T(8,128)(2,1)} %wa_ref.1) | copy-start | bytes 3145732
  7.2 112.9 %reduce-scatter.3.cloned.1.call-start = ((), (), s32[]{:S(2)}) async-start(), calls=%async_computation.4 | async-start | bytes 2359296 | tf_op jit(solution)/shard_map/reduce_scatter | solution.py:377
  7.2 64.4 %collective-permute-start.7 = (bf16[256,2048]{1,0:T(8,128)(2,1)}, bf16[256,2048]{1,0:T(8,128)(2,1)}, u32[]{:S(2)}, u32[]{:S(2)}) collective-permute-start(bf16[256,2048]{1,0:T(8,128)(2,1)} %wa_ref.1), channel_id=1, source_target_pairs={{0,1},{1,0},{2,3},{3,2},{4,5},{5,4},{6,7},{7,6},{8,9},{9,8},{10,11... | collective-permute-start | bytes 3145736 | tf_op jit(solution)/shard_map/ppermute | solution.py:353
  10.4 1.0 copy-start.7
  11.4 0.9 copy-start.8
  12.4 0.9 copy-start.9
  33.2 0.8 copy-start.5
  34.0 6.9 %collective-permute-start = (bf16[2,128,256]{2,1,0:T(8,128)(2,1)S(1)}, bf16[2,128,256]{2,1,0:T(8,128)(2,1)S(1)}, u32[]{:S(2)}, u32[]{:S(2)}) collective-permute-start(bf16[2,128,256]{2,1,0:T(8,128)(2,1)S(1)} %get-tuple-element.14.own), channel_id=1, source_target_pairs={{0,16},{16,32},{32,48},{48,0},{64,80},{80,96},{96,112},{112,64},{1... | collective-permute-start | bytes 393224 | tf_op jit(solution)/shard_map/ppermute | solution.py:356
  35.5 9.2 %collective-permute-start.1 = (bf16[2,128,256]{2,1,0:T(8,128)(2,1)S(1)}, bf16[2,128,256]{2,1,0:T(8,128)(2,1)S(1)}, u32[]{:S(2)}, u32[]{:S(2)}) collective-permute-start(bf16[2,128,256]{2,1,0:T(8,128)(2,1)S(1)} %get-tuple-element.14.own), channel_id=1, source_target_pairs={{0,32},{16,48},{32,0},{48,16},{64,96},{80,112},{96,64},{112,80},{1... | collective-permute-start | bytes 393224 | tf_op jit(solution)/shard_map/ppermute | solution.py:356
  38.2 7.2 %collective-permute-start.2 = (bf16[2,128,256]{2,1,0:T(8,128)(2,1)S(1)}, bf16[2,128,256]{2,1,0:T(8,128)(2,1)}, u32[]{:S(2)}, u32[]{:S(2)}) collective-permute-start(bf16[2,128,256]{2,1,0:T(8,128)(2,1)S(1)} %get-tuple-element.14.own), channel_id=1, source_target_pairs={{0,48},{16,0},{32,16},{48,32},{64,112},{80,64},{96,80},{112,96},{1... | collective-permute-start | bytes 393224 | tf_op jit(solution)/shard_map/ppermute | solution.py:356
  41.0 0.7 copy-start.10
  44.8 0.6 copy-start.12
  45.4 0.9 copy-start.11
  46.3 0.9 copy-start.13
  49.6 10.9 %collective-permute-start.3 = (bf16[2,128,256]{2,1,0:T(8,128)(2,1)}, bf16[2,128,256]{2,1,0:T(8,128)(2,1)S(1)}, u32[]{:S(2)}, u32[]{:S(2)}) collective-permute-start(bf16[2,128,256]{2,1,0:T(8,128)(2,1)} %get-tuple-element.16), channel_id=1, source_target_pairs={{0,64},{16,80},{32,96},{48,112},{64,128},{80,144},{96,160},{112,17... | collective-permute-start | bytes 393224 | tf_op jit(solution)/shard_map/ppermute | solution.py:365
  53.1 7.6 %collective-permute-start.4 = (bf16[2,128,256]{2,1,0:T(8,128)(2,1)}, bf16[2,128,256]{2,1,0:T(8,128)(2,1)}, u32[]{:S(2)}, u32[]{:S(2)}) collective-permute-start(bf16[2,128,256]{2,1,0:T(8,128)(2,1)} %get-tuple-element.16), channel_id=1, source_target_pairs={{0,128},{16,144},{32,160},{48,176},{64,192},{80,208},{96,224},{112... | collective-permute-start | bytes 393224 | tf_op jit(solution)/shard_map/ppermute | solution.py:365
  58.6 4.1 %collective-permute-start.5 = (bf16[2,128,256]{2,1,0:T(8,128)(2,1)}, bf16[2,128,256]{2,1,0:T(8,128)(2,1)}, u32[]{:S(2)}, u32[]{:S(2)}) collective-permute-start(bf16[2,128,256]{2,1,0:T(8,128)(2,1)} %get-tuple-element.16), channel_id=1, source_target_pairs={{0,192},{16,208},{32,224},{48,240},{1,193},{17,209},{33,225},{49,2... | collective-permute-start | bytes 393224 | tf_op jit(solution)/shard_map/ppermute | solution.py:365
  62.7 1.0 copy-start.4
  63.7 1.0 copy-start.6
  64.8 0.7 copy-start.14
  70.1 50.0 %copy-start.15 = (bf16[64,2048]{1,0:T(8,128)(2,1)S(1)}, bf16[64,2048]{1,0:T(8,128)(2,1)}, u32[]{:S(2)}) copy-start(bf16[64,2048]{1,0:T(8,128)(2,1)} %param.23) | copy-start | bytes 786436
  70.1 51.2 %copy-start.16 = (f32[2048]{0:T(1024)S(1)}, f32[2048]{0:T(1024)}, u32[]{:S(2)}) copy-start(f32[2048]{0:T(1024)} %param.24) | copy-start | bytes 24580
  70.1 1.5 collective-permute-start.6
  71.6 50.5 %copy-start.17 = (s32[64,10]{0,1:T(8,128)S(1)}, s32[64,10]{0,1:T(8,128)}, u32[]{:S(2)}) copy-start(s32[64,10]{0,1:T(8,128)} %param.26) | copy-start | bytes 7684
  71.6 68.0 %copy-start.18 = (s32[256]{0:T(256)S(1)}, s32[256]{0:T(256)}, u32[]{:S(2)}) copy-start(s32[256]{0:T(256)} %param.27) | copy-start | bytes 3076
  76.2 87.6 %all-gather.3.cloned.1.call-start = ((), (), s32[]{:S(2)}) async-start(), calls=%async_computation.5 | async-start | bytes 4456448 | tf_op jit(solution)/shard_map/all_gather | solution.py:384
  163.8 2.2 copy-start.1
  168.1 58.0 %copy-start.2 = (bf16[1,512,2048]{2,1,0:T(8,128)(2,1)S(1)}, bf16[1,512,2048]{2,1,0:T(8,128)(2,1)}, u32[]{:S(2)}) copy-start(bf16[1,512,2048]{2,1,0:T(8,128)(2,1)} %param.29) | copy-start | bytes 6291460
  237.2 65.6 %all-to-all-start.1 = ((bf16[16,64,2048]{2,1,0:T(8,128)(2,1)}), bf16[16,64,2048]{2,1,0:T(8,128)(2,1)}, u32[]{:S(2)}, u32[]{:S(2)}) async-start(bf16[16,64,2048]{2,1,0:T(8,128)(2,1)} %bitcast.41), calls=%async_computation.2 | async-start | bytes 8388608 | tf_op jit(solution)/shard_map/all_to_all | solution.py:418
  241.7 110.0 %reduce-scatter.5.cloned.1.call-start = ((), (), s32[]{:S(2)}) async-start(), calls=%async_computation.6 | async-start | bytes 2359296 | tf_op jit(solution)/shard_map/reduce_scatter | solution.py:422
  306.6 4.2 %collective-permute-start.8 = (bf16[512,2048]{1,0:T(8,128)(2,1)S(1)}, bf16[512,2048]{1,0:T(8,128)(2,1)S(1)}, u32[]{:S(2)}, u32[]{:S(2)}) collective-permute-start(bf16[512,2048]{1,0:T(8,128)(2,1)S(1)} %get-tuple-element.21), channel_id=1, source_target_pairs={{0,1},{1,0},{2,3},{3,2},{4,5},{5,4},{6,7},{7,6},{8,9},{9,8},{10,11... | collective-permute-start | bytes 6291464 | tf_op jit(solution)/shard_map/ppermute | solution.py:420
Sparse Core Ops, SparseCore 0:
  76.3 43.6 reduce-scatter.2
  122.5 41.3 all-gather.2
  313.2 38.5 reduce-scatter.4

commit v2 on v1

v2 whole, which is shorter than its diff:
```python
import math

import jax
import jax.numpy as jnp
from jax import lax
from jax.experimental import pallas as pl
from jax.experimental.pallas import tpu as pltpu
from jax.sharding import PartitionSpec as P

F32=jnp.float32; BF=jnp.bfloat16
EPS=1e-6
C=64
K=128
UNROLL = 8

def mm(a,b):
    return lax.dot_general(a,b,(((1,),(0,)),((),())),preferred_element_type=F32)

def split(a):
    hi=a.astype(BF)
    return hi,(a-hi.astype(F32)).astype(BF)

def mm3(a,b):
    ah,al=split(a); bh,bl=split(b)
    n=b.shape[1]
    if n==K:
        r=mm(jnp.concatenate([ah,al],1),jnp.concatenate([jnp.concatenate([bh,bl],1)]*2,0))
        return r[:,:n]+r[:,n:]
    return mm(jnp.concatenate([ah,al],1),jnp.concatenate([bh,bh],0))+mm(ah,bl)

def mm2(a,b):
    bh,bl=split(b)
    return mm(jnp.concatenate([a,a],1),jnp.concatenate([bh,bl],0))

def mm2l(a,b):
    ah,al=split(a)
    return mm(jnp.concatenate([ah,al],1),jnp.concatenate([b,b],0))

def mm1(a,b):
    return mm(a.astype(BF),b.astype(BF))

def delta_kernel(q_ref,k_ref,v_ref,row_ref,col_ref,go_g,go_o,z_out,wq_s,u_s,p_s,kw_s,dr_s,z_s,el_s):
    n=q_ref.shape[0]//C
    rows=lax.broadcasted_iota(jnp.int32,(2*C,2*C),0)
    cols=lax.broadcasted_iota(jnp.int32,(2*C,2*C),1)
    same=(rows//C)==(cols//C)
    strict=same&(rows>cols)
    within=same&(rows>=cols)
    lane=lax.broadcasted_iota(jnp.int32,(2*C,128),1)
    half=lax.broadcasted_iota(jnp.int32,(2*C,1),0)<C
    levels=[]
    b=1
    while b<C:
        levels.append(strict&((rows//(2*b))==(cols//(2*b)))&((rows//b)!=(cols//b)))
        b*=2
    def unit(m):
        return m*lax.rsqrt(jnp.sum(m*m,axis=-1,keepdims=True)+EPS)
    def prep(step,carry):
        amat=[];xs=[];rhs=[];kts=[];ids=[]
        allc=col_ref[...]
        for u in range(UNROLL):
            c=step*UNROLL+u
            ids.append(c)
            at=pl.ds(pl.multiple_of(c*C,C),C)
            kb=k_ref[at,:]
            qb=q_ref[at,:]
            k2=jnp.concatenate([kb,kb],0)
            q2=jnp.concatenate([qb,qb],0)
            kt=k2.T
            raw=mm(jnp.concatenate([k2,q2],0),kt)
            kf=k2.astype(F32)
            qf=q2.astype(F32)
            sk=lax.rsqrt(jnp.sum(kf*kf,axis=-1,keepdims=True)+EPS)
            sq=lax.rsqrt(jnp.sum(qf*qf,axis=-1,keepdims=True)+EPS)*(1.0/math.sqrt(K))
            sk_row=lax.rsqrt(jnp.sum(jnp.where(rows==cols,raw[:2*C],0.0),axis=0,keepdims=True)+EPS)
            g_row=row_ref[pl.ds(c,1),:]
            last_row=row_ref[pl.ds(n+c,1),:]
            b_row=row_ref[pl.ds(2*n+c,1),:]
            g_col=jnp.sum(jnp.where(lane==c,allc,0.0),axis=1,keepdims=True)
            b_col=jnp.sum(jnp.where(lane==n+c,allc,0.0),axis=1,keepdims=True)
            l_col=jnp.sum(jnp.where(lane==2*n+c,allc,0.0),axis=1,keepdims=True)
            fall=jnp.exp(jnp.where(within,g_col-g_row,0.0))*sk_row
            a=jnp.where(strict,fall*(b_col*sk)*raw[:2*C],0.0)
            p_s[c]=jnp.where(within,fall*sq*raw[2*C:],0.0).astype(BF)
            eg=jnp.exp(g_col)
            vb=v_ref[at,:]
            v2=jnp.concatenate([vb[:,:K],vb[:,K:]],0)
            rhs.append((b_row*jnp.exp(g_row)*sk_row,b_row,k2,v2))
            wq_s[c,1]=((eg*sq)*qf).astype(BF)
            kts.append((kt,sk*jnp.exp(l_col-g_col)))
            el_s[c]=jnp.exp(last_row)
            amat.append(a)
            xs.append(jnp.where(rows==cols,1.0,0.0)-jnp.where(levels[0],a,0.0))
        for lev in levels[1:]:
            mids=[mm3(jnp.where(lev,a,0.0),x) for a,x in zip(amat,xs)]
            xs=[x-mm3(x,m) for x,m in zip(xs,mids)]
        for c,x,(wr,br,k2,v2),(kt,kc) in zip(ids,xs,rhs,kts):
            w=mm2l(x*wr,k2)
            u=mm2l(x*br,v2)
            wq_s[c,0]=w.astype(BF)
            u_s[c]=u
            wu=jnp.concatenate([w,u],1)*kc
            both=jnp.concatenate([jnp.where(half,wu,0.0),jnp.where(half,0.0,wu)],1)
            td=mm2(kt,both)
            for h in range(2):
                kw_s[h,c]=td[:,h*2*K:h*2*K+K]
                dr_s[h,c]=td[:,h*2*K+K:(h+1)*2*K]
        return carry
    lax.fori_loop(0,n//UNROLL,prep,0)
    eye=jnp.where(lax.broadcasted_iota(jnp.int32,(K,K),0)==lax.broadcasted_iota(jnp.int32,(K,K),1),1.0,0.0)
    start=jnp.concatenate([eye,jnp.zeros((K,K),F32)],1)
    def chain(c,zs):
        new=[]
        el=el_s[c]
        for h in range(2):
            z=zs[h]
            z_s[c,h]=z.astype(BF)
            e=jnp.sum(jnp.where(lax.broadcasted_iota(jnp.int32,(1,2*C),1)==h*C,el,0.0),axis=1,keepdims=True)
            t=e*z-mm3(kw_s[h,c],z)
            new.append(jnp.concatenate([t[:,:K],t[:,K:]+dr_s[h,c]],1))
        return tuple(new)
    zs=lax.fori_loop(0,n,chain,(start,start),unroll=4)
    for h in range(2):
        z_out[h]=zs[h].astype(BF)
    def emit(step,carry):
        for u in range(UNROLL):
            c=step*UNROLL+u
            fresh=[];outs=[]
            for h in range(2):
                z=z_s[c,h]
                w=wq_s[c,0,h*C:(h+1)*C,:]
                q=wq_s[c,1,h*C:(h+1)*C,:]
                r=mm(jnp.concatenate([w,q],0),z)
                f=-r[:C]
                uu=u_s[c,h*C:(h+1)*C,:]
                fresh.append(jnp.concatenate([f[:,:K],f[:,K:]+uu],1))
                outs.append(r[C:])
            out=jnp.concatenate(outs,0)+mm(p_s[c],jnp.concatenate(fresh,0).astype(BF))
            at=pl.ds(pl.multiple_of(c*C,C),C)
            for h in range(2):
                go_g[h,at,:]=out[h*C:(h+1)*C,:K].astype(BF)
                go_o[h,at,:]=out[h*C:(h+1)*C,K:]
        return carry
    lax.fori_loop(0,n//UNROLL,emit,0)

def whole(shape):
    return pl.BlockSpec(tuple(shape),lambda *_: (0,)*len(shape))

def delta_local(q,k,v,ld,beta):
    t=q.shape[0]; n=t//C
    g=jnp.cumsum(ld.reshape(2,n,C),axis=-1)
    last=jnp.broadcast_to(g[:,:,-1:],g.shape)
    pack=lambda a: jnp.transpose(a,(1,0,2)).reshape(n,2*C)
    rate=pack(beta.reshape(2,n,C))
    row=jnp.concatenate([pack(g),pack(last),rate],0)
    col=jnp.concatenate([pack(g).T,rate.T,pack(last).T,jnp.zeros((2*C,128-3*n),F32)],1)
    shapes=[((2,t,K),BF),((2,t,K),F32),((2,K,2*K),BF)]
    return pl.pallas_call(
        delta_kernel,
        grid=(1,),
        out_shape=[jax.ShapeDtypeStruct(a,d) for a,d in shapes],
        in_specs=[whole(a.shape) for a in (q,k,v,row,col)],out_specs=[whole(a) for a,d in shapes],
        scratch_shapes=[pltpu.VMEM((n,2,2*C,K),BF),pltpu.VMEM((n,2*C,K),F32),pltpu.VMEM((n,2*C,2*C),BF),
            pltpu.VMEM((2,n,K,K),F32),pltpu.VMEM((2,n,K,K),F32),pltpu.VMEM((n,2,K,2*K),BF),pltpu.VMEM((n,1,2*C),F32)],
        compiler_params=pltpu.CompilerParams(vmem_limit_bytes=56*2**20),
    )(q,k,v,row,col)

CAP = 4
GROUP = 4
TOK = 64
SIDE = 4
D = 2048


def params(mib):
    return pltpu.CompilerParams(vmem_limit_bytes=mib * 2**20)


def fold_kernel(x_ref, own, a1, a2, a3, total_ref, prefix_ref):
    x = x_ref[0]
    eye = jnp.where(
        lax.broadcasted_iota(jnp.int32, (K, K), 0) == lax.broadcasted_iota(jnp.int32, (K, K), 1),
        1.0,
        0.0,
    )
    for h in range(2):
        near = [own[h].astype(F32), a1[h].astype(F32), a2[h].astype(F32), a3[h].astype(F32)]
        z = jnp.concatenate([eye, jnp.zeros((K, K), F32)], 1)
        prefix = z
        for j in range(SIDE):
            item = near[0]
            for d in range(1, SIDE):
                item = jnp.where((x - j) % SIDE == d, near[d], item)
            if j == 0:
                z = item
            else:
                zh, zl = split(z)
                m = item[:, :K].astype(BF)
                t = mm(m, zh) + mm(m, zl)
                z = jnp.concatenate([t[:, :K], t[:, K:] + item[:, K:]], 1)
            if j < SIDE - 1:
                prefix = jnp.where(x == j + 1, z, prefix)
        total_ref[h] = z.astype(BF)
        prefix_ref[h] = prefix


def core_kernel(
    par_ref, g_ref, o_ref, prefix, b1, b2, b3, gate_ref, gain_ref, core_ref, mine, sib, state
):
    gain = gain_ref[...]
    even = par_ref[0] == 0

    @pl.when(pl.program_id(0) == 0)
    def _():
        for h in range(2):
            e = b3[h][:, K:].astype(F32)
            for b in (b2, b1):
                eh, el = split(e)
                m = b[h][:, :K]
                e = mm(m, eh) + mm(m, el) + b[h][:, K:].astype(F32)
            e = mm3(prefix[h][:, :K], e) + prefix[h][:, K:]
            eh, el = split(e)
            state[h] = jnp.concatenate([eh, el], 1)

    step = 2 * TOK
    for i in range(g_ref.shape[1] // step):
        at = slice(i * step, (i + 1) * step)
        outs = []
        for h in range(2):
            both = mm(g_ref[h, at, :], state[h])
            core = o_ref[h, at, :] + both[:, :K] + both[:, K:]
            gate = gate_ref[at, h * K : (h + 1) * K].astype(F32)
            scaled = core * lax.rsqrt(jnp.mean(core * core, axis=-1, keepdims=True) + EPS)
            outs.append((scaled * gain * (gate / (1.0 + jnp.exp(-gate)))).astype(BF))
        out = jnp.concatenate(outs, 1)
        core_ref[at, :] = out
        to = slice(i * TOK, (i + 1) * TOK)
        mine[to, :] = jnp.where(even, out[:TOK], out[TOK:])
        sib[to, :] = jnp.where(even, out[TOK:], out[:TOK])


def core_local(parity, g, o, prefix, far, gate, gain):
    rows, wide = gate.shape
    part = 512
    half = jax.ShapeDtypeStruct((rows // 2, wide), BF)
    heads = pl.BlockSpec((2, part, K), lambda i: (0, i, 0))
    half_spec = pl.BlockSpec((part // 2, wide), lambda i: (i, 0))
    full_spec = pl.BlockSpec((part, wide), lambda i: (i, 0))
    return pl.pallas_call(
        core_kernel,
        grid=(rows // part,),
        out_shape=(jax.ShapeDtypeStruct(gate.shape, BF), half, half),
        in_specs=[pl.BlockSpec(memory_space=pltpu.SMEM), heads, heads]
        + [whole(prefix.shape)] * 4
        + [full_spec, whole(gain.shape)],
        out_specs=(full_spec, half_spec, half_spec),
        scratch_shapes=[pltpu.VMEM((2, K, 2 * K), BF)],
        compiler_params=params(56),
    )(parity, g, o, prefix, *far, gate, gain)


def project_kernel(a_ref, b_ref, wa_ref, wb_ref, out_ref):
    out_ref[...] = (mm(a_ref[...], wa_ref[...]) + mm(b_ref[...], wb_ref[...])).astype(BF)


def project(a, b, wa, wb):
    rows, depth = a.shape
    wide = 512
    return pl.pallas_call(
        project_kernel,
        grid=(D // wide,),
        out_shape=jax.ShapeDtypeStruct((rows, D), BF),
        in_specs=[
            pl.BlockSpec((rows, depth), lambda i: (0, 0)),
            pl.BlockSpec((rows, depth), lambda i: (0, 0)),
            pl.BlockSpec((depth, wide), lambda i: (0, i)),
            pl.BlockSpec((depth, wide), lambda i: (0, i)),
        ],
        out_specs=pl.BlockSpec((rows, wide), lambda i: (0, i)),
        compiler_params=params(16),
    )(a, b, wa, wb)


def pick(sel, rows):
    out = lax.dot_general(sel, rows, (((0,), (0,)), ((), ())), preferred_element_type=F32)
    return out.astype(BF).reshape(sel.shape[1] // (GROUP * CAP), GROUP * CAP, D)


def near_kernel(sel_ref, mine_ref, sib_ref, out_ref):
    out_ref[:, : GROUP * CAP, :] = pick(sel_ref[: GROUP * TOK], mine_ref[...])
    out_ref[:, GROUP * CAP :, :] = pick(sel_ref[GROUP * TOK :], sib_ref[...])


def dispatch_near(sel, mine, sib):
    return pl.pallas_call(
        near_kernel,
        grid=(1,),
        out_shape=jax.ShapeDtypeStruct((16, 2 * GROUP * CAP, D), BF),
        in_specs=[whole(sel.shape), whole(mine.shape), whole(sib.shape)],
        out_specs=whole((16, 2 * GROUP * CAP, D)),
        compiler_params=params(16),
    )(sel, mine, sib)


def far_kernel(order_ref, sel_ref, r0, r1, r2, r3, out_ref):
    rows = jnp.concatenate([r0[...], r1[...], r2[...], r3[...]], 0)
    out_ref[...] = pick(sel_ref[...], rows)


def dispatch_far(order, sel, rows):
    part = GROUP * TOK

    def block(j):
        return pl.BlockSpec((TOK, D), lambda g, order: (order[GROUP * g + j], 0))

    return pl.pallas_call(
        far_kernel,
        grid_spec=pltpu.PrefetchScalarGridSpec(
            num_scalar_prefetch=1,
            grid=(2,),
            in_specs=[pl.BlockSpec((part, sel.shape[1]), lambda g, order: (g, 0))]
            + [block(j) for j in range(GROUP)],
            out_specs=pl.BlockSpec((16, GROUP * CAP, D), lambda g, order: (0, g, 0)),
        ),
        out_shape=jax.ShapeDtypeStruct((16, 2 * GROUP * CAP, D), BF),
        compiler_params=params(16),
    )(order, sel, rows, rows, rows, rows)


def expert_kernel(x_ref, gate_ref, up_ref, down_ref, out_ref, total):
    x = x_ref[...]
    gate = mm(x, gate_ref[...])
    act = (gate / (1.0 + jnp.exp(-gate)) * mm(x, up_ref[...])).astype(BF)
    term = mm(act, down_ref[...])
    step = pl.program_id(0)

    @pl.when(step == 0)
    def _():
        total[...] = term

    @pl.when(step > 0)
    def _():
        out_ref[...] = (total[...] + term).astype(BF)


def expert(x, gate_up, down):
    part = down.shape[0] // 2
    return pl.pallas_call(
        expert_kernel,
        grid=(2,),
        out_shape=jax.ShapeDtypeStruct(x.shape, BF),
        in_specs=[
            whole(x.shape),
            pl.BlockSpec((D, part), lambda i: (0, i)),
            pl.BlockSpec((D, part), lambda i: (0, 2 + i)),
            pl.BlockSpec((part, D), lambda i: (i, 0)),
        ],
        out_specs=whole(x.shape),
        scratch_shapes=[pltpu.VMEM(x.shape, F32)],
        cost_estimate=pl.CostEstimate(
            flops=6 * x.shape[0] * D * down.shape[0], bytes_accessed=10 * 2**20, transcendentals=0
        ),
        compiler_params=params(32),
    )(x, gate_up, gate_up, down)


def combine_kernel(w_ref, y_ref, out_ref):
    rows = y_ref[...].reshape(w_ref.shape[1], D)
    out_ref[...] = mm(w_ref[...], rows).astype(BF)


def combine(weights, y, at, half):
    part = GROUP * TOK
    return pl.pallas_call(
        combine_kernel,
        grid=(1,),
        out_shape=jax.ShapeDtypeStruct((part, D), BF),
        in_specs=[
            pl.BlockSpec((part, weights.shape[1]), lambda i: (at, 0)),
            pl.BlockSpec((y.shape[0], GROUP * CAP, D), lambda i: (0, half, 0)),
        ],
        out_specs=pl.BlockSpec((part, D), lambda i: (0, 0)),
        compiler_params=params(16),
    )(weights, y)


def place_kernel(at_ref, own_ref, got_ref, out_ref):
    i = pl.program_id(0)
    total = own_ref[...].astype(F32) + got_ref[...].astype(F32)
    out_ref[...] = jnp.where(at_ref[i] < GROUP, total, 0.0).astype(BF)


def place(at, own, got):
    part = pl.BlockSpec((TOK, D), lambda i, at: (jnp.minimum(at[i], GROUP - 1), 0))
    chips = at.shape[0]
    return pl.pallas_call(
        place_kernel,
        grid_spec=pltpu.PrefetchScalarGridSpec(
            num_scalar_prefetch=1,
            grid=(chips,),
            in_specs=[part, part],
            out_specs=pl.BlockSpec((TOK, D), lambda i, at: (i, 0)),
        ),
        out_shape=jax.ShapeDtypeStruct((chips * TOK, D), BF),
        compiler_params=params(8),
    )(at, own, got)


NEAR = ((0, 1, -1, 2), (0, 1, -1, -2))
FAR = ((-2, 3, -3, 4), (2, 3, -3, 4))


def along_z(i, way, n):
    return [(j, (j + 2 * way * NEAR[j % 2][i]) % n) for j in range(n)]


def along_x(d):
    return [(i, (i // SIDE) * SIDE + (i % SIDE + d) % SIDE) for i in range(SIDE * SIDE)]


def along_y(d):
    return [(i, i + SIDE * d) for i in range(SIDE * (SIDE - d))]


def local(
    query_raw,
    key_raw,
    values,
    out_gate,
    log_decay,
    beta_rate,
    head_gain,
    out_weight,
    residual,
    post_gain,
    router_weight,
    routes,
    placement,
    expert_in,
    expert_out,
):
    n_exp = lax.axis_size("exp")
    experts = router_weight.shape[1]
    at_exp = lax.axis_index("exp")
    at_x = (lax.axis_index("ctx") % SIDE).reshape(1)
    parity = (at_exp % 2).reshape(1)
    core_pairs = [(i, i ^ 1) for i in range(n_exp)]
    same_core = [list(range(0, n_exp, 2)), list(range(1, n_exp, 2))]

    weight_sib = lax.ppermute(out_weight, "exp", core_pairs)

    g, o, z = delta_local(query_raw, key_raw, values, log_decay, beta_rate)
    near = [lax.ppermute(z, "ctx", along_x(d)) for d in range(1, SIDE)]
    total, prefix = pl.pallas_call(
        fold_kernel,
        grid=(1,),
        out_shape=(jax.ShapeDtypeStruct(z.shape, BF), jax.ShapeDtypeStruct(z.shape, F32)),
        in_specs=[pl.BlockSpec(memory_space=pltpu.SMEM)] + [whole(z.shape)] * 4,
        out_specs=(whole(z.shape), whole(z.shape)),
        compiler_params=params(56),
    )(at_x, z, *near)
    far = [lax.ppermute(total, "ctx", along_y(d)) for d in range(1, SIDE)]
    core_out, mine, sib = core_local(parity, g, o, prefix, far, out_gate, head_gain.reshape(1, K))

    got = lax.ppermute(sib, "exp", core_pairs)
    terms = project(mine, got, out_weight, weight_sib)
    terms, routes = lax.optimization_barrier((terms, routes))
    attn = lax.psum_scatter(
        terms, "exp", scatter_dimension=0, tiled=True, axis_index_groups=same_core
    ).astype(F32)
    routes_all = lax.all_gather(routes, "exp", tiled=True)
    rows = routes_all.shape[0]
    chips = n_exp // 2
    at_z = at_exp // 2
    at_core = at_exp % 2
    shift = jnp.where(
        at_core == 0,
        jnp.asarray(NEAR[0] + NEAR[1] + FAR[0] + FAR[1], jnp.int32),
        jnp.asarray(NEAR[1] + NEAR[0] + FAR[1] + FAR[0], jnp.int32),
    )
    flip = jnp.asarray(([0] * GROUP + [1] * GROUP) * 2, jnp.int32)
    order = 2 * ((at_z + shift) % chips) + (at_core + flip) % 2
    routes_rel = routes_all.reshape(n_exp, TOK, -1)[order].reshape(rows, -1)
    ids = jnp.arange(experts, dtype=jnp.int32)
    chosen = jnp.any(routes_rel[:, :, None] == ids[None, None, :], axis=1)
    wide = n_exp * GROUP * CAP
    lanes = jnp.arange(wide, dtype=jnp.int32)
    holder = (lanes // (GROUP * CAP)) * n_exp + at_exp
    spread = (placement[:, None] == holder[None, :]).astype(BF)
    named = jnp.dot(chosen.astype(BF), spread, preferred_element_type=F32)
    step = jnp.arange(TOK, dtype=jnp.int32)
    before = (step[:, None] > step[None, :]).astype(BF)
    rank = jnp.einsum(
        "ts,bsl->btl",
        before,
        named.astype(BF).reshape(rows // TOK, TOK, wide),
        preferred_element_type=F32,
    ).reshape(rows, wide)
    block = (jnp.arange(rows, dtype=jnp.int32) // TOK) % GROUP
    sel = (
        (named > 0.5)
        & (rank == (lanes % CAP).astype(F32)[None, :])
        & (block[:, None] == ((lanes // CAP) % GROUP)[None, :])
    )
    picks = sel.astype(BF)
    half_rows = rows // 2
    attn, picks, chosen = lax.optimization_barrier((attn, picks, chosen))
    mid = lax.optimization_barrier((residual.astype(F32) + attn).astype(BF)).astype(F32)
    normed = (mid / jnp.sqrt(jnp.mean(mid * mid, axis=-1, keepdims=True) + EPS) * post_gain).astype(
        BF
    )
    around = [lax.ppermute(normed, "exp", along_z(i, -1, n_exp)) for i in range(1, GROUP)]
    near_mine = jnp.concatenate([normed] + around, 0)
    near_mine, normed = lax.optimization_barrier((near_mine, normed))
    near_sib = lax.ppermute(near_mine, "exp", core_pairs)
    normed_all = lax.all_gather(normed, "exp", tiled=True)

    def spread_out(rows):
        return lax.all_to_all(rows, "ctx", split_axis=0, concat_axis=0, tiled=True)

    def experts_on(rows):
        return expert(rows.reshape(-1, D), expert_in[0], expert_out[0]).reshape(rows.shape)

    near_rows = dispatch_near(picks[:half_rows], near_mine, near_sib)
    near_in = spread_out(near_rows)
    near_in, normed_far = lax.optimization_barrier((near_in, normed_all))
    far_rows = dispatch_far(order[half_rows // TOK :], picks[half_rows:], normed_far)
    far_in = spread_out(far_rows)
    near_out = experts_on(near_in)
    far_out = experts_on(far_in)

    logits = jnp.dot(normed_far, router_weight, preferred_element_type=F32)
    logits = logits.reshape(n_exp, TOK, experts)[order].reshape(rows, experts)
    raised = jnp.where(chosen, jnp.exp(logits), 0.0)
    gates = raised / jnp.sum(raised, axis=-1, keepdims=True)
    mine_gates = jnp.dot(gates, spread.astype(F32), precision=lax.Precision.HIGHEST)
    weights = jnp.where(sel, mine_gates, 0.0).astype(BF)

    far_back = spread_out(far_out)
    near_out, far_back = lax.optimization_barrier((near_out, far_back))
    near_back = spread_out(near_out)

    far_got = lax.ppermute(combine(weights, far_back, 3, 1), "exp", core_pairs)
    far_own = combine(weights, far_back, 2, 0)
    tables = [[GROUP] * chips, [GROUP] * chips]
    for core in range(2):
        for i, d in enumerate(FAR[core]):
            tables[core][d % chips] = i
    table = jnp.where(at_core == 0, *[jnp.asarray(a, jnp.int32) for a in tables])
    at = table[(jnp.arange(chips, dtype=jnp.int32) - at_z) % chips]
    far_sum = lax.psum_scatter(
        place(at, far_own, far_got),
        "exp",
        scatter_dimension=0,
        tiled=True,
        axis_index_groups=same_core,
    )

    near_got = lax.ppermute(combine(weights, near_back, 1, 1), "exp", core_pairs)
    near_own = combine(weights, near_back, 0, 0)
    near_sum = (near_own.astype(F32) + near_got.astype(F32)).reshape(GROUP, TOK, D)
    mixture = near_sum[0] + far_sum.astype(F32)
    for i in (3, 1, 2):
        sent = lax.ppermute(near_sum[i].astype(BF), "exp", along_z(i, 1, n_exp))
        mixture += sent.astype(F32)
    return (core_out, (mid + mixture).astype(BF))


def solution(mesh):
    placed = (
        P("ctx", "exp"),
        P("ctx", "exp"),
        P("ctx", "exp"),
        P("ctx", "exp"),
        P("exp", "ctx"),
        P("exp", "ctx"),
        P(),
        P("exp", None),
        P(("ctx", "exp"), None),
        P(),
        P(),
        P(("ctx", "exp"), None),
        P(),
        P(("ctx", "exp"), None, None),
        P(("ctx", "exp"), None, None),
    )
    return jax.shard_map(
        local,
        mesh=mesh,
        in_specs=placed,
        out_specs=(P("ctx", "exp"), P(("ctx", "exp"), None)),
        check_vma=False,
    )
```

time: 362 us -> 320 us (0.88)
  waiting for transfers between devices: 175 us -> 125 us
  blocking collectives: 73.4 us -> 50.6 us
  starting transfers between devices: 21.4 us -> 40.3 us
  local copies, waits for them, and re-layouts: 14.4 us -> 25.2 us
    reduce_scatter x1, waiting for transfers between devices: 38.7 us -> 0.01 us  [local(): lax.psum_scatter(place(at, far_own, far_got), 'exp', scatter_dimension=0,...]
    all_to_all x1, blocking collectives: 58 us -> 32.2 us  [spread_out(): return lax.all_to_all(rows, 'ctx', split_axis=0, concat_axis=0, tiled=True)]
    reduce_scatter x1, waiting for transfers between devices: 43.8 us -> 20.3 us  [local(): lax.psum_scatter(terms, 'exp', scatter_dimension=0, tiled=True, axis_inde...]
    all_gather x1, waiting for transfers between devices: 23.1 us -> 0.01 us  [local(): normed_all = lax.all_gather(normed, 'exp', tiled=True)]
    ppermute x1 -> x9, waiting for transfers between devices: 4.15 us -> 23.4 us  [the longest x3 11 us: local(): sent = lax.ppermute(near_sum[i].astype(BF), 'exp', along_z(i, 1, n_exp))]
    all_to_all x1 -> x3, waiting for transfers between devices: 56.7 us -> 71 us  [spread_out(): return lax.all_to_all(rows, 'ctx', split_axis=0, concat_axis=0, tiled=True)]
    all_to_all x1 -> x3, starting transfers between devices: 4.54 us -> 14.9 us  [spread_out(): return lax.all_to_all(rows, 'ctx', split_axis=0, concat_axis=0, tiled=True)]
    ppermute x1 -> x9, starting transfers between devices: 0.09 us -> 9.91 us  [the longest x3 5.49 us: local(): sent = lax.ppermute(near_sum[i].astype(BF), 'exp', along_z(i, 1, n_exp))]
  transfers between devices with their start and end apart: 13 -> 23, of which waited for: 10 -> 16; matrix products, arithmetic and copies ran while one was open for 3% -> 6% of each run, Pallas kernels for 7% -> 12%
where the time goes in v2:
time: 320 us; the launch traced here: 319 us
  waiting for transfers between devices  125 us (39%)
  blocking collectives  50.6 us (16%)
  Pallas kernels  48.3 us (15%)
  starting transfers between devices  40.3 us (13%)
  local copies, waits for them, and re-layouts  25.2 us (8%)
  between operations  14.3 us (4%)
  other arithmetic  9.02 us (3%)
  matrix products  6.65 us (2%)
    all_to_all x3, waiting for transfers between devices, spread_out(): return lax.all_to_all(rows, 'ctx', split_axis=0, concat_axis=0, tiled=True)  71 us
    all_to_all x1, blocking collectives, spread_out(): return lax.all_to_all(rows, 'ctx', split_axis=0, concat_axis=0, tiled=True)  32.2 us
    reduce_scatter x1, waiting for transfers between devices, local(): lax.psum_scatter(terms, 'exp', scatter_dimension=0, tiled=True, axis_inde...  20.3 us
    all_gather x1, blocking collectives, local(): routes_all = lax.all_gather(routes, 'exp', tiled=True)  18.4 us
    pallas_call x1, Pallas kernels, delta_local(): pl.pallas_call(delta_kernel, grid=(1,), out_shape=[jax.ShapeDtypeStruct(a...  17.5 us
    unnamed x80, local copies, waits for them, and re-layouts  17 us
    all_to_all x3, starting transfers between devices, spread_out(): return lax.all_to_all(rows, 'ctx', split_axis=0, concat_axis=0, tiled=True)  14.9 us
    ppermute x3, waiting for transfers between devices, local(): sent = lax.ppermute(near_sum[i].astype(BF), 'exp', along_z(i, 1, n_exp))  11 us
  transfers between devices with their start and end apart: 23, of which 16 were waited for; matrix products, arithmetic and copies ran while one was open for 6% of the time, Pallas kernels for 12%

profile of v2, /device:TPU:32, one launch (start us, length us, event | category | flops | bytes accessed | tf_op | source)
XLA Modules:
  0.0 319.1 jit_solution(8021344277456167932)
XLA Ops:
  11.4 17.5 %shard_map.203 = (bf16[2,1024,128]{2,1,0:T(8,128)(2,1)}, f32[2,1024,128]{2,1,0:T(8,128)}, bf16[2,128,256]{2,1,0:T(8,128)(2,1)}) custom-call(bf16[1024,128]{1,0:T(8,128)(2,1)} %q_ref.1, bf16[1024,128]{1,0:T(8,128)(2,1)} %k_ref.1, bf16[1024,256]{1,0:T(8,128)(2,1)} %v_ref.1, f32[48,128]{1,0:T(8,128)} %pad_maximum_fusion.1.row_ref, ...), custom_call_target="tpu_custom_call" | custom-call | tf_op jit(solution)/shard_map/pallas_call | solution.py:158
  28.9 1.5 collective-permute-start
  30.4 2.7 collective-permute-start.1
  33.1 1.4 collective-permute-start.2
  34.5 1.6 collective-permute-done.a1
  36.2 3.8 %collective-permute-done.1.a2 = bf16[2,128,256]{2,1,0:T(8,128)(2,1)S(1)} collective-permute-done((bf16[2,128,256]{2,1,0:T(8,128)(2,1)}, bf16[2,128,256]{2,1,0:T(8,128)(2,1)S(1)}, u32[]{:S(2)}, u32[]{:S(2)}) %collective-permute-start.1) | collective-permute-done | bytes 131104 | tf_op jit(solution)/shard_map/ppermute | solution.py:453
  40.6 2.6 shard_map.204
  43.3 3.5 %collective-permute-start.3 = (bf16[2,128,256]{2,1,0:T(8,128)(2,1)}, bf16[2,128,256]{2,1,0:T(8,128)(2,1)S(1)}, u32[]{:S(2)}, u32[]{:S(2)}) collective-permute-start(bf16[2,128,256]{2,1,0:T(8,128)(2,1)} %get-tuple-element.25), channel_id=1, source_target_pairs={{0,64},{16,80},{32,96},{48,112},{64,128},{80,144},{96,160},{112,17... | collective-permute-start | bytes 393224 | tf_op jit(solution)/shard_map/ppermute | solution.py:462
  46.7 4.8 %collective-permute-start.4 = (bf16[2,128,256]{2,1,0:T(8,128)(2,1)}, bf16[2,128,256]{2,1,0:T(8,128)(2,1)S(1)}, u32[]{:S(2)}, u32[]{:S(2)}) collective-permute-start(bf16[2,128,256]{2,1,0:T(8,128)(2,1)} %get-tuple-element.25), channel_id=1, source_target_pairs={{0,128},{16,144},{32,160},{48,176},{64,192},{80,208},{96,224},{112... | collective-permute-start | bytes 393224 | tf_op jit(solution)/shard_map/ppermute | solution.py:462
  52.9 1.5 collective-permute-done.4.b2
  54.4 1.3 collective-permute-done.5.b3
  56.3 3.9 %shard_map.205 = (bf16[1024,256]{1,0:T(8,128)(2,1)}, bf16[512,256]{1,0:T(8,128)(2,1)}, bf16[512,256]{1,0:T(8,128)(2,1)}) custom-call(s32[1]{0:T(128)} %bitcast.par_ref, bf16[2,1024,128]{2,1,0:T(8,128)(2,1)} %get-tuple-element.21.g_ref, f32[2,1024,128]{2,1,0:T(8,128)} %get-tuple-element.22.o_ref, f32[2,128,256]{2,1,0:T(8,128)} %get-tuple-element.24.prefix, ...), custom_call_target="tpu_custom_call" | custom-call | tf_op jit(solution)/shard_map/pallas_call | solution.py:249
  60.2 1.7 collective-permute-done.6.b_ref
  62.9 3.1 shard_map.206
  66.8 18.4 %all-gather = s32[16,64,10]{1,2,0:T(8,128)S(1)} all-gather(s32[1,64,10]{1,2,0:T(8,128)S(1)} %bitcast.69), channel_id=1, replica_groups=mesh['ctx'=16,'exp'=16] {'exp'}, dimensions={0}, use_global_device_ids=true | all-gather | bytes 43520 | tf_op jit(solution)/shard_map/all_gather | solution.py:471
  85.8 1.9 fusion
  89.9 20.3 %reduce-scatter.3.cloned.1.call-done = bf16[64,2048]{1,0:T(8,128)(2,1)} async-done(((bf16[512,2048]{1,0:T(8,128)(2,1)}), bf16[64,2048]{1,0:T(8,128)(2,1)}) %reduce-scatter.3.cloned.1.call-update) | async-done | bytes 262160 | tf_op jit(solution)/shard_map/reduce_scatter | solution.py:468
  112.1 2.2 collective-permute-start.10
  116.4 5.8 %collective-permute-done.10 = bf16[64,2048]{1,0:T(8,128)(2,1)S(1)} collective-permute-done((bf16[64,2048]{1,0:T(8,128)(2,1)S(1)}, bf16[64,2048]{1,0:T(8,128)(2,1)S(1)}, u32[]{:S(2)}, u32[]{:S(2)}) %collective-permute-start.10) | collective-permute-done | bytes 262176 | tf_op jit(solution)/shard_map/ppermute | solution.py:512
  122.5 2.7 collective-permute-done.8
  125.4 2.6 collective-permute-done.11.sib_ref
  128.8 1.4 copy-done.14
  130.1 6.5 %all-to-all-start = ((bf16[16,32,2048]{2,1,0:T(8,128)(2,1)}), bf16[16,32,2048]{2,1,0:T(8,128)(2,1)S(1)}, u32[]{:S(2)}, u32[]{:S(2)}) async-start(bf16[16,32,2048]{2,1,0:T(8,128)(2,1)} %copy-done.14), calls=%async_computation.1 | async-start | bytes 4194304 | tf_op jit(solution)/shard_map/all_to_all | solution.py:519
  136.7 32.8 %all-to-all-done = bf16[16,32,2048]{2,1,0:T(8,128)(2,1)S(1)} async-done(((bf16[16,32,2048]{2,1,0:T(8,128)(2,1)}), bf16[16,32,2048]{2,1,0:T(8,128)(2,1)S(1)}, u32[]{:S(2)}, u32[]{:S(2)}) %all-to-all-start) | async-done | bytes 2097184 | tf_op jit(solution)/shard_map/all_to_all | solution.py:519
  169.5 2.9 copy-done.3
  172.5 1.6 shard_map.209
  174.1 32.2 %all_to_all.20 = bf16[16,32,2048]{2,1,0:T(8,128)(2,1)S(1)} all-to-all(bf16[16,32,2048]{2,1,0:T(8,128)(2,1)S(1)} %shard_map.209), channel_id=1, replica_groups=mesh['ctx'=16,'exp'=16] {'ctx'}, dimensions={0} | all-to-all | bytes 4194304 | tf_op jit(solution)/shard_map/all_to_all | solution.py:519
  206.4 4.8 %shard_map.210 = bf16[512,2048]{1,0:T(8,128)(2,1)S(1)} custom-call(bf16[512,2048]{1,0:T(8,128)(2,1)S(1)} %bitcast.59, bf16[2048,1024]{1,0:T(8,128)(2,1)S(1)} %bitcast.50, bf16[2048,1024]{1,0:T(8,128)(2,1)S(1)} %bitcast.51, bf16[512,2048]{1,0:T(8,128)(2,1)S(1)} %bitcast.54), custom_call_target="tpu_custom_call" | custom-call | flops 3221225472 | bytes 10485760 | tf_op jit(solution)/shard_map/pallas_call | solution.py:348
  211.2 1.4 copy-done.12
  212.6 3.9 %all-to-all-start.2 = ((bf16[16,32,2048]{2,1,0:T(8,128)(2,1)}), bf16[16,32,2048]{2,1,0:T(8,128)(2,1)S(1)}, u32[]{:S(2)}, u32[]{:S(2)}) async-start(bf16[16,32,2048]{2,1,0:T(8,128)(2,1)} %bitcast.58), calls=%async_computation.3 | async-start | bytes 4194304 | tf_op jit(solution)/shard_map/all_to_all | solution.py:519
  216.5 4.4 %fusion.48 = f32[1024,256]{1,0:T(8,128)} fusion(bf16[1024,2048]{1,0:T(8,128)(2,1)} %all-gather.3.cloned.1.call-done.r0.r1.r2.r3, bf16[2048,256]{1,0:T(8,128)(2,1)S(1)} %copy-done), kind=kOutput, calls=%fused_computation.96 | convolution fusion | flops 1073741824 | bytes 6291456 | tf_op jit(solution)/shard_map/dot_general | solution.py:532
  221.0 2.9 gather_fusion.1
  223.9 1.5 exp.6
  225.7 1.6 fusion.1.w_ref
  228.5 4.8 %shard_map.208 = bf16[512,2048]{1,0:T(8,128)(2,1)S(1)} custom-call(bf16[512,2048]{1,0:T(8,128)(2,1)S(1)} %bitcast.56, bf16[2048,1024]{1,0:T(8,128)(2,1)S(1)} %bitcast.52, bf16[2048,1024]{1,0:T(8,128)(2,1)S(1)} %bitcast.53, bf16[512,2048]{1,0:T(8,128)(2,1)S(1)} %bitcast.55), custom_call_target="tpu_custom_call" | custom-call | flops 3221225472 | bytes 10485760 | tf_op jit(solution)/shard_map/pallas_call | solution.py:348
  233.4 1.3 copy-done.11
  234.7 11.1 %all-to-all-done.2.y_ref = bf16[16,32,2048]{2,1,0:T(8,128)(2,1)S(1)} async-done(((bf16[16,32,2048]{2,1,0:T(8,128)(2,1)}), bf16[16,32,2048]{2,1,0:T(8,128)(2,1)S(1)}, u32[]{:S(2)}, u32[]{:S(2)}) %all-to-all-start.2) | async-done | bytes 2097184 | tf_op jit(solution)/shard_map/all_to_all | solution.py:519
  246.8 1.4 shard_map.214
  248.3 4.5 %all-to-all-start.3 = ((bf16[16,32,2048]{2,1,0:T(8,128)(2,1)}), bf16[16,32,2048]{2,1,0:T(8,128)(2,1)}, u32[]{:S(2)}, u32[]{:S(2)}) async-start(bf16[16,32,2048]{2,1,0:T(8,128)(2,1)} %bitcast.57), calls=%async_computation.4 | async-start | bytes 4194304 | tf_op jit(solution)/shard_map/all_to_all | solution.py:519
  255.0 4.0 %shard_map.215 = bf16[512,2048]{1,0:T(8,128)(2,1)S(1)} custom-call(s32[8]{0:T(128)S(1)} %gather_fusion.2, bf16[256,2048]{1,0:T(8,128)(2,1)S(1)} %shard_map.213.own_ref, bf16[256,2048]{1,0:T(8,128)(2,1)} %collective-permute-done.13.got_ref), custom_call_target="tpu_custom_call" | custom-call | tf_op jit(solution)/shard_map/pallas_call | solution.py:396
  259.0 1.4 copy-done.13
  260.4 27.1 %all-to-all-done.3.y_ref = bf16[16,32,2048]{2,1,0:T(8,128)(2,1)} async-done(((bf16[16,32,2048]{2,1,0:T(8,128)(2,1)}), bf16[16,32,2048]{2,1,0:T(8,128)(2,1)}, u32[]{:S(2)}, u32[]{:S(2)}) %all-to-all-start.3) | async-done | bytes 2097184 | tf_op jit(solution)/shard_map/all_to_all | solution.py:519
  287.5 1.7 shard_map.212
  289.3 1.7 shard_map.211
  294.6 3.4 %collective-permute-start.14 = (bf16[64,2048]{1,0:T(8,128)(2,1)S(1)}, bf16[64,2048]{1,0:T(8,128)(2,1)}, u32[]{:S(2)}, u32[]{:S(2)}) collective-permute-start(bf16[64,2048]{1,0:T(8,128)(2,1)S(1)} %get-tuple-element.48), channel_id=1, source_target_pairs={{0,4},{1,13},{2,6},{3,15},{4,8},{5,1},{6,10},{7,3},{8,12},{9,5},{1... | collective-permute-start | bytes 786440 | tf_op jit(solution)/shard_map/ppermute | solution.py:564
  298.0 5.1 %collective-permute-done.16 = bf16[64,2048]{1,0:T(8,128)(2,1)S(1)} collective-permute-done((bf16[64,2048]{1,0:T(8,128)(2,1)S(1)}, bf16[64,2048]{1,0:T(8,128)(2,1)S(1)}, u32[]{:S(2)}, u32[]{:S(2)}) %collective-permute-start.16) | collective-permute-done | bytes 262176 | tf_op jit(solution)/shard_map/ppermute | solution.py:564
  304.5 5.9 %collective-permute-done.14 = bf16[64,2048]{1,0:T(8,128)(2,1)} collective-permute-done((bf16[64,2048]{1,0:T(8,128)(2,1)S(1)}, bf16[64,2048]{1,0:T(8,128)(2,1)}, u32[]{:S(2)}, u32[]{:S(2)}) %collective-permute-start.14) | collective-permute-done | bytes 262176 | tf_op jit(solution)/shard_map/ppermute | solution.py:564
  310.4 2.1 fusion.9
  (142 shorter events, 26.4 us)
Async XLA Ops:
  7.2 209.4 %copy-start = (bf16[2048,256]{1,0:T(8,128)(2,1)S(1)}, bf16[2048,256]{1,0:T(8,128)(2,1)}, u32[]{:S(2)}) copy-start(bf16[2048,256]{1,0:T(8,128)(2,1)} %param.30) | copy-start | bytes 3145732
  7.2 103.0 %reduce-scatter.3.cloned.1.call-start = ((), (), s32[]{:S(2)}) async-start(), calls=%async_computation.6 | async-start | bytes 2359296 | tf_op jit(solution)/shard_map/reduce_scatter | solution.py:468
  7.2 54.7 %collective-permute-start.7 = (bf16[256,2048]{1,0:T(8,128)(2,1)}, bf16[256,2048]{1,0:T(8,128)(2,1)S(1)}, u32[]{:S(2)}, u32[]{:S(2)}) collective-permute-start(bf16[256,2048]{1,0:T(8,128)(2,1)} %wa_ref.1), channel_id=1, source_target_pairs={{0,1},{1,0},{2,3},{3,2},{4,5},{5,4},{6,7},{7,6},{8,9},{9,8},{10,11... | collective-permute-start | bytes 3145736 | tf_op jit(solution)/shard_map/ppermute | solution.py:450
  11.4 50.6 %copy-start.15 = (bf16[256,2048]{1,0:T(8,128)(2,1)S(1)}, bf16[256,2048]{1,0:T(8,128)(2,1)}, u32[]{:S(2)}) copy-start(bf16[256,2048]{1,0:T(8,128)(2,1)} %wa_ref.1) | copy-start | bytes 3145732
  28.9 7.3 %collective-permute-start = (bf16[2,128,256]{2,1,0:T(8,128)(2,1)}, bf16[2,128,256]{2,1,0:T(8,128)(2,1)S(1)}, u32[]{:S(2)}, u32[]{:S(2)}) collective-permute-start(bf16[2,128,256]{2,1,0:T(8,128)(2,1)} %get-tuple-element.23.own), channel_id=1, source_target_pairs={{0,16},{16,32},{32,48},{48,0},{64,80},{80,96},{96,112},{112,64},{1... | collective-permute-start | bytes 393224 | tf_op jit(solution)/shard_map/ppermute | solution.py:453
  30.4 9.6 %collective-permute-start.1 = (bf16[2,128,256]{2,1,0:T(8,128)(2,1)}, bf16[2,128,256]{2,1,0:T(8,128)(2,1)S(1)}, u32[]{:S(2)}, u32[]{:S(2)}) collective-permute-start(bf16[2,128,256]{2,1,0:T(8,128)(2,1)} %get-tuple-element.23.own), channel_id=1, source_target_pairs={{0,32},{16,48},{32,0},{48,16},{64,96},{80,112},{96,64},{112,80},{1... | collective-permute-start | bytes 393224 | tf_op jit(solution)/shard_map/ppermute | solution.py:453
  33.1 6.8 %collective-permute-start.2 = (bf16[2,128,256]{2,1,0:T(8,128)(2,1)}, bf16[2,128,256]{2,1,0:T(8,128)(2,1)S(1)}, u32[]{:S(2)}, u32[]{:S(2)}) collective-permute-start(bf16[2,128,256]{2,1,0:T(8,128)(2,1)} %get-tuple-element.23.own), channel_id=1, source_target_pairs={{0,48},{16,0},{32,16},{48,32},{64,112},{80,64},{96,80},{112,96},{1... | collective-permute-start | bytes 393224 | tf_op jit(solution)/shard_map/ppermute | solution.py:453
  36.2 3.8 %copy-start.26 = (bf16[2,128,256]{2,1,0:T(8,128)(2,1)}, bf16[2,128,256]{2,1,0:T(8,128)(2,1)S(1)}, u32[]{:S(2)}) copy-start(bf16[2,128,256]{2,1,0:T(8,128)(2,1)S(1)} %collective-permute-done.a1) | copy-start | bytes 393220
  43.3 9.6 %collective-permute-start.3 = (bf16[2,128,256]{2,1,0:T(8,128)(2,1)}, bf16[2,128,256]{2,1,0:T(8,128)(2,1)S(1)}, u32[]{:S(2)}, u32[]{:S(2)}) collective-permute-start(bf16[2,128,256]{2,1,0:T(8,128)(2,1)} %get-tuple-element.25), channel_id=1, source_target_pairs={{0,64},{16,80},{32,96},{48,112},{64,128},{80,144},{96,160},{112,17... | collective-permute-start | bytes 393224 | tf_op jit(solution)/shard_map/ppermute | solution.py:462
  46.7 7.6 %collective-permute-start.4 = (bf16[2,128,256]{2,1,0:T(8,128)(2,1)}, bf16[2,128,256]{2,1,0:T(8,128)(2,1)S(1)}, u32[]{:S(2)}, u32[]{:S(2)}) collective-permute-start(bf16[2,128,256]{2,1,0:T(8,128)(2,1)} %get-tuple-element.25), channel_id=1, source_target_pairs={{0,128},{16,144},{32,160},{48,176},{64,192},{80,208},{96,224},{112... | collective-permute-start | bytes 393224 | tf_op jit(solution)/shard_map/ppermute | solution.py:462
  51.6 4.1 %collective-permute-start.5 = (bf16[2,128,256]{2,1,0:T(8,128)(2,1)}, bf16[2,128,256]{2,1,0:T(8,128)(2,1)S(1)}, u32[]{:S(2)}, u32[]{:S(2)}) collective-permute-start(bf16[2,128,256]{2,1,0:T(8,128)(2,1)} %get-tuple-element.25), channel_id=1, source_target_pairs={{0,192},{16,208},{32,224},{48,240},{1,193},{17,209},{33,225},{49,2... | collective-permute-start | bytes 393224 | tf_op jit(solution)/shard_map/ppermute | solution.py:462
  52.9 2.8 copy-start.27
  60.2 1.7 collective-permute-start.6
  66.1 21.7 %copy-start.34 = (s32[256]{0:T(256)S(1)}, s32[256]{0:T(256)}, u32[]{:S(2)}) copy-start(s32[256]{0:T(256)} %param.32) | copy-start | bytes 3076
  66.1 103.4 %all-gather.3.cloned.1.call-start = ((), (), s32[]{:S(2)}) async-start(), calls=%async_computation.7 | async-start | bytes 4456448 | tf_op jit(solution)/shard_map/all_gather | solution.py:516
  88.8 22.4 %copy-start.23 = (bf16[64,2048]{1,0:T(8,128)(2,1)S(1)}, bf16[64,2048]{1,0:T(8,128)(2,1)}, u32[]{:S(2)}) copy-start(bf16[64,2048]{1,0:T(8,128)(2,1)} %param.28) | copy-start | bytes 786436
  88.8 23.2 %copy-start.32 = (f32[2048]{0:T(1024)S(1)}, f32[2048]{0:T(1024)}, u32[]{:S(2)}) copy-start(f32[2048]{0:T(1024)} %param.29) | copy-start | bytes 24580
  112.1 13.1 %copy-start.21 = (bf16[64,2048]{1,0:T(8,128)(2,1)}, bf16[64,2048]{1,0:T(8,128)(2,1)S(1)}, u32[]{:S(2)}) copy-start(bf16[64,2048]{1,0:T(8,128)(2,1)S(1)} %fusion.8) | copy-start | bytes 786436
  112.1 10.1 %collective-permute-start.10 = (bf16[64,2048]{1,0:T(8,128)(2,1)S(1)}, bf16[64,2048]{1,0:T(8,128)(2,1)S(1)}, u32[]{:S(2)}, u32[]{:S(2)}) collective-permute-start(bf16[64,2048]{1,0:T(8,128)(2,1)S(1)} %fusion.8), channel_id=1, source_target_pairs={{0,12},{1,5},{2,14},{3,7},{4,0},{5,9},{6,2},{7,11},{8,4},{9,13},{1... | collective-permute-start | bytes 786440 | tf_op jit(solution)/shard_map/ppermute | solution.py:512
  114.3 8.1 %collective-permute-start.9 = (bf16[64,2048]{1,0:T(8,128)(2,1)S(1)}, bf16[64,2048]{1,0:T(8,128)(2,1)S(1)}, u32[]{:S(2)}, u32[]{:S(2)}) collective-permute-start(bf16[64,2048]{1,0:T(8,128)(2,1)S(1)} %fusion.8), channel_id=1, source_target_pairs={{0,2},{1,3},{2,4},{3,5},{4,6},{5,7},{6,8},{7,9},{8,10},{9,11},{10,... | collective-permute-start | bytes 786440 | tf_op jit(solution)/shard_map/ppermute | solution.py:512
  115.1 10.0 %collective-permute-start.8 = (bf16[64,2048]{1,0:T(8,128)(2,1)S(1)}, bf16[64,2048]{1,0:T(8,128)(2,1)S(1)}, u32[]{:S(2)}, u32[]{:S(2)}) collective-permute-start(bf16[64,2048]{1,0:T(8,128)(2,1)S(1)} %fusion.8), channel_id=1, source_target_pairs={{0,14},{1,15},{2,0},{3,1},{4,2},{5,3},{6,4},{7,5},{8,6},{9,7},{10,... | collective-permute-start | bytes 786440 | tf_op jit(solution)/shard_map/ppermute | solution.py:512
  125.3 2.7 collective-permute-start.11
  128.8 1.4 copy-start.14
  130.1 39.4 %all-to-all-start = ((bf16[16,32,2048]{2,1,0:T(8,128)(2,1)}), bf16[16,32,2048]{2,1,0:T(8,128)(2,1)S(1)}, u32[]{:S(2)}, u32[]{:S(2)}) async-start(bf16[16,32,2048]{2,1,0:T(8,128)(2,1)} %copy-done.14), calls=%async_computation.1 | async-start | bytes 4194304 | tf_op jit(solution)/shard_map/all_to_all | solution.py:519
  169.5 4.6 %copy-start.9 = (bf16[16,32,2048]{2,1,0:T(8,128)(2,1)}, bf16[16,32,2048]{2,1,0:T(8,128)(2,1)S(1)}, u32[]{:S(2)}) copy-start(bf16[16,32,2048]{2,1,0:T(8,128)(2,1)S(1)} %all-to-all-done) | copy-start | bytes 6291460
  169.5 2.9 copy-start.3
  172.5 33.9 %copy-start.4 = (bf16[1,512,2048]{2,1,0:T(8,128)(2,1)S(1)}, bf16[1,512,2048]{2,1,0:T(8,128)(2,1)}, u32[]{:S(2)}) copy-start(bf16[1,512,2048]{2,1,0:T(8,128)(2,1)} %param.34) | copy-start | bytes 6291460
  174.1 32.2 %copy-start.1 = (bf16[1,2048,1024]{2,1,0:T(8,128)(2,1)S(1)}, bf16[1,2048,1024]{2,1,0:T(8,128)(2,1)}, u32[]{:S(2)}) copy-start(bf16[1,2048,1024]{2,1,0:T(8,128)(2,1)} %param.33) | copy-start | bytes 12582916
  211.2 1.4 copy-start.12
  212.6 33.2 %all-to-all-start.2 = ((bf16[16,32,2048]{2,1,0:T(8,128)(2,1)}), bf16[16,32,2048]{2,1,0:T(8,128)(2,1)S(1)}, u32[]{:S(2)}, u32[]{:S(2)}) async-start(bf16[16,32,2048]{2,1,0:T(8,128)(2,1)} %bitcast.58), calls=%async_computation.3 | async-start | bytes 4194304 | tf_op jit(solution)/shard_map/all_to_all | solution.py:519
  220.9 4.5 %copy-start.20 = (pred[1024,256]{1,0:T(8,128)(4,1)S(1)}, pred[1024,256]{1,0:T(8,128)(4,1)}, u32[]{:S(2)}) copy-start(pred[1024,256]{1,0:T(8,128)(4,1)} %copy-done.19) | copy-start | bytes 786436
  223.9 1.8 copy-start.22
  223.9 3.4 %copy-start.10 = (bf16[16,32,2048]{2,1,0:T(8,128)(2,1)S(1)}, bf16[16,32,2048]{2,1,0:T(8,128)(2,1)}, u32[]{:S(2)}) copy-start(bf16[16,32,2048]{2,1,0:T(8,128)(2,1)} %copy-done.9) | copy-start | bytes 6291460
  225.4 1.8 copy-start.5
  225.7 2.9 copy-start.2
  233.3 1.4 copy-start.11
  234.7 13.6 %copy-start.35 = (s32[8]{0:T(128)S(1)}, s32[8]{0:T(128)}, u32[]{:S(2)}) copy-start(s32[8]{0:T(128)} %constant.167.clone) | copy-start | bytes 100
  234.7 13.6 %copy-start.36 = (s32[8]{0:T(128)S(1)}, s32[8]{0:T(128)}, u32[]{:S(2)}) copy-start(s32[8]{0:T(128)} %constant.168.clone) | copy-start | bytes 100
  248.3 6.7 %collective-permute-start.13 = (bf16[256,2048]{1,0:T(8,128)(2,1)}, bf16[256,2048]{1,0:T(8,128)(2,1)}, u32[]{:S(2)}, u32[]{:S(2)}) collective-permute-start(bf16[256,2048]{1,0:T(8,128)(2,1)} %shard_map.214), channel_id=1, source_target_pairs={{0,1},{1,0},{2,3},{3,2},{4,5},{5,4},{6,7},{7,6},{8,9},{9,8},{10,11... | collective-permute-start | bytes 3145736 | tf_op jit(solution)/shard_map/ppermute | solution.py:543
  248.3 39.2 %all-to-all-start.3 = ((bf16[16,32,2048]{2,1,0:T(8,128)(2,1)}), bf16[16,32,2048]{2,1,0:T(8,128)(2,1)}, u32[]{:S(2)}, u32[]{:S(2)}) async-start(bf16[16,32,2048]{2,1,0:T(8,128)(2,1)} %bitcast.57), calls=%async_computation.4 | async-start | bytes 4194304 | tf_op jit(solution)/shard_map/all_to_all | solution.py:519
  252.8 57.7 %reduce-scatter.5.cloned.1.call-start = ((), (), s32[]{:S(2)}) async-start(), calls=%async_computation.8 | async-start | bytes 2359296 | tf_op jit(solution)/shard_map/reduce_scatter | solution.py:551
  259.0 1.4 copy-start.13
  260.4 27.1 %copy-start.8 = (bf16[1024,256]{1,0:T(8,128)(2,1)S(1)}, bf16[1024,256]{1,0:T(8,128)(2,1)}, u32[]{:S(2)}) copy-start(bf16[1024,256]{1,0:T(8,128)(2,1)} %fusion.1.w_ref) | copy-start | bytes 1572868
  289.2 2.7 collective-permute-start.12
  291.0 19.5 %copy-start.18 = (bf16[64,2048]{1,0:T(8,128)(2,1)S(1)}, bf16[64,2048]{1,0:T(8,128)(2,1)}, u32[]{:S(2)}) copy-start(bf16[64,2048]{1,0:T(8,128)(2,1)} %copy-done.17) | copy-start | bytes 786436
  292.5 10.6 %collective-permute-start.16 = (bf16[64,2048]{1,0:T(8,128)(2,1)S(1)}, bf16[64,2048]{1,0:T(8,128)(2,1)S(1)}, u32[]{:S(2)}, u32[]{:S(2)}) collective-permute-start(bf16[64,2048]{1,0:T(8,128)(2,1)S(1)} %get-tuple-element.49), channel_id=1, source_target_pairs={{0,14},{1,15},{2,0},{3,1},{4,2},{5,3},{6,4},{7,5},{8,6},{9,7},{10,... | collective-permute-start | bytes 786440 | tf_op jit(solution)/shard_map/ppermute | solution.py:564
  293.6 9.5 %collective-permute-start.15 = (bf16[64,2048]{1,0:T(8,128)(2,1)S(1)}, bf16[64,2048]{1,0:T(8,128)(2,1)S(1)}, u32[]{:S(2)}, u32[]{:S(2)}) collective-permute-start(bf16[64,2048]{1,0:T(8,128)(2,1)S(1)} %get-tuple-element.50), channel_id=1, source_target_pairs={{0,2},{1,3},{2,4},{3,5},{4,6},{5,7},{6,8},{7,9},{8,10},{9,11},{10,... | collective-permute-start | bytes 786440 | tf_op jit(solution)/shard_map/ppermute | solution.py:564
  294.6 15.9 %collective-permute-start.14 = (bf16[64,2048]{1,0:T(8,128)(2,1)S(1)}, bf16[64,2048]{1,0:T(8,128)(2,1)}, u32[]{:S(2)}, u32[]{:S(2)}) collective-permute-start(bf16[64,2048]{1,0:T(8,128)(2,1)S(1)} %get-tuple-element.48), channel_id=1, source_target_pairs={{0,4},{1,13},{2,6},{3,15},{4,8},{5,1},{6,10},{7,3},{8,12},{9,5},{1... | collective-permute-start | bytes 786440 | tf_op jit(solution)/shard_map/ppermute | solution.py:564
  (15 other events, 12.0 us)
Sparse Core Ops, SparseCore 0:
  66.2 43.9 reduce-scatter.2
  125.4 41.4 all-gather.2
  260.6 42.6 reduce-scatter.4

commit v3 on v2

--- a/solution.py
+++ b/solution.py
@@ -11,7 +11,7 @@
 EPS=1e-6
 C=64
 K=128
-UNROLL = 8
+UNROLL = 16
 
 def mm(a,b):
     return lax.dot_general(a,b,(((1,),(0,)),((),())),preferred_element_type=F32)
@@ -39,7 +39,7 @@
 def mm1(a,b):
     return mm(a.astype(BF),b.astype(BF))
 
-def delta_kernel(q_ref,k_ref,v_ref,row_ref,col_ref,go_g,go_o,z_out,wq_s,u_s,p_s,kw_s,dr_s,z_s,el_s):
+def delta_kernel(q_ref,k_ref,v_ref,row_ref,col_ref,go_g,go_o,z_out,wq_s,u_s,p_s,kw_s,dr_s,el_s):
     n=q_ref.shape[0]//C
     rows=lax.broadcasted_iota(jnp.int32,(2*C,2*C),0)
     cols=lax.broadcasted_iota(jnp.int32,(2*C,2*C),1)
@@ -110,38 +110,30 @@
     eye=jnp.where(lax.broadcasted_iota(jnp.int32,(K,K),0)==lax.broadcasted_iota(jnp.int32,(K,K),1),1.0,0.0)
     start=jnp.concatenate([eye,jnp.zeros((K,K),F32)],1)
     def chain(c,zs):
-        new=[]
+        new=[];fresh=[];outs=[]
         el=el_s[c]
         for h in range(2):
             z=zs[h]
-            z_s[c,h]=z.astype(BF)
+            zb=z.astype(BF)
             e=jnp.sum(jnp.where(lax.broadcasted_iota(jnp.int32,(1,2*C),1)==h*C,el,0.0),axis=1,keepdims=True)
             t=e*z-mm3(kw_s[h,c],z)
             new.append(jnp.concatenate([t[:,:K],t[:,K:]+dr_s[h,c]],1))
+            w=wq_s[c,0,h*C:(h+1)*C,:]
+            q=wq_s[c,1,h*C:(h+1)*C,:]
+            r=mm(jnp.concatenate([w,q],0),zb)
+            f=-r[:C]
+            uu=u_s[c,h*C:(h+1)*C,:]
+            fresh.append(jnp.concatenate([f[:,:K],f[:,K:]+uu],1))
+            outs.append(r[C:])
+        out=jnp.concatenate(outs,0)+mm(p_s[c],jnp.concatenate(fresh,0).astype(BF))
+        at=pl.ds(pl.multiple_of(c*C,C),C)
+        for h in range(2):
+            go_g[h,at,:]=out[h*C:(h+1)*C,:K].astype(BF)
+            go_o[h,at,:]=out[h*C:(h+1)*C,K:]
         return tuple(new)
-    zs=lax.fori_loop(0,n,chain,(start,start),unroll=4)
+    zs=lax.fori_loop(0,n,chain,(start,start),unroll=8)
     for h in range(2):
         z_out[h]=zs[h].astype(BF)
-    def emit(step,carry):
-        for u in range(UNROLL):
-            c=step*UNROLL+u
-            fresh=[];outs=[]
-            for h in range(2):
-                z=z_s[c,h]
-                w=wq_s[c,0,h*C:(h+1)*C,:]
-                q=wq_s[c,1,h*C:(h+1)*C,:]
-                r=mm(jnp.concatenate([w,q],0),z)
-                f=-r[:C]
-                uu=u_s[c,h*C:(h+1)*C,:]
-                fresh.append(jnp.concatenate([f[:,:K],f[:,K:]+uu],1))
-                outs.append(r[C:])
-            out=jnp.concatenate(outs,0)+mm(p_s[c],jnp.concatenate(fresh,0).astype(BF))
-            at=pl.ds(pl.multiple_of(c*C,C),C)
-            for h in range(2):
-                go_g[h,at,:]=out[h*C:(h+1)*C,:K].astype(BF)
-                go_o[h,at,:]=out[h*C:(h+1)*C,K:]
-        return carry
-    lax.fori_loop(0,n//UNROLL,emit,0)
 
 def whole(shape):
     return pl.BlockSpec(tuple(shape),lambda *_: (0,)*len(shape))
@@ -161,7 +153,7 @@
         out_shape=[jax.ShapeDtypeStruct(a,d) for a,d in shapes],
         in_specs=[whole(a.shape) for a in (q,k,v,row,col)],out_specs=[whole(a) for a,d in shapes],
         scratch_shapes=[pltpu.VMEM((n,2,2*C,K),BF),pltpu.VMEM((n,2*C,K),F32),pltpu.VMEM((n,2*C,2*C),BF),
-            pltpu.VMEM((2,n,K,K),F32),pltpu.VMEM((2,n,K,K),F32),pltpu.VMEM((n,2,K,2*K),BF),pltpu.VMEM((n,1,2*C),F32)],
+            pltpu.VMEM((2,n,K,K),F32),pltpu.VMEM((2,n,K,K),F32),pltpu.VMEM((n,1,2*C),F32)],
         compiler_params=pltpu.CompilerParams(vmem_limit_bytes=56*2**20),
     )(q,k,v,row,col)
 
@@ -369,40 +361,37 @@
     out_ref[...] = mm(w_ref[...], rows).astype(BF)
 
 
-def combine(weights, y, at, half):
+def combine(weights, y, half):
     part = GROUP * TOK
     return pl.pallas_call(
         combine_kernel,
         grid=(1,),
         out_shape=jax.ShapeDtypeStruct((part, D), BF),
         in_specs=[
-            pl.BlockSpec((part, weights.shape[1]), lambda i: (at, 0)),
+            whole(weights.shape),
             pl.BlockSpec((y.shape[0], GROUP * CAP, D), lambda i: (0, half, 0)),
         ],
-        out_specs=pl.BlockSpec((part, D), lambda i: (0, 0)),
+        out_specs=whole((part, D)),
         compiler_params=params(16),
     )(weights, y)
 
 
 def place_kernel(at_ref, own_ref, got_ref, out_ref):
-    i = pl.program_id(0)
-    total = own_ref[...].astype(F32) + got_ref[...].astype(F32)
-    out_ref[...] = jnp.where(at_ref[i] < GROUP, total, 0.0).astype(BF)
-
-
-def place(at, own, got):
-    part = pl.BlockSpec((TOK, D), lambda i, at: (jnp.minimum(at[i], GROUP - 1), 0))
-    chips = at.shape[0]
+    out_ref[...] = jnp.zeros_like(out_ref)
+    for i in range(GROUP):
+        rows = slice(i * TOK, (i + 1) * TOK)
+        total = own_ref[rows, :].astype(F32) + got_ref[rows, :].astype(F32)
+        out_ref[pl.ds(pl.multiple_of(at_ref[i] * TOK, TOK), TOK), :] = total.astype(BF)
+
+
+def place(at, own, got, chips):
     return pl.pallas_call(
         place_kernel,
-        grid_spec=pltpu.PrefetchScalarGridSpec(
-            num_scalar_prefetch=1,
-            grid=(chips,),
-            in_specs=[part, part],
-            out_specs=pl.BlockSpec((TOK, D), lambda i, at: (i, 0)),
-        ),
+        grid=(1,),
+        in_specs=[pl.BlockSpec(memory_space=pltpu.SMEM), whole(own.shape), whole(got.shape)],
+        out_specs=whole((chips * TOK, D)),
         out_shape=jax.ShapeDtypeStruct((chips * TOK, D), BF),
-        compiler_params=params(8),
+        compiler_params=params(16),
     )(at, own, got)
 
 
@@ -504,14 +493,14 @@
     )
     picks = sel.astype(BF)
     half_rows = rows // 2
-    attn, picks, chosen = lax.optimization_barrier((attn, picks, chosen))
+    far_order = order[rows // TOK // 2 :]
+    attn, picks, chosen, far_order = lax.optimization_barrier((attn, picks, chosen, far_order))
     mid = lax.optimization_barrier((residual.astype(F32) + attn).astype(BF)).astype(F32)
     normed = (mid / jnp.sqrt(jnp.mean(mid * mid, axis=-1, keepdims=True) + EPS) * post_gain).astype(
         BF
     )
     around = [lax.ppermute(normed, "exp", along_z(i, -1, n_exp)) for i in range(1, GROUP)]
     near_mine = jnp.concatenate([normed] + around, 0)
-    near_mine, normed = lax.optimization_barrier((near_mine, normed))
     near_sib = lax.ppermute(near_mine, "exp", core_pairs)
     normed_all = lax.all_gather(normed, "exp", tiled=True)
 
@@ -524,7 +513,7 @@
     near_rows = dispatch_near(picks[:half_rows], near_mine, near_sib)
     near_in = spread_out(near_rows)
     near_in, normed_far = lax.optimization_barrier((near_in, normed_all))
-    far_rows = dispatch_far(order[half_rows // TOK :], picks[half_rows:], normed_far)
+    far_rows = dispatch_far(far_order, picks[half_rows:], normed_far)
     far_in = spread_out(far_rows)
     near_out = experts_on(near_in)
     far_out = experts_on(far_in)
@@ -534,30 +523,24 @@
     raised = jnp.where(chosen, jnp.exp(logits), 0.0)
     gates = raised / jnp.sum(raised, axis=-1, keepdims=True)
     mine_gates = jnp.dot(gates, spread.astype(F32), precision=lax.Precision.HIGHEST)
-    weights = jnp.where(sel, mine_gates, 0.0).astype(BF)
+    weights = jnp.where(sel, mine_gates, 0.0).astype(BF).reshape(4, rows // 4, wide)
+    weights = lax.optimization_barrier([weights[i] for i in range(4)])
 
     far_back = spread_out(far_out)
     near_out, far_back = lax.optimization_barrier((near_out, far_back))
+
+    far_got = lax.ppermute(combine(weights[3], far_back, 1), "exp", core_pairs)
+    far_own = combine(weights[2], far_back, 0)
+    far_shift = jnp.where(at_core == 0, *[jnp.asarray(a, jnp.int32) for a in FAR])
+    far_placed = place((at_z + far_shift + chips) % chips, far_own, far_got, chips)
+    near_out, far_placed = lax.optimization_barrier((near_out, far_placed))
     near_back = spread_out(near_out)
-
-    far_got = lax.ppermute(combine(weights, far_back, 3, 1), "exp", core_pairs)
-    far_own = combine(weights, far_back, 2, 0)
-    tables = [[GROUP] * chips, [GROUP] * chips]
-    for core in range(2):
-        for i, d in enumerate(FAR[core]):
-            tables[core][d % chips] = i
-    table = jnp.where(at_core == 0, *[jnp.asarray(a, jnp.int32) for a in tables])
-    at = table[(jnp.arange(chips, dtype=jnp.int32) - at_z) % chips]
     far_sum = lax.psum_scatter(
-        place(at, far_own, far_got),
-        "exp",
-        scatter_dimension=0,
-        tiled=True,
-        axis_index_groups=same_core,
-    )
-
-    near_got = lax.ppermute(combine(weights, near_back, 1, 1), "exp", core_pairs)
-    near_own = combine(weights, near_back, 0, 0)
+        far_placed, "exp", scatter_dimension=0, tiled=True, axis_index_groups=same_core
+    )
+
+    near_got = lax.ppermute(combine(weights[1], near_back, 1), "exp", core_pairs)
+    near_own = combine(weights[0], near_back, 0)
     near_sum = (near_own.astype(F32) + near_got.astype(F32)).reshape(GROUP, TOK, D)
     mixture = near_sum[0] + far_sum.astype(F32)
     for i in (3, 1, 2):

time: 320 us -> 315 us (0.984)
  blocking collectives: 50.6 us -> 84.6 us
  waiting for transfers between devices: 125 us -> 107 us
  Pallas kernels: 48.3 us -> 38.8 us
  starting transfers between devices: 40.3 us -> 32 us
  local copies, waits for them, and re-layouts: 25.2 us -> 20.8 us
    all_to_all x1 -> x2, blocking collectives: 32.2 us -> 66.4 us  [spread_out(): return lax.all_to_all(rows, 'ctx', split_axis=0, concat_axis=0, tiled=True)]
    all_to_all x3 -> x2, waiting for transfers between devices: 71 us -> 44.1 us  [spread_out(): return lax.all_to_all(rows, 'ctx', split_axis=0, concat_axis=0, tiled=True)]
    all_to_all x3 -> x2, starting transfers between devices: 14.9 us -> 7.66 us  [spread_out(): return lax.all_to_all(rows, 'ctx', split_axis=0, concat_axis=0, tiled=True)]
    unnamed x80 -> x66, local copies, waits for them, and re-layouts: 17 us -> 12.6 us
    ppermute x3, waiting for transfers between devices: 11 us -> 14.7 us  [local(): sent = lax.ppermute(near_sum[i].astype(BF), 'exp', along_z(i, 1, n_exp))]
    pallas_call x4, Pallas kernels: 5.19 us -> 1.74 us  [combine(): pl.pallas_call(combine_kernel, grid=(1,), out_shape=jax.ShapeDtypeStruct(...]
    ppermute x2, waiting for transfers between devices: 0.96 us -> 4.36 us  [the longest x1 2.19 us: local(): lax.ppermute(combine(weights[1], near_back, 1), 'exp', core_pairs)]
  transfers between devices with their start and end apart: 23 -> 22, of which waited for: 16 -> 16; matrix products, arithmetic and copies ran while one was open for 6% -> 7% of each run, Pallas kernels for 12% -> 9%
where the time goes in v3:
time: 315 us; the launch traced here: 314 us
  waiting for transfers between devices  107 us (34%)
  blocking collectives  84.6 us (27%)
  Pallas kernels  38.8 us (12%)
  starting transfers between devices  32 us (10%)
  local copies, waits for them, and re-layouts  20.8 us (7%)
  between operations  14.2 us (5%)
  other arithmetic  10.6 us (3%)
  matrix products  5.81 us (2%)
    all_to_all x2, blocking collectives, spread_out(): return lax.all_to_all(rows, 'ctx', split_axis=0, concat_axis=0, tiled=True)  66.4 us
    all_to_all x2, waiting for transfers between devices, spread_out(): return lax.all_to_all(rows, 'ctx', split_axis=0, concat_axis=0, tiled=True)  44.1 us
    reduce_scatter x1, waiting for transfers between devices, local(): lax.psum_scatter(terms, 'exp', scatter_dimension=0, tiled=True, axis_inde...  21.1 us
    all_gather x1, blocking collectives, local(): routes_all = lax.all_gather(routes, 'exp', tiled=True)  18.2 us
    ppermute x3, waiting for transfers between devices, local(): sent = lax.ppermute(near_sum[i].astype(BF), 'exp', along_z(i, 1, n_exp))  14.7 us
    pallas_call x1, Pallas kernels, delta_local(): pl.pallas_call(delta_kernel, grid=(1,), out_shape=[jax.ShapeDtypeStruct(a...  14.5 us
    unnamed x66, local copies, waits for them, and re-layouts  12.6 us
    ppermute x3, waiting for transfers between devices, local(): lax.ppermute(normed, 'exp', along_z(i, -1, n_exp))  9.78 us
  transfers between devices with their start and end apart: 22, of which 16 were waited for; matrix products, arithmetic and copies ran while one was open for 7% of the time, Pallas kernels for 9%

profile of v3, /device:TPU:32, one launch (start us, length us, event | category | flops | bytes accessed | tf_op | source)
XLA Modules:
  0.0 314.0 jit_solution(1064634346873430401)
XLA Ops:
  11.4 14.5 %shard_map.203 = (bf16[2,1024,128]{2,1,0:T(8,128)(2,1)}, f32[2,1024,128]{2,1,0:T(8,128)}, bf16[2,128,256]{2,1,0:T(8,128)(2,1)}) custom-call(bf16[1024,128]{1,0:T(8,128)(2,1)} %q_ref.1, bf16[1024,128]{1,0:T(8,128)(2,1)} %k_ref.1, bf16[1024,256]{1,0:T(8,128)(2,1)} %v_ref.1, f32[48,128]{1,0:T(8,128)} %pad_maximum_fusion.1.row_ref, ...), custom_call_target="tpu_custom_call" | custom-call | tf_op jit(solution)/shard_map/pallas_call | solution.py:150
  25.9 1.5 collective-permute-start
  27.4 2.7 collective-permute-start.1
  30.1 1.4 collective-permute-start.2
  31.6 1.6 collective-permute-done.a1
  33.2 3.8 %collective-permute-done.1.a2 = bf16[2,128,256]{2,1,0:T(8,128)(2,1)S(1)} collective-permute-done((bf16[2,128,256]{2,1,0:T(8,128)(2,1)}, bf16[2,128,256]{2,1,0:T(8,128)(2,1)S(1)}, u32[]{:S(2)}, u32[]{:S(2)}) %collective-permute-start.1) | collective-permute-done | bytes 131104 | tf_op jit(solution)/shard_map/ppermute | solution.py:442
  37.7 2.6 shard_map.204
  40.3 3.5 %collective-permute-start.3 = (bf16[2,128,256]{2,1,0:T(8,128)(2,1)}, bf16[2,128,256]{2,1,0:T(8,128)(2,1)S(1)}, u32[]{:S(2)}, u32[]{:S(2)}) collective-permute-start(bf16[2,128,256]{2,1,0:T(8,128)(2,1)} %get-tuple-element.30), channel_id=1, source_target_pairs={{0,64},{16,80},{32,96},{48,112},{64,128},{80,144},{96,160},{112,17... | collective-permute-start | bytes 393224 | tf_op jit(solution)/shard_map/ppermute | solution.py:451
  43.8 4.8 %collective-permute-start.4 = (bf16[2,128,256]{2,1,0:T(8,128)(2,1)}, bf16[2,128,256]{2,1,0:T(8,128)(2,1)S(1)}, u32[]{:S(2)}, u32[]{:S(2)}) collective-permute-start(bf16[2,128,256]{2,1,0:T(8,128)(2,1)} %get-tuple-element.30), channel_id=1, source_target_pairs={{0,128},{16,144},{32,160},{48,176},{64,192},{80,208},{96,224},{112... | collective-permute-start | bytes 393224 | tf_op jit(solution)/shard_map/ppermute | solution.py:451
  48.6 1.3 collective-permute-start.5
  49.9 1.5 collective-permute-done.4.b2
  51.4 1.3 collective-permute-done.5.b3
  53.3 3.9 %shard_map.205 = (bf16[1024,256]{1,0:T(8,128)(2,1)}, bf16[512,256]{1,0:T(8,128)(2,1)}, bf16[512,256]{1,0:T(8,128)(2,1)}) custom-call(s32[1]{0:T(128)} %bitcast.par_ref, bf16[2,1024,128]{2,1,0:T(8,128)(2,1)} %get-tuple-element.26.g_ref, f32[2,1024,128]{2,1,0:T(8,128)} %get-tuple-element.27.o_ref, f32[2,128,256]{2,1,0:T(8,128)} %get-tuple-element.29.prefix, ...), custom_call_target="tpu_custom_call" | custom-call | tf_op jit(solution)/shard_map/pallas_call | solution.py:241
  57.2 1.7 collective-permute-done.6.b_ref
  59.9 3.1 %shard_map.206 = bf16[512,2048]{1,0:T(8,128)(2,1)} custom-call(bf16[512,256]{1,0:T(8,128)(2,1)S(1)} %copy-done.12, bf16[512,256]{1,0:T(8,128)(2,1)S(1)} %collective-permute-done.6.b_ref, bf16[256,2048]{1,0:T(8,128)(2,1)S(1)} %copy-done.10, bf16[256,2048]{1,0:T(8,128)(2,1)S(1)} %collective-permute-done.7.wb_ref), custom_call_target="tpu_custom_call" | custom-call | tf_op jit(solution)/shard_map/pallas_call | solution.py:261
  63.9 18.2 %all-gather = s32[16,64,10]{1,2,0:T(8,128)S(1)} all-gather(s32[1,64,10]{1,2,0:T(8,128)S(1)} %bitcast.67), channel_id=1, replica_groups=mesh['ctx'=16,'exp'=16] {'exp'}, dimensions={0}, use_global_device_ids=true | all-gather | bytes 43520 | tf_op jit(solution)/shard_map/all_gather | solution.py:460
  82.8 1.9 fusion
  86.4 21.1 %reduce-scatter.3.cloned.1.call-done = bf16[64,2048]{1,0:T(8,128)(2,1)} async-done(((bf16[512,2048]{1,0:T(8,128)(2,1)}), bf16[64,2048]{1,0:T(8,128)(2,1)}) %reduce-scatter.3.cloned.1.call-update) | async-done | bytes 262160 | tf_op jit(solution)/shard_map/reduce_scatter | solution.py:457
  110.2 1.8 collective-permute-start.10
  112.7 1.3 collective-permute-start.8
  114.0 6.7 %collective-permute-done.10 = bf16[64,2048]{1,0:T(8,128)(2,1)S(1)} collective-permute-done((bf16[64,2048]{1,0:T(8,128)(2,1)}, bf16[64,2048]{1,0:T(8,128)(2,1)S(1)}, u32[]{:S(2)}, u32[]{:S(2)}) %collective-permute-start.10) | collective-permute-done | bytes 262176 | tf_op jit(solution)/shard_map/ppermute | solution.py:502
  120.7 3.1 collective-permute-done.8
  124.9 2.6 collective-permute-done.11.sib_ref
  128.3 35.2 %all_to_all.20 = bf16[16,32,2048]{2,1,0:T(8,128)(2,1)} all-to-all(bf16[16,32,2048]{2,1,0:T(8,128)(2,1)S(1)} %shard_map.207), channel_id=1, replica_groups=mesh['ctx'=16,'exp'=16] {'ctx'}, dimensions={0} | all-to-all | bytes 4194304 | tf_op jit(solution)/shard_map/all_to_all | solution.py:508
  163.5 2.2 copy-done.3
  165.7 1.6 shard_map.209
  167.3 31.2 %all_to_all.21 = bf16[16,32,2048]{2,1,0:T(8,128)(2,1)S(1)} all-to-all(bf16[16,32,2048]{2,1,0:T(8,128)(2,1)S(1)} %shard_map.209), channel_id=1, replica_groups=mesh['ctx'=16,'exp'=16] {'ctx'}, dimensions={0} | all-to-all | bytes 4194304 | tf_op jit(solution)/shard_map/all_to_all | solution.py:508
  198.5 4.8 %shard_map.210 = bf16[512,2048]{1,0:T(8,128)(2,1)S(1)} custom-call(bf16[512,2048]{1,0:T(8,128)(2,1)S(1)} %bitcast.57, bf16[2048,1024]{1,0:T(8,128)(2,1)S(1)} %bitcast.48, bf16[2048,1024]{1,0:T(8,128)(2,1)S(1)} %bitcast.49, bf16[512,2048]{1,0:T(8,128)(2,1)S(1)} %bitcast.52), custom_call_target="tpu_custom_call" | custom-call | flops 3221225472 | bytes 10485760 | tf_op jit(solution)/shard_map/pallas_call | solution.py:340
  203.3 1.4 copy-done.8
  204.7 3.9 %all-to-all-start.2 = ((bf16[16,32,2048]{2,1,0:T(8,128)(2,1)}), bf16[16,32,2048]{2,1,0:T(8,128)(2,1)S(1)}, u32[]{:S(2)}, u32[]{:S(2)}) async-start(bf16[16,32,2048]{2,1,0:T(8,128)(2,1)} %bitcast.56), calls=%async_computation.3 | async-start | bytes 4194304 | tf_op jit(solution)/shard_map/all_to_all | solution.py:508
  208.6 4.4 %fusion.50 = f32[1024,256]{1,0:T(8,128)} fusion(bf16[1024,2048]{1,0:T(8,128)(2,1)} %all-gather.3.cloned.1.call-done.r0.r1.r2.r3, bf16[2048,256]{1,0:T(8,128)(2,1)S(1)} %copy-done), kind=kOutput, calls=%fused_computation.95 | convolution fusion | flops 1073741824 | bytes 6291456 | tf_op jit(solution)/shard_map/dot_general | solution.py:521
  213.0 2.8 gather_fusion.1
  215.9 1.5 exp.6
  219.1 1.3 copy-done.2
  220.4 4.8 %shard_map.208 = bf16[512,2048]{1,0:T(8,128)(2,1)S(1)} custom-call(bf16[512,2048]{1,0:T(8,128)(2,1)S(1)} %bitcast.54, bf16[2048,1024]{1,0:T(8,128)(2,1)S(1)} %bitcast.50, bf16[2048,1024]{1,0:T(8,128)(2,1)S(1)} %bitcast.51, bf16[512,2048]{1,0:T(8,128)(2,1)S(1)} %bitcast.53), custom_call_target="tpu_custom_call" | custom-call | flops 3221225472 | bytes 10485760 | tf_op jit(solution)/shard_map/pallas_call | solution.py:340
  225.2 1.4 copy-done.7
  226.6 10.9 %all-to-all-done.2.y_ref = bf16[16,32,2048]{2,1,0:T(8,128)(2,1)S(1)} async-done(((bf16[16,32,2048]{2,1,0:T(8,128)(2,1)}), bf16[16,32,2048]{2,1,0:T(8,128)(2,1)S(1)}, u32[]{:S(2)}, u32[]{:S(2)}) %all-to-all-start.2) | async-done | bytes 2097184 | tf_op jit(solution)/shard_map/all_to_all | solution.py:508
  239.4 2.2 collective-permute-done.12.got_ref
  242.5 1.3 copy-done.9
  243.8 3.7 %all-to-all-start.3 = ((bf16[16,32,2048]{2,1,0:T(8,128)(2,1)}), bf16[16,32,2048]{2,1,0:T(8,128)(2,1)S(1)}, u32[]{:S(2)}, u32[]{:S(2)}) async-start(bf16[16,32,2048]{2,1,0:T(8,128)(2,1)} %bitcast.55), calls=%async_computation.4 | async-start | bytes 4194304 | tf_op jit(solution)/shard_map/all_to_all | solution.py:508
  248.3 33.2 %all-to-all-done.3.y_ref = bf16[16,32,2048]{2,1,0:T(8,128)(2,1)S(1)} async-done(((bf16[16,32,2048]{2,1,0:T(8,128)(2,1)}), bf16[16,32,2048]{2,1,0:T(8,128)(2,1)S(1)}, u32[]{:S(2)}, u32[]{:S(2)}) %all-to-all-start.3) | async-done | bytes 2097184 | tf_op jit(solution)/shard_map/all_to_all | solution.py:508
  282.5 2.2 collective-permute-done.13
  285.2 2.4 collective-permute-start.16
  287.6 2.4 collective-permute-start.14
  290.0 6.0 %collective-permute-done.16 = bf16[64,2048]{1,0:T(8,128)(2,1)S(1)} collective-permute-done((bf16[64,2048]{1,0:T(8,128)(2,1)S(1)}, bf16[64,2048]{1,0:T(8,128)(2,1)S(1)}, u32[]{:S(2)}, u32[]{:S(2)}) %collective-permute-start.16) | collective-permute-done | bytes 262176 | tf_op jit(solution)/shard_map/ppermute | solution.py:547
  296.0 1.3 collective-permute-done.15
  297.9 7.4 %collective-permute-done.14 = bf16[64,2048]{1,0:T(8,128)(2,1)} collective-permute-done((bf16[64,2048]{1,0:T(8,128)(2,1)S(1)}, bf16[64,2048]{1,0:T(8,128)(2,1)}, u32[]{:S(2)}, u32[]{:S(2)}) %collective-permute-start.14) | collective-permute-done | bytes 262176 | tf_op jit(solution)/shard_map/ppermute | solution.py:547
  305.4 2.1 fusion.9
  (125 shorter events, 22.3 us)
Async XLA Ops:
  7.2 201.5 %copy-start = (bf16[2048,256]{1,0:T(8,128)(2,1)S(1)}, bf16[2048,256]{1,0:T(8,128)(2,1)}, u32[]{:S(2)}) copy-start(bf16[2048,256]{1,0:T(8,128)(2,1)} %param.30) | copy-start | bytes 3145732
  7.2 100.4 %reduce-scatter.3.cloned.1.call-start = ((), (), s32[]{:S(2)}) async-start(), calls=%async_computation.6 | async-start | bytes 2359296 | tf_op jit(solution)/shard_map/reduce_scatter | solution.py:457
  7.2 51.7 %collective-permute-start.7 = (bf16[256,2048]{1,0:T(8,128)(2,1)}, bf16[256,2048]{1,0:T(8,128)(2,1)S(1)}, u32[]{:S(2)}, u32[]{:S(2)}) collective-permute-start(bf16[256,2048]{1,0:T(8,128)(2,1)} %wa_ref.1), channel_id=1, source_target_pairs={{0,1},{1,0},{2,3},{3,2},{4,5},{5,4},{6,7},{7,6},{8,9},{9,8},{10,11... | collective-permute-start | bytes 3145736 | tf_op jit(solution)/shard_map/ppermute | solution.py:439
  11.4 47.5 %copy-start.10 = (bf16[256,2048]{1,0:T(8,128)(2,1)S(1)}, bf16[256,2048]{1,0:T(8,128)(2,1)}, u32[]{:S(2)}) copy-start(bf16[256,2048]{1,0:T(8,128)(2,1)} %wa_ref.1) | copy-start | bytes 3145732
  25.9 7.3 %collective-permute-start = (bf16[2,128,256]{2,1,0:T(8,128)(2,1)}, bf16[2,128,256]{2,1,0:T(8,128)(2,1)S(1)}, u32[]{:S(2)}, u32[]{:S(2)}) collective-permute-start(bf16[2,128,256]{2,1,0:T(8,128)(2,1)} %get-tuple-element.28.own), channel_id=1, source_target_pairs={{0,16},{16,32},{32,48},{48,0},{64,80},{80,96},{96,112},{112,64},{1... | collective-permute-start | bytes 393224 | tf_op jit(solution)/shard_map/ppermute | solution.py:442
  27.4 9.6 %collective-permute-start.1 = (bf16[2,128,256]{2,1,0:T(8,128)(2,1)}, bf16[2,128,256]{2,1,0:T(8,128)(2,1)S(1)}, u32[]{:S(2)}, u32[]{:S(2)}) collective-permute-start(bf16[2,128,256]{2,1,0:T(8,128)(2,1)} %get-tuple-element.28.own), channel_id=1, source_target_pairs={{0,32},{16,48},{32,0},{48,16},{64,96},{80,112},{96,64},{112,80},{1... | collective-permute-start | bytes 393224 | tf_op jit(solution)/shard_map/ppermute | solution.py:442
  30.1 6.8 %collective-permute-start.2 = (bf16[2,128,256]{2,1,0:T(8,128)(2,1)}, bf16[2,128,256]{2,1,0:T(8,128)(2,1)S(1)}, u32[]{:S(2)}, u32[]{:S(2)}) collective-permute-start(bf16[2,128,256]{2,1,0:T(8,128)(2,1)} %get-tuple-element.28.own), channel_id=1, source_target_pairs={{0,48},{16,0},{32,16},{48,32},{64,112},{80,64},{96,80},{112,96},{1... | collective-permute-start | bytes 393224 | tf_op jit(solution)/shard_map/ppermute | solution.py:442
  33.2 3.8 %copy-start.19 = (bf16[2,128,256]{2,1,0:T(8,128)(2,1)}, bf16[2,128,256]{2,1,0:T(8,128)(2,1)S(1)}, u32[]{:S(2)}) copy-start(bf16[2,128,256]{2,1,0:T(8,128)(2,1)S(1)} %collective-permute-done.a1) | copy-start | bytes 393220
  40.3 9.6 %collective-permute-start.3 = (bf16[2,128,256]{2,1,0:T(8,128)(2,1)}, bf16[2,128,256]{2,1,0:T(8,128)(2,1)S(1)}, u32[]{:S(2)}, u32[]{:S(2)}) collective-permute-start(bf16[2,128,256]{2,1,0:T(8,128)(2,1)} %get-tuple-element.30), channel_id=1, source_target_pairs={{0,64},{16,80},{32,96},{48,112},{64,128},{80,144},{96,160},{112,17... | collective-permute-start | bytes 393224 | tf_op jit(solution)/shard_map/ppermute | solution.py:451
  43.8 7.6 %collective-permute-start.4 = (bf16[2,128,256]{2,1,0:T(8,128)(2,1)}, bf16[2,128,256]{2,1,0:T(8,128)(2,1)S(1)}, u32[]{:S(2)}, u32[]{:S(2)}) collective-permute-start(bf16[2,128,256]{2,1,0:T(8,128)(2,1)} %get-tuple-element.30), channel_id=1, source_target_pairs={{0,128},{16,144},{32,160},{48,176},{64,192},{80,208},{96,224},{112... | collective-permute-start | bytes 393224 | tf_op jit(solution)/shard_map/ppermute | solution.py:451
  48.6 4.1 %collective-permute-start.5 = (bf16[2,128,256]{2,1,0:T(8,128)(2,1)}, bf16[2,128,256]{2,1,0:T(8,128)(2,1)S(1)}, u32[]{:S(2)}, u32[]{:S(2)}) collective-permute-start(bf16[2,128,256]{2,1,0:T(8,128)(2,1)} %get-tuple-element.30), channel_id=1, source_target_pairs={{0,192},{16,208},{32,224},{48,240},{1,193},{17,209},{33,225},{49,2... | collective-permute-start | bytes 393224 | tf_op jit(solution)/shard_map/ppermute | solution.py:451
  49.9 2.8 copy-start.20
  51.4 1.3 copy-start.22
  57.2 1.7 collective-permute-start.6
  58.9 1.0 copy-start.12
  63.1 0.8 copy-start.26
  63.1 21.6 %copy-start.27 = (s32[256]{0:T(256)S(1)}, s32[256]{0:T(256)}, u32[]{:S(2)}) copy-start(s32[256]{0:T(256)} %param.32) | copy-start | bytes 3076
  63.1 100.4 %all-gather.3.cloned.1.call-start = ((), (), s32[]{:S(2)}) async-start(), calls=%async_computation.7 | async-start | bytes 4456448 | tf_op jit(solution)/shard_map/all_gather | solution.py:505
  85.4 23.2 %copy-start.16 = (bf16[64,2048]{1,0:T(8,128)(2,1)S(1)}, bf16[64,2048]{1,0:T(8,128)(2,1)}, u32[]{:S(2)}) copy-start(bf16[64,2048]{1,0:T(8,128)(2,1)} %param.28) | copy-start | bytes 786436
  85.4 23.9 %copy-start.25 = (f32[2048]{0:T(1024)S(1)}, f32[2048]{0:T(1024)}, u32[]{:S(2)}) copy-start(f32[2048]{0:T(1024)} %param.29) | copy-start | bytes 24580
  108.6 0.7 copy-start.13
  110.2 10.5 %collective-permute-start.10 = (bf16[64,2048]{1,0:T(8,128)(2,1)}, bf16[64,2048]{1,0:T(8,128)(2,1)S(1)}, u32[]{:S(2)}, u32[]{:S(2)}) collective-permute-start(bf16[64,2048]{1,0:T(8,128)(2,1)} %fusion.8), channel_id=1, source_target_pairs={{0,12},{1,5},{2,14},{3,7},{4,0},{5,9},{6,2},{7,11},{8,4},{9,13},{1... | collective-permute-start | bytes 786440 | tf_op jit(solution)/shard_map/ppermute | solution.py:502
  112.0 8.7 %collective-permute-start.9 = (bf16[64,2048]{1,0:T(8,128)(2,1)}, bf16[64,2048]{1,0:T(8,128)(2,1)S(1)}, u32[]{:S(2)}, u32[]{:S(2)}) collective-permute-start(bf16[64,2048]{1,0:T(8,128)(2,1)} %fusion.8), channel_id=1, source_target_pairs={{0,2},{1,3},{2,4},{3,5},{4,6},{5,7},{6,8},{7,9},{8,10},{9,11},{10,... | collective-permute-start | bytes 786440 | tf_op jit(solution)/shard_map/ppermute | solution.py:502
  112.7 11.1 %collective-permute-start.8 = (bf16[64,2048]{1,0:T(8,128)(2,1)}, bf16[64,2048]{1,0:T(8,128)(2,1)S(1)}, u32[]{:S(2)}, u32[]{:S(2)}) collective-permute-start(bf16[64,2048]{1,0:T(8,128)(2,1)} %fusion.8), channel_id=1, source_target_pairs={{0,14},{1,15},{2,0},{3,1},{4,2},{5,3},{6,4},{7,5},{8,6},{9,7},{10,... | collective-permute-start | bytes 786440 | tf_op jit(solution)/shard_map/ppermute | solution.py:502
  124.8 2.7 collective-permute-start.11
  163.5 2.2 copy-start.3
  165.7 32.8 %copy-start.4 = (bf16[1,512,2048]{2,1,0:T(8,128)(2,1)S(1)}, bf16[1,512,2048]{2,1,0:T(8,128)(2,1)}, u32[]{:S(2)}) copy-start(bf16[1,512,2048]{2,1,0:T(8,128)(2,1)} %param.34) | copy-start | bytes 6291460
  167.3 31.2 %copy-start.1 = (bf16[1,2048,1024]{2,1,0:T(8,128)(2,1)S(1)}, bf16[1,2048,1024]{2,1,0:T(8,128)(2,1)}, u32[]{:S(2)}) copy-start(bf16[1,2048,1024]{2,1,0:T(8,128)(2,1)} %param.33) | copy-start | bytes 12582916
  203.3 1.4 copy-start.8
  204.7 32.8 %all-to-all-start.2 = ((bf16[16,32,2048]{2,1,0:T(8,128)(2,1)}), bf16[16,32,2048]{2,1,0:T(8,128)(2,1)S(1)}, u32[]{:S(2)}, u32[]{:S(2)}) async-start(bf16[16,32,2048]{2,1,0:T(8,128)(2,1)} %bitcast.56), calls=%async_computation.3 | async-start | bytes 4194304 | tf_op jit(solution)/shard_map/all_to_all | solution.py:508
  215.9 1.8 copy-start.15
  215.9 3.2 %copy-start.6 = (bf16[16,32,2048]{2,1,0:T(8,128)(2,1)S(1)}, bf16[16,32,2048]{2,1,0:T(8,128)(2,1)}, u32[]{:S(2)}) copy-start(bf16[16,32,2048]{2,1,0:T(8,128)(2,1)} %all_to_all.20) | copy-start | bytes 6291460
  217.4 1.7 copy-start.5
  217.7 2.7 copy-start.2
  225.2 1.4 copy-start.7
  226.6 12.4 %copy-start.28 = (s32[4]{0:T(128)S(1)}, s32[4]{0:T(128)}, u32[]{:S(2)}) copy-start(s32[4]{0:T(128)} %constant.166.clone) | copy-start | bytes 52
  226.6 12.4 %copy-start.29 = (s32[4]{0:T(128)S(1)}, s32[4]{0:T(128)}, u32[]{:S(2)}) copy-start(s32[4]{0:T(128)} %constant.167.clone) | copy-start | bytes 52
  237.5 0.9 copy-start.11
  238.8 2.7 collective-permute-start.12
  242.5 1.3 copy-start.9
  243.8 37.6 %all-to-all-start.3 = ((bf16[16,32,2048]{2,1,0:T(8,128)(2,1)}), bf16[16,32,2048]{2,1,0:T(8,128)(2,1)S(1)}, u32[]{:S(2)}, u32[]{:S(2)}) async-start(bf16[16,32,2048]{2,1,0:T(8,128)(2,1)} %bitcast.55), calls=%async_computation.4 | async-start | bytes 4194304 | tf_op jit(solution)/shard_map/all_to_all | solution.py:508
  247.6 57.8 %reduce-scatter.5.cloned.1.call-start = ((), (), s32[]{:S(2)}) async-start(), calls=%async_computation.8 | async-start | bytes 2359296 | tf_op jit(solution)/shard_map/reduce_scatter | solution.py:538
  281.9 2.7 collective-permute-start.13
  282.5 22.9 %copy-start.14 = (bf16[64,2048]{1,0:T(8,128)(2,1)S(1)}, bf16[64,2048]{1,0:T(8,128)(2,1)}, u32[]{:S(2)}) copy-start(bf16[64,2048]{1,0:T(8,128)(2,1)} %copy-done.13) | copy-start | bytes 786436
  285.2 10.8 %collective-permute-start.16 = (bf16[64,2048]{1,0:T(8,128)(2,1)S(1)}, bf16[64,2048]{1,0:T(8,128)(2,1)S(1)}, u32[]{:S(2)}, u32[]{:S(2)}) collective-permute-start(bf16[64,2048]{1,0:T(8,128)(2,1)S(1)} %get-tuple-element.59), channel_id=1, source_target_pairs={{0,14},{1,15},{2,0},{3,1},{4,2},{5,3},{6,4},{7,5},{8,6},{9,7},{10,... | collective-permute-start | bytes 786440 | tf_op jit(solution)/shard_map/ppermute | solution.py:547
  287.6 9.7 %collective-permute-start.15 = (bf16[64,2048]{1,0:T(8,128)(2,1)S(1)}, bf16[64,2048]{1,0:T(8,128)(2,1)S(1)}, u32[]{:S(2)}, u32[]{:S(2)}) collective-permute-start(bf16[64,2048]{1,0:T(8,128)(2,1)S(1)} %get-tuple-element.60), channel_id=1, source_target_pairs={{0,2},{1,3},{2,4},{3,5},{4,6},{5,7},{6,8},{7,9},{8,10},{9,11},{10,... | collective-permute-start | bytes 786440 | tf_op jit(solution)/shard_map/ppermute | solution.py:547
  287.6 17.8 %collective-permute-start.14 = (bf16[64,2048]{1,0:T(8,128)(2,1)S(1)}, bf16[64,2048]{1,0:T(8,128)(2,1)}, u32[]{:S(2)}, u32[]{:S(2)}) collective-permute-start(bf16[64,2048]{1,0:T(8,128)(2,1)S(1)} %get-tuple-element.58), channel_id=1, source_target_pairs={{0,4},{1,13},{2,6},{3,15},{4,8},{5,1},{6,10},{7,3},{8,12},{9,5},{1... | collective-permute-start | bytes 786440 | tf_op jit(solution)/shard_map/ppermute | solution.py:547
  296.0 1.3 copy-start.17
  (7 other events, 4.7 us)
Sparse Core Ops, SparseCore 0:
  63.2 44.2 reduce-scatter.2
  110.3 41.0 all-gather.2
  251.0 44.7 reduce-scatter.4

commit v4 on v3

--- a/solution.py
+++ b/solution.py
@@ -273,25 +273,49 @@
     )(a, b, wa, wb)
 
 
+def norm_kernel(res_ref, attn_ref, gain_ref, mid_ref, normed_ref):
+    mid = (res_ref[...].astype(F32) + attn_ref[...].astype(F32)).astype(BF)
+    mid_ref[...] = mid
+    mid = mid.astype(F32)
+    scale = lax.rsqrt(jnp.mean(mid * mid, axis=-1, keepdims=True) + EPS)
+    normed_ref[...] = (mid * scale * gain_ref[...]).astype(BF)
+
+
+def norm_rows(residual, attn, gain):
+    spec = whole(residual.shape)
+    shape = jax.ShapeDtypeStruct(residual.shape, BF)
+    return pl.pallas_call(
+        norm_kernel,
+        grid=(1,),
+        out_shape=(shape, shape),
+        in_specs=[spec, spec, whole(gain.shape)],
+        out_specs=(spec, spec),
+        compiler_params=params(16),
+    )(residual, attn, gain)
+
+
 def pick(sel, rows):
     out = lax.dot_general(sel, rows, (((0,), (0,)), ((), ())), preferred_element_type=F32)
     return out.astype(BF).reshape(sel.shape[1] // (GROUP * CAP), GROUP * CAP, D)
 
 
-def near_kernel(sel_ref, mine_ref, sib_ref, out_ref):
-    out_ref[:, : GROUP * CAP, :] = pick(sel_ref[: GROUP * TOK], mine_ref[...])
-    out_ref[:, GROUP * CAP :, :] = pick(sel_ref[GROUP * TOK :], sib_ref[...])
-
-
-def dispatch_near(sel, mine, sib):
+def near_kernel(sel_ref, *refs):
+    *parts, out_ref = refs
+    mine = jnp.concatenate([a[...] for a in parts[:GROUP]], 0)
+    sib = jnp.concatenate([a[...] for a in parts[GROUP:]], 0)
+    out_ref[:, : GROUP * CAP, :] = pick(sel_ref[: GROUP * TOK], mine)
+    out_ref[:, GROUP * CAP :, :] = pick(sel_ref[GROUP * TOK :], sib)
+
+
+def dispatch_near(sel, *parts):
     return pl.pallas_call(
         near_kernel,
         grid=(1,),
         out_shape=jax.ShapeDtypeStruct((16, 2 * GROUP * CAP, D), BF),
-        in_specs=[whole(sel.shape), whole(mine.shape), whole(sib.shape)],
+        in_specs=[whole(sel.shape)] + [whole(a.shape) for a in parts],
         out_specs=whole((16, 2 * GROUP * CAP, D)),
         compiler_params=params(16),
-    )(sel, mine, sib)
+    )(sel, *parts)
 
 
 def far_kernel(order_ref, sel_ref, r0, r1, r2, r3, out_ref):
@@ -456,7 +480,7 @@
     terms, routes = lax.optimization_barrier((terms, routes))
     attn = lax.psum_scatter(
         terms, "exp", scatter_dimension=0, tiled=True, axis_index_groups=same_core
-    ).astype(F32)
+    )
     routes_all = lax.all_gather(routes, "exp", tiled=True)
     rows = routes_all.shape[0]
     chips = n_exp // 2
@@ -495,13 +519,11 @@
     half_rows = rows // 2
     far_order = order[rows // TOK // 2 :]
     attn, picks, chosen, far_order = lax.optimization_barrier((attn, picks, chosen, far_order))
-    mid = lax.optimization_barrier((residual.astype(F32) + attn).astype(BF)).astype(F32)
-    normed = (mid / jnp.sqrt(jnp.mean(mid * mid, axis=-1, keepdims=True) + EPS) * post_gain).astype(
-        BF
-    )
+    mid, normed = norm_rows(residual, attn, post_gain.reshape(1, D))
+    mid = mid.astype(F32)
     around = [lax.ppermute(normed, "exp", along_z(i, -1, n_exp)) for i in range(1, GROUP)]
-    near_mine = jnp.concatenate([normed] + around, 0)
-    near_sib = lax.ppermute(near_mine, "exp", core_pairs)
+    near_mine = [normed] + around
+    near_sib = [lax.ppermute(a, "exp", core_pairs) for a in near_mine]
     normed_all = lax.all_gather(normed, "exp", tiled=True)
 
     def spread_out(rows):
@@ -510,7 +532,7 @@
     def experts_on(rows):
         return expert(rows.reshape(-1, D), expert_in[0], expert_out[0]).reshape(rows.shape)
 
-    near_rows = dispatch_near(picks[:half_rows], near_mine, near_sib)
+    near_rows = dispatch_near(picks[:half_rows], *near_mine, *near_sib)
     near_in = spread_out(near_rows)
     near_in, normed_far = lax.optimization_barrier((near_in, normed_all))
     far_rows = dispatch_far(far_order, picks[half_rows:], normed_far)

time: 315 us -> 312 us (level)
  waiting for transfers between devices: 107 us -> 100 us
  starting transfers between devices: 32 us -> 35.9 us
    ppermute x3, waiting for transfers between devices: 14.7 us -> 10.4 us  [local(): sent = lax.ppermute(near_sum[i].astype(BF), 'exp', along_z(i, 1, n_exp))]
    unnamed x66 -> x68, local copies, waits for them, and re-layouts: 12.6 us -> 13.9 us
  transfers between devices with their start and end apart: 22 -> 25, of which waited for: 16 -> 17; matrix products, arithmetic and copies ran while one was open for 7% -> 6% of each run, Pallas kernels for 9% -> 9%
where the time goes in v4:
time: 312 us
  waiting for transfers between devices  100 us (32%)
  blocking collectives  84.8 us (27%)
  Pallas kernels  40.7 us (13%)
  starting transfers between devices  35.9 us (12%)
  local copies, waits for them, and re-layouts  22.1 us (7%)
  between operations  14.2 us (5%)
  other arithmetic  7.55 us (2%)
  matrix products  5.83 us (2%)
    all_to_all x2, blocking collectives, spread_out(): return lax.all_to_all(rows, 'ctx', split_axis=0, concat_axis=0, tiled=True)  66.6 us
    all_to_all x2, waiting for transfers between devices, spread_out(): return lax.all_to_all(rows, 'ctx', split_axis=0, concat_axis=0, tiled=True)  44.2 us
    reduce_scatter x1, waiting for transfers between devices, local(): lax.psum_scatter(terms, 'exp', scatter_dimension=0, tiled=True, axis_inde...  21 us
    all_gather x1, blocking collectives, local(): routes_all = lax.all_gather(routes, 'exp', tiled=True)  18.2 us
    pallas_call x1, Pallas kernels, delta_local(): pl.pallas_call(delta_kernel, grid=(1,), out_shape=[jax.ShapeDtypeStruct(a...  14.5 us
    unnamed x68, local copies, waits for them, and re-layouts  13.9 us
    ppermute x3, waiting for transfers between devices, local(): sent = lax.ppermute(near_sum[i].astype(BF), 'exp', along_z(i, 1, n_exp))  10.4 us
    pallas_call x2, Pallas kernels, expert(): pl.pallas_call(expert_kernel, grid=(2,), out_shape=jax.ShapeDtypeStruct(x...  9.63 us
  transfers between devices with their start and end apart: 25, of which 17 were waited for; matrix products, arithmetic and copies ran while one was open for 6% of the time, Pallas kernels for 9%

profile of v4, /device:TPU:32, one launch (start us, length us, event | category | flops | bytes accessed | tf_op | source)
XLA Modules:
  0.0 311.6 jit_solution(17220723128500331230)
XLA Ops:
  11.4 14.5 %shard_map.203 = (bf16[2,1024,128]{2,1,0:T(8,128)(2,1)}, f32[2,1024,128]{2,1,0:T(8,128)}, bf16[2,128,256]{2,1,0:T(8,128)(2,1)}) custom-call(bf16[1024,128]{1,0:T(8,128)(2,1)} %q_ref.1, bf16[1024,128]{1,0:T(8,128)(2,1)} %k_ref.1, bf16[1024,256]{1,0:T(8,128)(2,1)} %v_ref.1, f32[48,128]{1,0:T(8,128)} %pad_maximum_fusion.row_ref, ...), custom_call_target="tpu_custom_call" | custom-call | tf_op jit(solution)/shard_map/pallas_call | solution.py:150
  25.9 1.5 collective-permute-start
  27.4 2.7 collective-permute-start.1
  30.1 1.4 collective-permute-start.2
  31.6 1.6 collective-permute-done.a1
  33.2 3.8 %collective-permute-done.1.a2 = bf16[2,128,256]{2,1,0:T(8,128)(2,1)S(1)} collective-permute-done((bf16[2,128,256]{2,1,0:T(8,128)(2,1)}, bf16[2,128,256]{2,1,0:T(8,128)(2,1)S(1)}, u32[]{:S(2)}, u32[]{:S(2)}) %collective-permute-start.1) | collective-permute-done | bytes 131104 | tf_op jit(solution)/shard_map/ppermute | solution.py:466
  37.7 2.6 shard_map.204
  40.3 3.5 %collective-permute-start.3 = (bf16[2,128,256]{2,1,0:T(8,128)(2,1)}, bf16[2,128,256]{2,1,0:T(8,128)(2,1)S(1)}, u32[]{:S(2)}, u32[]{:S(2)}) collective-permute-start(bf16[2,128,256]{2,1,0:T(8,128)(2,1)} %get-tuple-element.32), channel_id=1, source_target_pairs={{0,64},{16,80},{32,96},{48,112},{64,128},{80,144},{96,160},{112,17... | collective-permute-start | bytes 393224 | tf_op jit(solution)/shard_map/ppermute | solution.py:475
  43.8 4.8 %collective-permute-start.4 = (bf16[2,128,256]{2,1,0:T(8,128)(2,1)}, bf16[2,128,256]{2,1,0:T(8,128)(2,1)S(1)}, u32[]{:S(2)}, u32[]{:S(2)}) collective-permute-start(bf16[2,128,256]{2,1,0:T(8,128)(2,1)} %get-tuple-element.32), channel_id=1, source_target_pairs={{0,128},{16,144},{32,160},{48,176},{64,192},{80,208},{96,224},{112... | collective-permute-start | bytes 393224 | tf_op jit(solution)/shard_map/ppermute | solution.py:475
  48.6 1.3 collective-permute-start.5
  49.9 1.5 collective-permute-done.4.b2
  51.4 1.3 collective-permute-done.5.b3
  53.4 3.9 %shard_map.205 = (bf16[1024,256]{1,0:T(8,128)(2,1)}, bf16[512,256]{1,0:T(8,128)(2,1)}, bf16[512,256]{1,0:T(8,128)(2,1)}) custom-call(s32[1]{0:T(128)} %bitcast.par_ref, bf16[2,1024,128]{2,1,0:T(8,128)(2,1)} %get-tuple-element.28.g_ref, f32[2,1024,128]{2,1,0:T(8,128)} %get-tuple-element.29.o_ref, f32[2,128,256]{2,1,0:T(8,128)} %get-tuple-element.31.prefix, ...), custom_call_target="tpu_custom_call" | custom-call | tf_op jit(solution)/shard_map/pallas_call | solution.py:241
  57.2 1.7 collective-permute-done.6.b_ref
  59.9 3.1 %shard_map.206 = bf16[512,2048]{1,0:T(8,128)(2,1)} custom-call(bf16[512,256]{1,0:T(8,128)(2,1)S(1)} %copy-done.12, bf16[512,256]{1,0:T(8,128)(2,1)S(1)} %collective-permute-done.6.b_ref, bf16[256,2048]{1,0:T(8,128)(2,1)S(1)} %copy-done.10, bf16[256,2048]{1,0:T(8,128)(2,1)S(1)} %collective-permute-done.7.wb_ref), custom_call_target="tpu_custom_call" | custom-call | tf_op jit(solution)/shard_map/pallas_call | solution.py:261
  63.9 18.2 %all-gather = s32[16,64,10]{1,2,0:T(8,128)S(1)} all-gather(s32[1,64,10]{1,2,0:T(8,128)S(1)} %bitcast.69), channel_id=1, replica_groups=mesh['ctx'=16,'exp'=16] {'exp'}, dimensions={0}, use_global_device_ids=true | all-gather | bytes 43520 | tf_op jit(solution)/shard_map/all_gather | solution.py:484
  82.8 1.9 fusion
  86.5 21.0 %reduce-scatter.3.cloned.1.call-done.attn_ref = bf16[64,2048]{1,0:T(8,128)(2,1)} async-done(((bf16[512,2048]{1,0:T(8,128)(2,1)}), bf16[64,2048]{1,0:T(8,128)(2,1)}) %reduce-scatter.3.cloned.1.call-update) | async-done | bytes 262160 | tf_op jit(solution)/shard_map/reduce_scatter | solution.py:481
  110.1 1.3 collective-permute-start.8
  112.2 3.0 collective-permute-start.10
  115.2 1.5 collective-permute-done.8.refs_1_
  116.7 3.3 %collective-permute-done.9.refs_2_ = bf16[64,2048]{1,0:T(8,128)(2,1)S(1)} collective-permute-done((bf16[64,2048]{1,0:T(8,128)(2,1)}, bf16[64,2048]{1,0:T(8,128)(2,1)S(1)}, u32[]{:S(2)}, u32[]{:S(2)}) %collective-permute-start.9) | collective-permute-done | bytes 262176 | tf_op jit(solution)/shard_map/ppermute | solution.py:524
  120.1 3.5 %collective-permute-done.10.refs_3_ = bf16[64,2048]{1,0:T(8,128)(2,1)S(1)} collective-permute-done((bf16[64,2048]{1,0:T(8,128)(2,1)}, bf16[64,2048]{1,0:T(8,128)(2,1)S(1)}, u32[]{:S(2)}, u32[]{:S(2)}) %collective-permute-start.10) | collective-permute-done | bytes 262176 | tf_op jit(solution)/shard_map/ppermute | solution.py:524
  123.7 1.5 collective-permute-done.14.refs_7_
  125.1 1.7 shard_map.208
  126.8 35.4 %all_to_all.20 = bf16[16,32,2048]{2,1,0:T(8,128)(2,1)} all-to-all(bf16[16,32,2048]{2,1,0:T(8,128)(2,1)S(1)} %shard_map.208), channel_id=1, replica_groups=mesh['ctx'=16,'exp'=16] {'ctx'}, dimensions={0} | all-to-all | bytes 4194304 | tf_op jit(solution)/shard_map/all_to_all | solution.py:530
  162.2 2.2 copy-done.3
  164.4 1.6 shard_map.210
  166.0 31.2 %all_to_all.21 = bf16[16,32,2048]{2,1,0:T(8,128)(2,1)S(1)} all-to-all(bf16[16,32,2048]{2,1,0:T(8,128)(2,1)S(1)} %shard_map.210), channel_id=1, replica_groups=mesh['ctx'=16,'exp'=16] {'ctx'}, dimensions={0} | all-to-all | bytes 4194304 | tf_op jit(solution)/shard_map/all_to_all | solution.py:530
  197.2 4.8 %shard_map.211 = bf16[512,2048]{1,0:T(8,128)(2,1)S(1)} custom-call(bf16[512,2048]{1,0:T(8,128)(2,1)S(1)} %bitcast.58, bf16[2048,1024]{1,0:T(8,128)(2,1)S(1)} %bitcast.49, bf16[2048,1024]{1,0:T(8,128)(2,1)S(1)} %bitcast.50, bf16[512,2048]{1,0:T(8,128)(2,1)S(1)} %bitcast.53), custom_call_target="tpu_custom_call" | custom-call | flops 3221225472 | bytes 10485760 | tf_op jit(solution)/shard_map/pallas_call | solution.py:364
  202.1 1.4 copy-done.8
  203.4 3.7 %all-to-all-start.2 = ((bf16[16,32,2048]{2,1,0:T(8,128)(2,1)}), bf16[16,32,2048]{2,1,0:T(8,128)(2,1)S(1)}, u32[]{:S(2)}, u32[]{:S(2)}) async-start(bf16[16,32,2048]{2,1,0:T(8,128)(2,1)} %bitcast.57), calls=%async_computation.3 | async-start | bytes 4194304 | tf_op jit(solution)/shard_map/all_to_all | solution.py:530
  207.2 4.4 %fusion.48 = f32[1024,256]{1,0:T(8,128)} fusion(bf16[1024,2048]{1,0:T(8,128)(2,1)} %all-gather.3.cloned.1.call-done.r0.r1.r2.r3, bf16[2048,256]{1,0:T(8,128)(2,1)S(1)} %copy-done), kind=kOutput, calls=%fused_computation.87 | convolution fusion | flops 1073741824 | bytes 6291456 | tf_op jit(solution)/shard_map/dot_general | solution.py:543
  211.6 2.9 gather_fusion.1
  214.5 1.5 exp.6
  219.0 4.8 %shard_map.209 = bf16[512,2048]{1,0:T(8,128)(2,1)S(1)} custom-call(bf16[512,2048]{1,0:T(8,128)(2,1)S(1)} %bitcast.55, bf16[2048,1024]{1,0:T(8,128)(2,1)S(1)} %bitcast.51, bf16[2048,1024]{1,0:T(8,128)(2,1)S(1)} %bitcast.52, bf16[512,2048]{1,0:T(8,128)(2,1)S(1)} %bitcast.54), custom_call_target="tpu_custom_call" | custom-call | flops 3221225472 | bytes 10485760 | tf_op jit(solution)/shard_map/pallas_call | solution.py:364
  223.8 1.4 copy-done.7
  225.2 11.0 %all-to-all-done.2.y_ref = bf16[16,32,2048]{2,1,0:T(8,128)(2,1)S(1)} async-done(((bf16[16,32,2048]{2,1,0:T(8,128)(2,1)}), bf16[16,32,2048]{2,1,0:T(8,128)(2,1)S(1)}, u32[]{:S(2)}, u32[]{:S(2)}) %all-to-all-start.2) | async-done | bytes 2097184 | tf_op jit(solution)/shard_map/all_to_all | solution.py:530
  238.2 2.2 collective-permute-done.15.got_ref
  241.3 1.3 copy-done.9
  242.6 3.7 %all-to-all-start.3 = ((bf16[16,32,2048]{2,1,0:T(8,128)(2,1)}), bf16[16,32,2048]{2,1,0:T(8,128)(2,1)S(1)}, u32[]{:S(2)}, u32[]{:S(2)}) async-start(bf16[16,32,2048]{2,1,0:T(8,128)(2,1)} %bitcast.56), calls=%async_computation.4 | async-start | bytes 4194304 | tf_op jit(solution)/shard_map/all_to_all | solution.py:530
  247.1 33.2 %all-to-all-done.3.y_ref = bf16[16,32,2048]{2,1,0:T(8,128)(2,1)S(1)} async-done(((bf16[16,32,2048]{2,1,0:T(8,128)(2,1)}), bf16[16,32,2048]{2,1,0:T(8,128)(2,1)S(1)}, u32[]{:S(2)}, u32[]{:S(2)}) %all-to-all-start.3) | async-done | bytes 2097184 | tf_op jit(solution)/shard_map/all_to_all | solution.py:530
  281.2 2.2 collective-permute-done.16
  284.2 1.9 collective-permute-start.18
  286.1 5.6 %collective-permute-start.17 = (bf16[64,2048]{1,0:T(8,128)(2,1)S(1)}, bf16[64,2048]{1,0:T(8,128)(2,1)}, u32[]{:S(2)}, u32[]{:S(2)}) collective-permute-start(bf16[64,2048]{1,0:T(8,128)(2,1)S(1)} %get-tuple-element.62), channel_id=1, source_target_pairs={{0,4},{1,13},{2,6},{3,15},{4,8},{5,1},{6,10},{7,3},{8,12},{9,5},{1... | collective-permute-start | bytes 786440 | tf_op jit(solution)/shard_map/ppermute | solution.py:569
  291.7 2.9 collective-permute-done.19
  296.0 6.9 %collective-permute-done.17 = bf16[64,2048]{1,0:T(8,128)(2,1)} collective-permute-done((bf16[64,2048]{1,0:T(8,128)(2,1)S(1)}, bf16[64,2048]{1,0:T(8,128)(2,1)}, u32[]{:S(2)}, u32[]{:S(2)}) %collective-permute-start.17) | collective-permute-done | bytes 262176 | tf_op jit(solution)/shard_map/ppermute | solution.py:569
  302.9 2.1 fusion.10
  (128 shorter events, 22.8 us)
Async XLA Ops:
  7.2 200.0 %copy-start = (bf16[2048,256]{1,0:T(8,128)(2,1)S(1)}, bf16[2048,256]{1,0:T(8,128)(2,1)}, u32[]{:S(2)}) copy-start(bf16[2048,256]{1,0:T(8,128)(2,1)} %param.30) | copy-start | bytes 3145732
  7.2 100.2 %reduce-scatter.3.cloned.1.call-start = ((), (), s32[]{:S(2)}) async-start(), calls=%async_computation.6 | async-start | bytes 2359296 | tf_op jit(solution)/shard_map/reduce_scatter | solution.py:481
  7.2 51.7 %collective-permute-start.7 = (bf16[256,2048]{1,0:T(8,128)(2,1)}, bf16[256,2048]{1,0:T(8,128)(2,1)S(1)}, u32[]{:S(2)}, u32[]{:S(2)}) collective-permute-start(bf16[256,2048]{1,0:T(8,128)(2,1)} %wa_ref.1), channel_id=1, source_target_pairs={{0,1},{1,0},{2,3},{3,2},{4,5},{5,4},{6,7},{7,6},{8,9},{9,8},{10,11... | collective-permute-start | bytes 3145736 | tf_op jit(solution)/shard_map/ppermute | solution.py:463
  11.4 47.6 %copy-start.10 = (bf16[256,2048]{1,0:T(8,128)(2,1)S(1)}, bf16[256,2048]{1,0:T(8,128)(2,1)}, u32[]{:S(2)}) copy-start(bf16[256,2048]{1,0:T(8,128)(2,1)} %wa_ref.1) | copy-start | bytes 3145732
  25.9 7.3 %collective-permute-start = (bf16[2,128,256]{2,1,0:T(8,128)(2,1)}, bf16[2,128,256]{2,1,0:T(8,128)(2,1)S(1)}, u32[]{:S(2)}, u32[]{:S(2)}) collective-permute-start(bf16[2,128,256]{2,1,0:T(8,128)(2,1)} %get-tuple-element.30.own), channel_id=1, source_target_pairs={{0,16},{16,32},{32,48},{48,0},{64,80},{80,96},{96,112},{112,64},{1... | collective-permute-start | bytes 393224 | tf_op jit(solution)/shard_map/ppermute | solution.py:466
  27.4 9.6 %collective-permute-start.1 = (bf16[2,128,256]{2,1,0:T(8,128)(2,1)}, bf16[2,128,256]{2,1,0:T(8,128)(2,1)S(1)}, u32[]{:S(2)}, u32[]{:S(2)}) collective-permute-start(bf16[2,128,256]{2,1,0:T(8,128)(2,1)} %get-tuple-element.30.own), channel_id=1, source_target_pairs={{0,32},{16,48},{32,0},{48,16},{64,96},{80,112},{96,64},{112,80},{1... | collective-permute-start | bytes 393224 | tf_op jit(solution)/shard_map/ppermute | solution.py:466
  30.1 6.8 %collective-permute-start.2 = (bf16[2,128,256]{2,1,0:T(8,128)(2,1)}, bf16[2,128,256]{2,1,0:T(8,128)(2,1)S(1)}, u32[]{:S(2)}, u32[]{:S(2)}) collective-permute-start(bf16[2,128,256]{2,1,0:T(8,128)(2,1)} %get-tuple-element.30.own), channel_id=1, source_target_pairs={{0,48},{16,0},{32,16},{48,32},{64,112},{80,64},{96,80},{112,96},{1... | collective-permute-start | bytes 393224 | tf_op jit(solution)/shard_map/ppermute | solution.py:466
  33.2 3.8 %copy-start.21 = (bf16[2,128,256]{2,1,0:T(8,128)(2,1)}, bf16[2,128,256]{2,1,0:T(8,128)(2,1)S(1)}, u32[]{:S(2)}) copy-start(bf16[2,128,256]{2,1,0:T(8,128)(2,1)S(1)} %collective-permute-done.a1) | copy-start | bytes 393220
  40.3 9.6 %collective-permute-start.3 = (bf16[2,128,256]{2,1,0:T(8,128)(2,1)}, bf16[2,128,256]{2,1,0:T(8,128)(2,1)S(1)}, u32[]{:S(2)}, u32[]{:S(2)}) collective-permute-start(bf16[2,128,256]{2,1,0:T(8,128)(2,1)} %get-tuple-element.32), channel_id=1, source_target_pairs={{0,64},{16,80},{32,96},{48,112},{64,128},{80,144},{96,160},{112,17... | collective-permute-start | bytes 393224 | tf_op jit(solution)/shard_map/ppermute | solution.py:475
  43.8 7.6 %collective-permute-start.4 = (bf16[2,128,256]{2,1,0:T(8,128)(2,1)}, bf16[2,128,256]{2,1,0:T(8,128)(2,1)S(1)}, u32[]{:S(2)}, u32[]{:S(2)}) collective-permute-start(bf16[2,128,256]{2,1,0:T(8,128)(2,1)} %get-tuple-element.32), channel_id=1, source_target_pairs={{0,128},{16,144},{32,160},{48,176},{64,192},{80,208},{96,224},{112... | collective-permute-start | bytes 393224 | tf_op jit(solution)/shard_map/ppermute | solution.py:475
  48.6 4.1 %collective-permute-start.5 = (bf16[2,128,256]{2,1,0:T(8,128)(2,1)}, bf16[2,128,256]{2,1,0:T(8,128)(2,1)S(1)}, u32[]{:S(2)}, u32[]{:S(2)}) collective-permute-start(bf16[2,128,256]{2,1,0:T(8,128)(2,1)} %get-tuple-element.32), channel_id=1, source_target_pairs={{0,192},{16,208},{32,224},{48,240},{1,193},{17,209},{33,225},{49,2... | collective-permute-start | bytes 393224 | tf_op jit(solution)/shard_map/ppermute | solution.py:475
  49.9 2.8 copy-start.22
  51.4 1.3 copy-start.24
  57.2 1.7 collective-permute-start.6
  59.0 1.0 copy-start.12
  63.1 21.6 %copy-start.28 = (s32[256]{0:T(256)S(1)}, s32[256]{0:T(256)}, u32[]{:S(2)}) copy-start(s32[256]{0:T(256)} %param.32) | copy-start | bytes 3076
  63.1 99.1 %all-gather.3.cloned.1.call-start = ((), (), s32[]{:S(2)}) async-start(), calls=%async_computation.7 | async-start | bytes 4456448 | tf_op jit(solution)/shard_map/all_gather | solution.py:527
  85.1 22.3 %copy-start.13 = (bf16[64,2048]{1,0:T(8,128)(2,1)S(1)}, bf16[64,2048]{1,0:T(8,128)(2,1)}, u32[]{:S(2)}) copy-start(bf16[64,2048]{1,0:T(8,128)(2,1)} %res_ref.1) | copy-start | bytes 786436
  85.1 22.3 %copy-start.17 = (f32[2048]{0:T(1024)S(1)}, f32[2048]{0:T(1024)}, u32[]{:S(2)}) copy-start(f32[2048]{0:T(1024)} %param.29) | copy-start | bytes 24580
  107.4 1.0 copy-start.14
  110.1 6.7 %collective-permute-start.8 = (bf16[64,2048]{1,0:T(8,128)(2,1)}, bf16[64,2048]{1,0:T(8,128)(2,1)S(1)}, u32[]{:S(2)}, u32[]{:S(2)}) collective-permute-start(bf16[64,2048]{1,0:T(8,128)(2,1)} %get-tuple-element.42.refs_0_), channel_id=1, source_target_pairs={{0,14},{1,15},{2,0},{3,1},{4,2},{5,3},{6,4},{7,5},{8,6},{9,7},{10,... | collective-permute-start | bytes 786440 | tf_op jit(solution)/shard_map/ppermute | solution.py:524
  111.4 8.7 %collective-permute-start.9 = (bf16[64,2048]{1,0:T(8,128)(2,1)}, bf16[64,2048]{1,0:T(8,128)(2,1)S(1)}, u32[]{:S(2)}, u32[]{:S(2)}) collective-permute-start(bf16[64,2048]{1,0:T(8,128)(2,1)} %get-tuple-element.42.refs_0_), channel_id=1, source_target_pairs={{0,2},{1,3},{2,4},{3,5},{4,6},{5,7},{6,8},{7,9},{8,10},{9,11},{10,... | collective-permute-start | bytes 786440 | tf_op jit(solution)/shard_map/ppermute | solution.py:524
  112.2 11.4 %collective-permute-start.10 = (bf16[64,2048]{1,0:T(8,128)(2,1)}, bf16[64,2048]{1,0:T(8,128)(2,1)S(1)}, u32[]{:S(2)}, u32[]{:S(2)}) collective-permute-start(bf16[64,2048]{1,0:T(8,128)(2,1)} %get-tuple-element.42.refs_0_), channel_id=1, source_target_pairs={{0,12},{1,5},{2,14},{3,7},{4,0},{5,9},{6,2},{7,11},{8,4},{9,13},{1... | collective-permute-start | bytes 786440 | tf_op jit(solution)/shard_map/ppermute | solution.py:524
  115.2 8.5 %collective-permute-start.11 = (bf16[64,2048]{1,0:T(8,128)(2,1)}, bf16[64,2048]{1,0:T(8,128)(2,1)S(1)}, u32[]{:S(2)}, u32[]{:S(2)}) collective-permute-start(bf16[64,2048]{1,0:T(8,128)(2,1)} %get-tuple-element.42.refs_0_), channel_id=1, source_target_pairs={{0,1},{1,0},{2,3},{3,2},{4,5},{5,4},{6,7},{7,6},{8,9},{9,8},{10,11... | collective-permute-start | bytes 786440 | tf_op jit(solution)/shard_map/ppermute | solution.py:526
  116.7 6.9 %collective-permute-start.12 = (bf16[64,2048]{1,0:T(8,128)(2,1)S(1)}, bf16[64,2048]{1,0:T(8,128)(2,1)S(1)}, u32[]{:S(2)}, u32[]{:S(2)}) collective-permute-start(bf16[64,2048]{1,0:T(8,128)(2,1)S(1)} %collective-permute-done.8.refs_1_), channel_id=1, source_target_pairs={{0,1},{1,0},{2,3},{3,2},{4,5},{5,4},{6,7},{7,6},{8,9},{9,8},{10,11... | collective-permute-start | bytes 786440 | tf_op jit(solution)/shard_map/ppermute | solution.py:526
  120.1 3.6 %collective-permute-start.13 = (bf16[64,2048]{1,0:T(8,128)(2,1)S(1)}, bf16[64,2048]{1,0:T(8,128)(2,1)S(1)}, u32[]{:S(2)}, u32[]{:S(2)}) collective-permute-start(bf16[64,2048]{1,0:T(8,128)(2,1)S(1)} %collective-permute-done.9.refs_2_), channel_id=1, source_target_pairs={{0,1},{1,0},{2,3},{3,2},{4,5},{5,4},{6,7},{7,6},{8,9},{9,8},{10,11... | collective-permute-start | bytes 786440 | tf_op jit(solution)/shard_map/ppermute | solution.py:526
  123.6 1.5 collective-permute-start.14
  162.2 2.2 copy-start.3
  164.4 32.8 %copy-start.4 = (bf16[1,512,2048]{2,1,0:T(8,128)(2,1)S(1)}, bf16[1,512,2048]{2,1,0:T(8,128)(2,1)}, u32[]{:S(2)}) copy-start(bf16[1,512,2048]{2,1,0:T(8,128)(2,1)} %param.34) | copy-start | bytes 6291460
  166.0 31.2 %copy-start.1 = (bf16[1,2048,1024]{2,1,0:T(8,128)(2,1)S(1)}, bf16[1,2048,1024]{2,1,0:T(8,128)(2,1)}, u32[]{:S(2)}) copy-start(bf16[1,2048,1024]{2,1,0:T(8,128)(2,1)} %param.33) | copy-start | bytes 12582916
  202.1 1.4 copy-start.8
  203.4 32.8 %all-to-all-start.2 = ((bf16[16,32,2048]{2,1,0:T(8,128)(2,1)}), bf16[16,32,2048]{2,1,0:T(8,128)(2,1)S(1)}, u32[]{:S(2)}, u32[]{:S(2)}) async-start(bf16[16,32,2048]{2,1,0:T(8,128)(2,1)} %bitcast.57), calls=%async_computation.3 | async-start | bytes 4194304 | tf_op jit(solution)/shard_map/all_to_all | solution.py:530
  214.5 1.8 copy-start.18
  214.5 3.2 %copy-start.6 = (bf16[16,32,2048]{2,1,0:T(8,128)(2,1)S(1)}, bf16[16,32,2048]{2,1,0:T(8,128)(2,1)}, u32[]{:S(2)}) copy-start(bf16[16,32,2048]{2,1,0:T(8,128)(2,1)} %all_to_all.20) | copy-start | bytes 6291460
  216.0 1.7 copy-start.5
  216.3 2.7 copy-start.2
  223.8 1.4 copy-start.7
  225.2 12.5 %copy-start.29 = (s32[4]{0:T(128)S(1)}, s32[4]{0:T(128)}, u32[]{:S(2)}) copy-start(s32[4]{0:T(128)} %constant.161.clone) | copy-start | bytes 52
  225.2 12.5 %copy-start.30 = (s32[4]{0:T(128)S(1)}, s32[4]{0:T(128)}, u32[]{:S(2)}) copy-start(s32[4]{0:T(128)} %constant.162.clone) | copy-start | bytes 52
  237.6 2.7 collective-permute-start.15
  241.3 1.4 copy-start.9
  242.6 37.6 %all-to-all-start.3 = ((bf16[16,32,2048]{2,1,0:T(8,128)(2,1)}), bf16[16,32,2048]{2,1,0:T(8,128)(2,1)S(1)}, u32[]{:S(2)}, u32[]{:S(2)}) async-start(bf16[16,32,2048]{2,1,0:T(8,128)(2,1)} %bitcast.56), calls=%async_computation.4 | async-start | bytes 4194304 | tf_op jit(solution)/shard_map/all_to_all | solution.py:530
  246.3 56.6 %reduce-scatter.5.cloned.1.call-start = ((), (), s32[]{:S(2)}) async-start(), calls=%async_computation.8 | async-start | bytes 2359296 | tf_op jit(solution)/shard_map/reduce_scatter | solution.py:560
  280.7 2.7 collective-permute-start.16
  281.2 21.7 %copy-start.16 = (bf16[64,2048]{1,0:T(8,128)(2,1)S(1)}, bf16[64,2048]{1,0:T(8,128)(2,1)}, u32[]{:S(2)}) copy-start(bf16[64,2048]{1,0:T(8,128)(2,1)} %copy-done.15) | copy-start | bytes 786436
  283.9 10.6 %collective-permute-start.19 = (bf16[64,2048]{1,0:T(8,128)(2,1)S(1)}, bf16[64,2048]{1,0:T(8,128)(2,1)S(1)}, u32[]{:S(2)}, u32[]{:S(2)}) collective-permute-start(bf16[64,2048]{1,0:T(8,128)(2,1)S(1)} %get-tuple-element.63), channel_id=1, source_target_pairs={{0,14},{1,15},{2,0},{3,1},{4,2},{5,3},{6,4},{7,5},{8,6},{9,7},{10,... | collective-permute-start | bytes 786440 | tf_op jit(solution)/shard_map/ppermute | solution.py:569
  284.2 11.0 %collective-permute-start.18 = (bf16[64,2048]{1,0:T(8,128)(2,1)S(1)}, bf16[64,2048]{1,0:T(8,128)(2,1)S(1)}, u32[]{:S(2)}, u32[]{:S(2)}) collective-permute-start(bf16[64,2048]{1,0:T(8,128)(2,1)S(1)} %get-tuple-element.64), channel_id=1, source_target_pairs={{0,2},{1,3},{2,4},{3,5},{4,6},{5,7},{6,8},{7,9},{8,10},{9,11},{10,... | collective-permute-start | bytes 786440 | tf_op jit(solution)/shard_map/ppermute | solution.py:569
  286.1 16.9 %collective-permute-start.17 = (bf16[64,2048]{1,0:T(8,128)(2,1)S(1)}, bf16[64,2048]{1,0:T(8,128)(2,1)}, u32[]{:S(2)}, u32[]{:S(2)}) collective-permute-start(bf16[64,2048]{1,0:T(8,128)(2,1)S(1)} %get-tuple-element.62), channel_id=1, source_target_pairs={{0,4},{1,13},{2,6},{3,15},{4,8},{5,1},{6,10},{7,3},{8,12},{9,5},{1... | collective-permute-start | bytes 786440 | tf_op jit(solution)/shard_map/ppermute | solution.py:569
  (11 other events, 7.9 us)
Sparse Core Ops, SparseCore 0:
  63.2 44.1 reduce-scatter.2
  110.2 41.8 all-gather.2
  249.7 44.0 reduce-scatter.4

commit v5 on v4

--- a/solution.py
+++ b/solution.py
@@ -400,6 +400,28 @@
     )(weights, y)
 
 
+def blocks_kernel(w_ref, y_ref, *out_refs):
+    rows = y_ref[...].reshape(w_ref.shape[1], D)
+    out = mm(w_ref[...], rows).astype(BF)
+    for i, out_ref in enumerate(out_refs):
+        out_ref[...] = out[i * TOK : (i + 1) * TOK]
+
+
+def combine_blocks(weights, y, half):
+    block = jax.ShapeDtypeStruct((TOK, D), BF)
+    return pl.pallas_call(
+        blocks_kernel,
+        grid=(1,),
+        out_shape=[block] * GROUP,
+        in_specs=[
+            whole(weights.shape),
+            pl.BlockSpec((y.shape[0], GROUP * CAP, D), lambda i: (0, half, 0)),
+        ],
+        out_specs=[whole(block.shape)] * GROUP,
+        compiler_params=params(16),
+    )(weights, y)
+
+
 def place_kernel(at_ref, own_ref, got_ref, out_ref):
     out_ref[...] = jnp.zeros_like(out_ref)
     for i in range(GROUP):
@@ -561,9 +583,10 @@
         far_placed, "exp", scatter_dimension=0, tiled=True, axis_index_groups=same_core
     )
 
-    near_got = lax.ppermute(combine(weights[1], near_back, 1), "exp", core_pairs)
-    near_own = combine(weights[0], near_back, 0)
-    near_sum = (near_own.astype(F32) + near_got.astype(F32)).reshape(GROUP, TOK, D)
+    near_sent = combine_blocks(weights[1], near_back, 1)
+    near_got = {i: lax.ppermute(near_sent[i], "exp", core_pairs) for i in (3, 1, 2, 0)}
+    near_own = combine_blocks(weights[0], near_back, 0)
+    near_sum = [near_own[i].astype(F32) + near_got[i].astype(F32) for i in range(GROUP)]
     mixture = near_sum[0] + far_sum.astype(F32)
     for i in (3, 1, 2):
         sent = lax.ppermute(near_sum[i].astype(BF), "exp", along_z(i, 1, n_exp))

time: 312 us -> 319 us (1.022); the launches traced: 312 us -> 315 us
  blocking collectives: 84.8 us -> 126 us
  waiting for transfers between devices: 100 us -> 63.8 us
    all_to_all x2 -> x3, blocking collectives: 66.6 us -> 108 us  [spread_out(): return lax.all_to_all(rows, 'ctx', split_axis=0, concat_axis=0, tiled=True)]
    all_to_all x2 -> x1, waiting for transfers between devices: 44.2 us -> 10.9 us  [spread_out(): return lax.all_to_all(rows, 'ctx', split_axis=0, concat_axis=0, tiled=True)]
    all_to_all x2 -> x1, starting transfers between devices: 7.43 us -> 3.72 us  [spread_out(): return lax.all_to_all(rows, 'ctx', split_axis=0, concat_axis=0, tiled=True)]
    unnamed x68 -> x70, local copies, waits for them, and re-layouts: 13.9 us -> 15 us
  transfers between devices with their start and end apart: 25 -> 27, of which waited for: 17 -> 17; matrix products, arithmetic and copies ran while one was open for 6% -> 6% of each run, Pallas kernels for 9% -> 9%
where the time goes in v5:
time: 319 us; the launch traced here: 315 us
  blocking collectives  126 us (39%)
  waiting for transfers between devices  63.8 us (20%)
  Pallas kernels  40.6 us (13%)
  starting transfers between devices  33.5 us (11%)
  local copies, waits for them, and re-layouts  23.2 us (7%)
  between operations  14.4 us (5%)
  other arithmetic  7.13 us (2%)
  matrix products  5.83 us (2%)
    all_to_all x3, blocking collectives, spread_out(): return lax.all_to_all(rows, 'ctx', split_axis=0, concat_axis=0, tiled=True)  108 us
    reduce_scatter x1, waiting for transfers between devices, local(): lax.psum_scatter(terms, 'exp', scatter_dimension=0, tiled=True, axis_inde...  20.6 us
    all_gather x1, blocking collectives, local(): routes_all = lax.all_gather(routes, 'exp', tiled=True)  18.2 us
    unnamed x70, local copies, waits for them, and re-layouts  15 us
    pallas_call x1, Pallas kernels, delta_local(): pl.pallas_call(delta_kernel, grid=(1,), out_shape=[jax.ShapeDtypeStruct(a...  14.5 us
    all_to_all x1, waiting for transfers between devices, spread_out(): return lax.all_to_all(rows, 'ctx', split_axis=0, concat_axis=0, tiled=True)  10.9 us
    ppermute x3, waiting for transfers between devices, local(): sent = lax.ppermute(near_sum[i].astype(BF), 'exp', along_z(i, 1, n_exp))  10.2 us
    pallas_call x2, Pallas kernels, expert(): pl.pallas_call(expert_kernel, grid=(2,), out_shape=jax.ShapeDtypeStruct(x...  9.63 us
  transfers between devices with their start and end apart: 27, of which 17 were waited for; matrix products, arithmetic and copies ran while one was open for 6% of the time, Pallas kernels for 9%

profile of v5, /device:TPU:32, one launch (start us, length us, event | category | flops | bytes accessed | tf_op | source)
XLA Modules:
  0.0 314.8 jit_solution(15842570519252573753)
XLA Ops:
  11.4 14.5 %shard_map.203 = (bf16[2,1024,128]{2,1,0:T(8,128)(2,1)}, f32[2,1024,128]{2,1,0:T(8,128)}, bf16[2,128,256]{2,1,0:T(8,128)(2,1)}) custom-call(bf16[1024,128]{1,0:T(8,128)(2,1)} %q_ref.1, bf16[1024,128]{1,0:T(8,128)(2,1)} %k_ref.1, bf16[1024,256]{1,0:T(8,128)(2,1)} %v_ref.1, f32[48,128]{1,0:T(8,128)} %pad_maximum_fusion.row_ref, ...), custom_call_target="tpu_custom_call" | custom-call | tf_op jit(solution)/shard_map/pallas_call | solution.py:150
  25.9 1.5 collective-permute-start
  27.4 2.7 collective-permute-start.1
  30.1 1.7 collective-permute-start.2
  31.8 1.4 collective-permute-done.a1
  33.2 3.8 %collective-permute-done.1.a2 = bf16[2,128,256]{2,1,0:T(8,128)(2,1)S(1)} collective-permute-done((bf16[2,128,256]{2,1,0:T(8,128)(2,1)}, bf16[2,128,256]{2,1,0:T(8,128)(2,1)S(1)}, u32[]{:S(2)}, u32[]{:S(2)}) %collective-permute-start.1) | collective-permute-done | bytes 131104 | tf_op jit(solution)/shard_map/ppermute | solution.py:488
  37.7 2.6 shard_map.204
  40.3 3.5 %collective-permute-start.3 = (bf16[2,128,256]{2,1,0:T(8,128)(2,1)}, bf16[2,128,256]{2,1,0:T(8,128)(2,1)S(1)}, u32[]{:S(2)}, u32[]{:S(2)}) collective-permute-start(bf16[2,128,256]{2,1,0:T(8,128)(2,1)} %get-tuple-element.40), channel_id=1, source_target_pairs={{0,64},{16,80},{32,96},{48,112},{64,128},{80,144},{96,160},{112,17... | collective-permute-start | bytes 393224 | tf_op jit(solution)/shard_map/ppermute | solution.py:497
  43.8 4.8 %collective-permute-start.4 = (bf16[2,128,256]{2,1,0:T(8,128)(2,1)}, bf16[2,128,256]{2,1,0:T(8,128)(2,1)S(1)}, u32[]{:S(2)}, u32[]{:S(2)}) collective-permute-start(bf16[2,128,256]{2,1,0:T(8,128)(2,1)} %get-tuple-element.40), channel_id=1, source_target_pairs={{0,128},{16,144},{32,160},{48,176},{64,192},{80,208},{96,224},{112... | collective-permute-start | bytes 393224 | tf_op jit(solution)/shard_map/ppermute | solution.py:497
  48.6 1.3 collective-permute-start.5
  50.0 1.5 collective-permute-done.4.b2
  51.4 1.3 collective-permute-done.5.b3
  53.4 3.9 %shard_map.205 = (bf16[1024,256]{1,0:T(8,128)(2,1)}, bf16[512,256]{1,0:T(8,128)(2,1)}, bf16[512,256]{1,0:T(8,128)(2,1)}) custom-call(s32[1]{0:T(128)} %bitcast.par_ref, bf16[2,1024,128]{2,1,0:T(8,128)(2,1)} %get-tuple-element.36.g_ref, f32[2,1024,128]{2,1,0:T(8,128)} %get-tuple-element.37.o_ref, f32[2,128,256]{2,1,0:T(8,128)} %get-tuple-element.39.prefix, ...), custom_call_target="tpu_custom_call" | custom-call | tf_op jit(solution)/shard_map/pallas_call | solution.py:241
  57.3 1.7 collective-permute-done.6.b_ref
  60.0 3.1 shard_map.206
  63.9 18.2 %all-gather = s32[16,64,10]{1,2,0:T(8,128)S(1)} all-gather(s32[1,64,10]{1,2,0:T(8,128)S(1)} %bitcast.69), channel_id=1, replica_groups=mesh['ctx'=16,'exp'=16] {'exp'}, dimensions={0}, use_global_device_ids=true | all-gather | bytes 43520 | tf_op jit(solution)/shard_map/all_gather | solution.py:506
  82.8 1.9 fusion
  86.8 20.6 %reduce-scatter.3.cloned.1.call-done.attn_ref = bf16[64,2048]{1,0:T(8,128)(2,1)} async-done(((bf16[512,2048]{1,0:T(8,128)(2,1)}), bf16[64,2048]{1,0:T(8,128)(2,1)}) %reduce-scatter.3.cloned.1.call-update) | async-done | bytes 262160 | tf_op jit(solution)/shard_map/reduce_scatter | solution.py:503
  110.1 1.1 collective-permute-start.8
  112.2 2.9 collective-permute-start.10
  115.2 1.6 collective-permute-done.8.refs_1_
  116.8 3.0 collective-permute-done.9.refs_2_
  119.7 3.9 %collective-permute-done.10.refs_3_ = bf16[64,2048]{1,0:T(8,128)(2,1)S(1)} collective-permute-done((bf16[64,2048]{1,0:T(8,128)(2,1)}, bf16[64,2048]{1,0:T(8,128)(2,1)S(1)}, u32[]{:S(2)}, u32[]{:S(2)}) %collective-permute-start.10) | collective-permute-done | bytes 262176 | tf_op jit(solution)/shard_map/ppermute | solution.py:546
  123.7 1.5 collective-permute-done.14.refs_7_
  125.2 1.7 shard_map.208
  126.9 35.3 %all_to_all.20 = bf16[16,32,2048]{2,1,0:T(8,128)(2,1)} all-to-all(bf16[16,32,2048]{2,1,0:T(8,128)(2,1)S(1)} %shard_map.208), channel_id=1, replica_groups=mesh['ctx'=16,'exp'=16] {'ctx'}, dimensions={0} | all-to-all | bytes 4194304 | tf_op jit(solution)/shard_map/all_to_all | solution.py:552
  162.1 2.2 copy-done.3
  164.3 1.6 shard_map.210
  166.0 41.3 %all_to_all.21 = bf16[16,32,2048]{2,1,0:T(8,128)(2,1)S(1)} all-to-all(bf16[16,32,2048]{2,1,0:T(8,128)(2,1)S(1)} %shard_map.210), channel_id=1, replica_groups=mesh['ctx'=16,'exp'=16] {'ctx'}, dimensions={0} | all-to-all | bytes 4194304 | tf_op jit(solution)/shard_map/all_to_all | solution.py:552
  207.2 4.8 %shard_map.211 = bf16[512,2048]{1,0:T(8,128)(2,1)S(1)} custom-call(bf16[512,2048]{1,0:T(8,128)(2,1)S(1)} %bitcast.58, bf16[2048,1024]{1,0:T(8,128)(2,1)S(1)} %bitcast.49, bf16[2048,1024]{1,0:T(8,128)(2,1)S(1)} %bitcast.50, bf16[512,2048]{1,0:T(8,128)(2,1)S(1)} %bitcast.53), custom_call_target="tpu_custom_call" | custom-call | flops 3221225472 | bytes 10485760 | tf_op jit(solution)/shard_map/pallas_call | solution.py:364
  212.1 1.4 copy-done.9
  213.4 3.7 %all-to-all-start.2 = ((bf16[16,32,2048]{2,1,0:T(8,128)(2,1)}), bf16[16,32,2048]{2,1,0:T(8,128)(2,1)S(1)}, u32[]{:S(2)}, u32[]{:S(2)}) async-start(bf16[16,32,2048]{2,1,0:T(8,128)(2,1)} %bitcast.57), calls=%async_computation.3 | async-start | bytes 4194304 | tf_op jit(solution)/shard_map/all_to_all | solution.py:552
  217.2 4.4 %fusion.41 = f32[1024,256]{1,0:T(8,128)} fusion(bf16[1024,2048]{1,0:T(8,128)(2,1)} %all-gather.3.cloned.1.call-done.r0.r1.r2.r3, bf16[2048,256]{1,0:T(8,128)(2,1)S(1)} %copy-done), kind=kOutput, calls=%fused_computation.82 | convolution fusion | flops 1073741824 | bytes 6291456 | tf_op jit(solution)/shard_map/dot_general | solution.py:565
  221.6 2.9 gather_fusion.1
  224.5 1.5 exp.6
  227.8 1.3 copy-done.2
  229.1 4.8 %shard_map.209 = bf16[512,2048]{1,0:T(8,128)(2,1)S(1)} custom-call(bf16[512,2048]{1,0:T(8,128)(2,1)S(1)} %bitcast.55, bf16[2048,1024]{1,0:T(8,128)(2,1)S(1)} %bitcast.51, bf16[2048,1024]{1,0:T(8,128)(2,1)S(1)} %bitcast.52, bf16[512,2048]{1,0:T(8,128)(2,1)S(1)} %bitcast.54), custom_call_target="tpu_custom_call" | custom-call | flops 3221225472 | bytes 10485760 | tf_op jit(solution)/shard_map/pallas_call | solution.py:364
  233.9 1.3 copy-done.7
  235.2 10.9 %all-to-all-done.2.y_ref = bf16[16,32,2048]{2,1,0:T(8,128)(2,1)S(1)} async-done(((bf16[16,32,2048]{2,1,0:T(8,128)(2,1)}), bf16[16,32,2048]{2,1,0:T(8,128)(2,1)S(1)}, u32[]{:S(2)}, u32[]{:S(2)}) %all-to-all-start.2) | async-done | bytes 2097184 | tf_op jit(solution)/shard_map/all_to_all | solution.py:552
  248.1 2.2 collective-permute-done.15.got_ref
  251.2 1.4 copy-done.10
  252.6 1.6 copy-done.8
  254.1 31.6 %all_to_all.22.y_ref = bf16[16,32,2048]{2,1,0:T(8,128)(2,1)S(1)} all-to-all(bf16[16,32,2048]{2,1,0:T(8,128)(2,1)S(1)} %bitcast.56), channel_id=1, replica_groups=mesh['ctx'=16,'exp'=16] {'ctx'}, dimensions={0} | all-to-all | bytes 4194304 | tf_op jit(solution)/shard_map/all_to_all | solution.py:552
  288.2 1.9 collective-permute-start.20
  290.2 5.8 %collective-permute-start.18 = (bf16[64,2048]{1,0:T(8,128)(2,1)S(1)}, bf16[64,2048]{1,0:T(8,128)(2,1)S(1)}, u32[]{:S(2)}, u32[]{:S(2)}) collective-permute-start(bf16[64,2048]{1,0:T(8,128)(2,1)S(1)} %add_convert_fusion.3), channel_id=1, source_target_pairs={{0,4},{1,13},{2,6},{3,15},{4,8},{5,1},{6,10},{7,3},{8,12},{9,5},{1... | collective-permute-start | bytes 786440 | tf_op jit(solution)/shard_map/ppermute | solution.py:592
  297.1 1.1 collective-permute-done.20
  298.2 8.0 %collective-permute-done.18 = bf16[64,2048]{1,0:T(8,128)(2,1)S(1)} collective-permute-done((bf16[64,2048]{1,0:T(8,128)(2,1)S(1)}, bf16[64,2048]{1,0:T(8,128)(2,1)S(1)}, u32[]{:S(2)}, u32[]{:S(2)}) %collective-permute-start.18) | collective-permute-done | bytes 262176 | tf_op jit(solution)/shard_map/ppermute | solution.py:592
  306.2 1.9 add_convert_fusion
  (136 shorter events, 21.9 us)
Async XLA Ops:
  7.2 210.0 %copy-start = (bf16[2048,256]{1,0:T(8,128)(2,1)S(1)}, bf16[2048,256]{1,0:T(8,128)(2,1)}, u32[]{:S(2)}) copy-start(bf16[2048,256]{1,0:T(8,128)(2,1)} %param.30) | copy-start | bytes 3145732
  7.2 100.3 %reduce-scatter.3.cloned.1.call-start = ((), (), s32[]{:S(2)}) async-start(), calls=%async_computation.6 | async-start | bytes 2359296 | tf_op jit(solution)/shard_map/reduce_scatter | solution.py:503
  7.2 51.8 %collective-permute-start.7 = (bf16[256,2048]{1,0:T(8,128)(2,1)}, bf16[256,2048]{1,0:T(8,128)(2,1)S(1)}, u32[]{:S(2)}, u32[]{:S(2)}) collective-permute-start(bf16[256,2048]{1,0:T(8,128)(2,1)} %wa_ref.1), channel_id=1, source_target_pairs={{0,1},{1,0},{2,3},{3,2},{4,5},{5,4},{6,7},{7,6},{8,9},{9,8},{10,11... | collective-permute-start | bytes 3145736 | tf_op jit(solution)/shard_map/ppermute | solution.py:485
  11.4 47.6 %copy-start.11 = (bf16[256,2048]{1,0:T(8,128)(2,1)S(1)}, bf16[256,2048]{1,0:T(8,128)(2,1)}, u32[]{:S(2)}) copy-start(bf16[256,2048]{1,0:T(8,128)(2,1)} %wa_ref.1) | copy-start | bytes 3145732
  25.9 7.3 %collective-permute-start = (bf16[2,128,256]{2,1,0:T(8,128)(2,1)}, bf16[2,128,256]{2,1,0:T(8,128)(2,1)S(1)}, u32[]{:S(2)}, u32[]{:S(2)}) collective-permute-start(bf16[2,128,256]{2,1,0:T(8,128)(2,1)} %get-tuple-element.38.own), channel_id=1, source_target_pairs={{0,16},{16,32},{32,48},{48,0},{64,80},{80,96},{96,112},{112,64},{1... | collective-permute-start | bytes 393224 | tf_op jit(solution)/shard_map/ppermute | solution.py:488
  27.4 9.6 %collective-permute-start.1 = (bf16[2,128,256]{2,1,0:T(8,128)(2,1)}, bf16[2,128,256]{2,1,0:T(8,128)(2,1)S(1)}, u32[]{:S(2)}, u32[]{:S(2)}) collective-permute-start(bf16[2,128,256]{2,1,0:T(8,128)(2,1)} %get-tuple-element.38.own), channel_id=1, source_target_pairs={{0,32},{16,48},{32,0},{48,16},{64,96},{80,112},{96,64},{112,80},{1... | collective-permute-start | bytes 393224 | tf_op jit(solution)/shard_map/ppermute | solution.py:488
  30.1 6.8 %collective-permute-start.2 = (bf16[2,128,256]{2,1,0:T(8,128)(2,1)}, bf16[2,128,256]{2,1,0:T(8,128)(2,1)S(1)}, u32[]{:S(2)}, u32[]{:S(2)}) collective-permute-start(bf16[2,128,256]{2,1,0:T(8,128)(2,1)} %get-tuple-element.38.own), channel_id=1, source_target_pairs={{0,48},{16,0},{32,16},{48,32},{64,112},{80,64},{96,80},{112,96},{1... | collective-permute-start | bytes 393224 | tf_op jit(solution)/shard_map/ppermute | solution.py:488
  33.2 3.8 %copy-start.22 = (bf16[2,128,256]{2,1,0:T(8,128)(2,1)}, bf16[2,128,256]{2,1,0:T(8,128)(2,1)S(1)}, u32[]{:S(2)}) copy-start(bf16[2,128,256]{2,1,0:T(8,128)(2,1)S(1)} %collective-permute-done.a1) | copy-start | bytes 393220
  40.3 9.6 %collective-permute-start.3 = (bf16[2,128,256]{2,1,0:T(8,128)(2,1)}, bf16[2,128,256]{2,1,0:T(8,128)(2,1)S(1)}, u32[]{:S(2)}, u32[]{:S(2)}) collective-permute-start(bf16[2,128,256]{2,1,0:T(8,128)(2,1)} %get-tuple-element.40), channel_id=1, source_target_pairs={{0,64},{16,80},{32,96},{48,112},{64,128},{80,144},{96,160},{112,17... | collective-permute-start | bytes 393224 | tf_op jit(solution)/shard_map/ppermute | solution.py:497
  43.8 7.6 %collective-permute-start.4 = (bf16[2,128,256]{2,1,0:T(8,128)(2,1)}, bf16[2,128,256]{2,1,0:T(8,128)(2,1)S(1)}, u32[]{:S(2)}, u32[]{:S(2)}) collective-permute-start(bf16[2,128,256]{2,1,0:T(8,128)(2,1)} %get-tuple-element.40), channel_id=1, source_target_pairs={{0,128},{16,144},{32,160},{48,176},{64,192},{80,208},{96,224},{112... | collective-permute-start | bytes 393224 | tf_op jit(solution)/shard_map/ppermute | solution.py:497
  48.6 4.1 %collective-permute-start.5 = (bf16[2,128,256]{2,1,0:T(8,128)(2,1)}, bf16[2,128,256]{2,1,0:T(8,128)(2,1)S(1)}, u32[]{:S(2)}, u32[]{:S(2)}) collective-permute-start(bf16[2,128,256]{2,1,0:T(8,128)(2,1)} %get-tuple-element.40), channel_id=1, source_target_pairs={{0,192},{16,208},{32,224},{48,240},{1,193},{17,209},{33,225},{49,2... | collective-permute-start | bytes 393224 | tf_op jit(solution)/shard_map/ppermute | solution.py:497
  49.9 2.8 copy-start.23
  57.3 1.7 collective-permute-start.6
  63.1 21.6 %copy-start.29 = (s32[256]{0:T(256)S(1)}, s32[256]{0:T(256)}, u32[]{:S(2)}) copy-start(s32[256]{0:T(256)} %param.32) | copy-start | bytes 3076
  63.2 99.0 %all-gather.3.cloned.1.call-start = ((), (), s32[]{:S(2)}) async-start(), calls=%async_computation.7 | async-start | bytes 4456448 | tf_op jit(solution)/shard_map/all_gather | solution.py:549
  85.5 22.0 %copy-start.14 = (bf16[64,2048]{1,0:T(8,128)(2,1)S(1)}, bf16[64,2048]{1,0:T(8,128)(2,1)}, u32[]{:S(2)}) copy-start(bf16[64,2048]{1,0:T(8,128)(2,1)} %res_ref.1) | copy-start | bytes 786436
  85.5 22.0 %copy-start.18 = (f32[2048]{0:T(1024)S(1)}, f32[2048]{0:T(1024)}, u32[]{:S(2)}) copy-start(f32[2048]{0:T(1024)} %param.29) | copy-start | bytes 24580
  110.1 6.7 %collective-permute-start.8 = (bf16[64,2048]{1,0:T(8,128)(2,1)}, bf16[64,2048]{1,0:T(8,128)(2,1)S(1)}, u32[]{:S(2)}, u32[]{:S(2)}) collective-permute-start(bf16[64,2048]{1,0:T(8,128)(2,1)} %get-tuple-element.50.refs_0_), channel_id=1, source_target_pairs={{0,14},{1,15},{2,0},{3,1},{4,2},{5,3},{6,4},{7,5},{8,6},{9,7},{10,... | collective-permute-start | bytes 786440 | tf_op jit(solution)/shard_map/ppermute | solution.py:546
  111.2 8.5 %collective-permute-start.9 = (bf16[64,2048]{1,0:T(8,128)(2,1)}, bf16[64,2048]{1,0:T(8,128)(2,1)S(1)}, u32[]{:S(2)}, u32[]{:S(2)}) collective-permute-start(bf16[64,2048]{1,0:T(8,128)(2,1)} %get-tuple-element.50.refs_0_), channel_id=1, source_target_pairs={{0,2},{1,3},{2,4},{3,5},{4,6},{5,7},{6,8},{7,9},{8,10},{9,11},{10,... | collective-permute-start | bytes 786440 | tf_op jit(solution)/shard_map/ppermute | solution.py:546
  112.2 11.4 %collective-permute-start.10 = (bf16[64,2048]{1,0:T(8,128)(2,1)}, bf16[64,2048]{1,0:T(8,128)(2,1)S(1)}, u32[]{:S(2)}, u32[]{:S(2)}) collective-permute-start(bf16[64,2048]{1,0:T(8,128)(2,1)} %get-tuple-element.50.refs_0_), channel_id=1, source_target_pairs={{0,12},{1,5},{2,14},{3,7},{4,0},{5,9},{6,2},{7,11},{8,4},{9,13},{1... | collective-permute-start | bytes 786440 | tf_op jit(solution)/shard_map/ppermute | solution.py:546
  115.2 8.5 %collective-permute-start.11 = (bf16[64,2048]{1,0:T(8,128)(2,1)}, bf16[64,2048]{1,0:T(8,128)(2,1)S(1)}, u32[]{:S(2)}, u32[]{:S(2)}) collective-permute-start(bf16[64,2048]{1,0:T(8,128)(2,1)} %get-tuple-element.50.refs_0_), channel_id=1, source_target_pairs={{0,1},{1,0},{2,3},{3,2},{4,5},{5,4},{6,7},{7,6},{8,9},{9,8},{10,11... | collective-permute-start | bytes 786440 | tf_op jit(solution)/shard_map/ppermute | solution.py:548
  116.8 6.9 %collective-permute-start.12 = (bf16[64,2048]{1,0:T(8,128)(2,1)S(1)}, bf16[64,2048]{1,0:T(8,128)(2,1)S(1)}, u32[]{:S(2)}, u32[]{:S(2)}) collective-permute-start(bf16[64,2048]{1,0:T(8,128)(2,1)S(1)} %collective-permute-done.8.refs_1_), channel_id=1, source_target_pairs={{0,1},{1,0},{2,3},{3,2},{4,5},{5,4},{6,7},{7,6},{8,9},{9,8},{10,11... | collective-permute-start | bytes 786440 | tf_op jit(solution)/shard_map/ppermute | solution.py:548
  119.7 4.0 %collective-permute-start.13 = (bf16[64,2048]{1,0:T(8,128)(2,1)S(1)}, bf16[64,2048]{1,0:T(8,128)(2,1)S(1)}, u32[]{:S(2)}, u32[]{:S(2)}) collective-permute-start(bf16[64,2048]{1,0:T(8,128)(2,1)S(1)} %collective-permute-done.9.refs_2_), channel_id=1, source_target_pairs={{0,1},{1,0},{2,3},{3,2},{4,5},{5,4},{6,7},{7,6},{8,9},{9,8},{10,11... | collective-permute-start | bytes 786440 | tf_op jit(solution)/shard_map/ppermute | solution.py:548
  123.7 1.5 collective-permute-start.14
  162.1 2.2 copy-start.3
  164.3 42.9 %copy-start.4 = (bf16[1,512,2048]{2,1,0:T(8,128)(2,1)S(1)}, bf16[1,512,2048]{2,1,0:T(8,128)(2,1)}, u32[]{:S(2)}) copy-start(bf16[1,512,2048]{2,1,0:T(8,128)(2,1)} %param.34) | copy-start | bytes 6291460
  166.0 41.3 %copy-start.1 = (bf16[1,2048,1024]{2,1,0:T(8,128)(2,1)S(1)}, bf16[1,2048,1024]{2,1,0:T(8,128)(2,1)}, u32[]{:S(2)}) copy-start(bf16[1,2048,1024]{2,1,0:T(8,128)(2,1)} %param.33) | copy-start | bytes 12582916
  212.0 1.4 copy-start.9
  213.4 32.7 %all-to-all-start.2 = ((bf16[16,32,2048]{2,1,0:T(8,128)(2,1)}), bf16[16,32,2048]{2,1,0:T(8,128)(2,1)S(1)}, u32[]{:S(2)}, u32[]{:S(2)}) async-start(bf16[16,32,2048]{2,1,0:T(8,128)(2,1)} %bitcast.57), calls=%async_computation.3 | async-start | bytes 4194304 | tf_op jit(solution)/shard_map/all_to_all | solution.py:552
  217.2 89.0 %reduce-scatter.5.cloned.1.call-start = ((), (), s32[]{:S(2)}) async-start(), calls=%async_computation.8 | async-start | bytes 2359296 | tf_op jit(solution)/shard_map/reduce_scatter | solution.py:582
  221.6 4.5 %copy-start.20 = (pred[1024,256]{1,0:T(8,128)(4,1)S(1)}, pred[1024,256]{1,0:T(8,128)(4,1)}, u32[]{:S(2)}) copy-start(pred[1024,256]{1,0:T(8,128)(4,1)} %copy-done.19) | copy-start | bytes 786436
  224.5 1.8 copy-start.21
  224.5 3.2 %copy-start.6 = (bf16[16,32,2048]{2,1,0:T(8,128)(2,1)S(1)}, bf16[16,32,2048]{2,1,0:T(8,128)(2,1)}, u32[]{:S(2)}) copy-start(bf16[16,32,2048]{2,1,0:T(8,128)(2,1)} %all_to_all.20) | copy-start | bytes 6291460
  226.1 1.7 copy-start.5
  226.3 2.7 copy-start.2
  235.2 12.4 %copy-start.30 = (s32[4]{0:T(128)S(1)}, s32[4]{0:T(128)}, u32[]{:S(2)}) copy-start(s32[4]{0:T(128)} %constant.161.clone) | copy-start | bytes 52
  235.2 12.4 %copy-start.31 = (s32[4]{0:T(128)S(1)}, s32[4]{0:T(128)}, u32[]{:S(2)}) copy-start(s32[4]{0:T(128)} %constant.162.clone) | copy-start | bytes 52
  247.5 2.7 collective-permute-start.15
  251.2 1.4 copy-start.10
  252.5 1.6 copy-start.8
  286.2 1.6 collective-permute-start.21
  286.3 1.9 collective-permute-start.19
  286.8 3.3 %collective-permute-start.17 = (bf16[64,2048]{1,0:T(8,128)(2,1)S(1)}, bf16[64,2048]{1,0:T(8,128)(2,1)S(1)}, u32[]{:S(2)}, u32[]{:S(2)}) collective-permute-start(bf16[64,2048]{1,0:T(8,128)(2,1)S(1)} %get-tuple-element.65), channel_id=1, source_target_pairs={{0,1},{1,0},{2,3},{3,2},{4,5},{5,4},{6,7},{7,6},{8,9},{9,8},{10,11... | collective-permute-start | bytes 786440 | tf_op jit(solution)/shard_map/ppermute | solution.py:587
  286.9 19.3 %copy-start.17 = (bf16[64,2048]{1,0:T(8,128)(2,1)S(1)}, bf16[64,2048]{1,0:T(8,128)(2,1)}, u32[]{:S(2)}) copy-start(bf16[64,2048]{1,0:T(8,128)(2,1)} %copy-done.16) | copy-start | bytes 786436
  286.9 9.1 %collective-permute-start.16 = (bf16[64,2048]{1,0:T(8,128)(2,1)S(1)}, bf16[64,2048]{1,0:T(8,128)(2,1)S(1)}, u32[]{:S(2)}, u32[]{:S(2)}) collective-permute-start(bf16[64,2048]{1,0:T(8,128)(2,1)S(1)} %get-tuple-element.62), channel_id=1, source_target_pairs={{0,1},{1,0},{2,3},{3,2},{4,5},{5,4},{6,7},{7,6},{8,9},{9,8},{10,11... | collective-permute-start | bytes 786440 | tf_op jit(solution)/shard_map/ppermute | solution.py:587
  287.9 9.2 %collective-permute-start.22 = (bf16[64,2048]{1,0:T(8,128)(2,1)S(1)}, bf16[64,2048]{1,0:T(8,128)(2,1)S(1)}, u32[]{:S(2)}, u32[]{:S(2)}) collective-permute-start(bf16[64,2048]{1,0:T(8,128)(2,1)S(1)} %add_convert_fusion.1), channel_id=1, source_target_pairs={{0,14},{1,15},{2,0},{3,1},{4,2},{5,3},{6,4},{7,5},{8,6},{9,7},{10,... | collective-permute-start | bytes 786440 | tf_op jit(solution)/shard_map/ppermute | solution.py:592
  288.2 9.9 %collective-permute-start.20 = (bf16[64,2048]{1,0:T(8,128)(2,1)S(1)}, bf16[64,2048]{1,0:T(8,128)(2,1)S(1)}, u32[]{:S(2)}, u32[]{:S(2)}) collective-permute-start(bf16[64,2048]{1,0:T(8,128)(2,1)S(1)} %add_convert_fusion.2), channel_id=1, source_target_pairs={{0,2},{1,3},{2,4},{3,5},{4,6},{5,7},{6,8},{7,9},{8,10},{9,11},{10,... | collective-permute-start | bytes 786440 | tf_op jit(solution)/shard_map/ppermute | solution.py:592
  290.2 16.0 %collective-permute-start.18 = (bf16[64,2048]{1,0:T(8,128)(2,1)S(1)}, bf16[64,2048]{1,0:T(8,128)(2,1)S(1)}, u32[]{:S(2)}, u32[]{:S(2)}) collective-permute-start(bf16[64,2048]{1,0:T(8,128)(2,1)S(1)} %add_convert_fusion.3), channel_id=1, source_target_pairs={{0,4},{1,13},{2,6},{3,15},{4,8},{5,1},{6,10},{7,3},{8,12},{9,5},{1... | collective-permute-start | bytes 786440 | tf_op jit(solution)/shard_map/ppermute | solution.py:592
  (14 other events, 11.8 us)
Sparse Core Ops, SparseCore 0:
  63.3 44.1 reduce-scatter.2
  110.2 41.7 all-gather.2
  252.7 39.0 reduce-scatter.4
